TPU v7x, 32 devices: a whole 2x2x4 slice. The times are simulated.
32 devices in a mesh: groups: 2 (over x), role: 8 (over z, y), head: 2 (over core).
Axes of the slice: x: 2, y: 2, z: 4, core: 2. Of those that a mesh axis runs over, the one named last changes fastest.
Arguments:
- queries: bfloat16 [128, 64, 576], P(('groups', 'role'), 'head'), parts along dimension 0, may hold values from -120 to 120
- kv_cache: bfloat16 [128, 256, 576], P(('groups', 'role')), parts along dimension 0, may hold values from -5 to 5
- cache_lengths: int32 [128], P(('groups', 'role')), parts along dimension 0, may hold values from 2 to 256, as said below
- uv_weight: bfloat16 [64, 512, 128], P('head'), may hold values from -0.25 to 0.25
- out_weight: bfloat16 [8192, 7168], P('head', 'role'), may hold values from -0.0625 to 0.0625
- residual: bfloat16 [128, 7168], P(('groups', 'role', 'head')), parts along dimension 0, may hold values from -6 to 6
- norm_gain: float32 [7168], replicated, may hold values from 0.25 to 1.75
- expert_ids: int32 [128, 2], P(('groups', 'role', 'head')), parts along dimension 0, may hold values from 0 to 7, all different within a row; in each aligned block of 4 rows (0 to 3, 4 to 7, ...) at most 2 rows name the same one
- route_weights: float32 [128, 2], P(('groups', 'role', 'head')), parts along dimension 0, may hold values from 0.25 to 1
- gate_weight: bfloat16 [7168, 16384], P(None, ('role', 'head')), may hold values from -0.0625 to 0.0625
- up_weight: bfloat16 [7168, 16384], P(None, ('role', 'head')), may hold values from -0.0625 to 0.0625
- down_weight: bfloat16 [16384, 7168], P(('role', 'head')), may hold values from -0.125 to 0.125
Outputs:
- layer_out: bfloat16 [128, 7168], P(('groups', 'role', 'head')), parts along dimension 0
There are 2 independent parts, one for each index of `groups`. A program takes and returns all parts, laid end to end along the dimension named above; an argument that names none is the same for every part. Nothing has to cross between parts.
Inputs may be any that keep to these rules, and one draw needn't show every extreme that they name: `cache_lengths`: every request has at least 2 live positions and some request has 256. `expert_ids`: the 2 ids of a row differ; in each aligned block of 4 rows no id appears more than 2 times, and some id appears exactly 2 times in some block.
All inputs are finite; a program needn't handle non-finite values.
Results may differ from a plain program's by a relative error of at most 0.006.
Values may be sent and summed in bfloat16 or wider, within the bound.
No kernel may reach another device: no remote copies, remote signals or barrier semaphores. Data moves between devices by JAX's collectives and lax.ppermute only.
A program may use at most 128 MiB of HBM per device.

v0:
```python
import jax
import jax.numpy as jnp
from jax import lax
from jax.sharding import PartitionSpec as P

LATENT = 512
ROPE = 64
VDIM = 128
EXPERTS = 8
CAP = 2


def attend(queries, kv_cache, cache_lengths, uv_weight):
    scale_factor = (VDIM + ROPE) ** (-0.5)
    scores = (
        jnp.einsum("thc,tsc->ths", queries, kv_cache, preferred_element_type=jnp.float32)
        * scale_factor
    )
    position = lax.broadcasted_iota(jnp.int32, scores.shape, 2)
    scores = jnp.where(position < cache_lengths[:, None, None], scores, -jnp.inf)
    top_score = jnp.max(scores, axis=2, keepdims=True)
    weights = jnp.exp(scores - top_score)
    attn_probs = (weights / jnp.sum(weights, axis=2, keepdims=True)).astype(jnp.bfloat16)
    latent_out = jnp.einsum(
        "ths,tsc->thc", attn_probs, kv_cache[:, :, :LATENT], preferred_element_type=jnp.float32
    ).astype(jnp.bfloat16)
    head_out = jnp.einsum(
        "thc,hcv->thv", latent_out, uv_weight, preferred_element_type=jnp.float32
    ).astype(jnp.bfloat16)
    return head_out.reshape(head_out.shape[0], -1)


def on_device(
    queries,
    kv_cache,
    cache_lengths,
    uv_weight,
    out_weight,
    residual,
    norm_gain,
    expert_ids,
    route_weights,
    gate_weight,
    up_weight,
    down_weight,
):
    role_n = lax.axis_size("role")
    head_n = lax.axis_size("head")
    share_rows = residual.shape[0]
    model_width = residual.shape[1]
    head_out = attend(queries, kv_cache, cache_lengths, uv_weight)
    partial_value = jnp.dot(
        lax.all_gather(head_out, "role", axis=0, tiled=True),
        out_weight,
        preferred_element_type=jnp.float32,
    )
    summed_cols = lax.psum(partial_value, "head").astype(jnp.bfloat16)
    own_rows = lax.all_to_all(summed_cols, "role", split_axis=0, concat_axis=1, tiled=True)
    attn_out = lax.dynamic_slice_in_dim(
        own_rows, lax.axis_index("head") * share_rows, share_rows, 0
    )
    hidden = (residual.astype(jnp.float32) + attn_out.astype(jnp.float32)).astype(jnp.bfloat16)
    hidden_f = hidden.astype(jnp.float32)
    inverse = lax.rsqrt(jnp.mean(hidden_f * hidden_f, axis=1, keepdims=True) + 1e-06)
    normed = (hidden_f * inverse * norm_gain[None, :]).astype(jnp.bfloat16)
    flat_ids = expert_ids.reshape(-1)
    onehot = (
        flat_ids[:, None] == lax.broadcasted_iota(jnp.int32, (flat_ids.shape[0], EXPERTS), 1)
    ).astype(jnp.int32)
    slot_rank = jnp.sum(onehot * (jnp.cumsum(onehot, axis=0) - onehot), axis=1).reshape(
        expert_ids.shape
    )
    position = expert_ids * CAP + slot_rank
    slot_grid = lax.broadcasted_iota(jnp.int32, (EXPERTS * CAP,) + expert_ids.shape, 0)
    matches = slot_grid == position[None, :, :]
    placing = jnp.any(matches, axis=2).astype(jnp.bfloat16)
    mixing = jnp.sum(jnp.where(matches, route_weights[None, :, :], 0.0), axis=2).T
    buffer = (
        jnp.dot(placing, normed, preferred_element_type=jnp.float32)
        .astype(jnp.bfloat16)
        .reshape(EXPERTS, CAP, model_width)
    )
    devices = role_n * head_n
    group_size = devices // EXPERTS
    outgoing = jnp.repeat(buffer, group_size, axis=0)
    received = lax.all_to_all(outgoing, ("role", "head"), split_axis=0, concat_axis=0, tiled=True)
    item_count = received.shape[1]
    token_rows = received.reshape(-1, model_width)
    gate_val = jnp.dot(token_rows, gate_weight, preferred_element_type=jnp.float32)
    up_val = jnp.dot(token_rows, up_weight, preferred_element_type=jnp.float32)
    act_val = (jax.nn.silu(gate_val) * up_val).astype(jnp.bfloat16)
    expert_part = jnp.dot(act_val, down_weight, preferred_element_type=jnp.float32).reshape(
        devices, item_count, model_width
    )
    returned = lax.all_to_all(
        expert_part, ("role", "head"), split_axis=0, concat_axis=0, tiled=True
    )
    expert_out = jnp.sum(returned.reshape(EXPERTS, group_size, CAP, model_width), axis=1)
    combined = jnp.dot(
        mixing,
        expert_out.reshape(EXPERTS * CAP, model_width),
        precision=lax.Precision.HIGHEST,
        preferred_element_type=jnp.float32,
    )
    return (hidden_f + combined).astype(jnp.bfloat16)


def solution(mesh):
    return jax.shard_map(
        on_device,
        mesh=mesh,
        in_specs=(
            P(("groups", "role"), "head", None),
            P(("groups", "role"), None, None),
            P(("groups", "role")),
            P("head", None, None),
            P("head", "role"),
            P(("groups", "role", "head"), None),
            P(),
            P(("groups", "role", "head"), None),
            P(("groups", "role", "head"), None),
            P(None, ("role", "head")),
            P(None, ("role", "head")),
            P(("role", "head"), None),
        ),
        out_specs=P(("groups", "role", "head"), None),
        check_vma=False,
    )
```

profile of v0, /device:TPU:0, one launch (start us, length us, event | category | flops | bytes accessed | tf_op | source)
XLA Modules:
  0.0 130.5 jit_solution(8331126139758035119)
XLA Ops:
  0.0 0.0 copy-start
  0.0 1.0 copy-done
  1.0 2.1 %fusion.9 = f32[8,32,256]{2,1,0:T(8,128)S(1)} fusion(bf16[8,32,576]{2,1,0:T(8,128)(2,1)S(1)} %copy-done, bf16[8,256,576]{1,2,0:T(8,128)(2,1)} %param.13, s32[8]{0:T(128)} %param.14), kind=kOutput, calls=%fused_computation.10 | convolution fusion | flops 75694080 | bytes 2916384 | tf_op jit(solution)/shard_map/thc,tsc->ths/dot_general | solution.py:16
  3.1 0.2 fusion.31
  3.3 2.3 %fusion.5 = bf16[8,32,512]{2,1,0:T(8,128)(2,1)S(1)} fusion(bf16[8,256,576]{1,2,0:T(8,128)(2,1)} %param.13, f32[8,32]{1,0:T(8,128)S(1)} %fusion.31, f32[8,32,256]{2,1,0:T(8,128)S(1)} %fusion.9), kind=kOutput, calls=%fused_computation.7 | convolution fusion | flops 67437056 | bytes 2887680 | tf_op jit(solution)/shard_map/ths,tsc->thc/dot_general | solution.py:24
  5.6 0.0 copy-start.3
  5.6 0.0 copy-start.1
  5.7 0.0 copy-start.2
  5.7 2.9 %fusion.11 = bf16[8,4096]{1,0:T(8,128)(2,1)S(1)} fusion(bf16[32,512,128]{2,1,0:T(8,128)(2,1)} %param.15, bf16[8,32,512]{2,1,0:T(8,128)(2,1)S(1)} %fusion.5), kind=kOutput, calls=%fused_computation.14 | convolution fusion | flops 33587200 | bytes 4521984 | tf_op jit(solution)/shard_map/thc,hcv->thv/dot_general | solution.py:27
  8.6 33.0 %all_gather.3 = bf16[64,4096]{1,0:T(8,128)(2,1)S(1)} all-gather(bf16[8,4096]{1,0:T(8,128)(2,1)S(1)} %fusion.11), channel_id=1, replica_groups=mesh['groups'=2,'role'=8,'head'=2] {'role'}, dimensions={0}, use_global_device_ids=true | all-gather | bytes 589824 | tf_op jit(solution)/shard_map/all_gather | solution.py:53
  41.6 4.3 %fusion.32 = f32[64,896]{1,0:T(8,128)S(1)} fusion(bf16[64,4096]{1,0:T(8,128)(2,1)S(1)} %all_gather.3, bf16[4096,896]{1,0:T(8,128)(2,1)} %param.16), kind=kOutput, calls=%fused_computation.47 | convolution fusion | flops 469762048 | bytes 8093696 | tf_op jit(solution)/shard_map/dot_general | solution.py:52
  46.0 4.5 %all-reduce.1 = bf16[64,896]{1,0:T(8,128)(2,1)} all-reduce(f32[64,896]{1,0:T(8,128)S(1)} %fusion.32), channel_id=1, replica_groups=mesh['groups'=2,'role'=8,'head'=2] {'head'}, use_global_device_ids=true, to_apply=%region_2.3 | all-reduce | flops 57344 | bytes 344064 | tf_op jit(solution)/shard_map/psum | solution.py:57
  50.5 5.7 %all-to-all-start = ((bf16[8,8,896]{2,1,0:T(8,128)(2,1)}), bf16[8,8,896]{2,1,0:T(8,128)(2,1)S(1)}, u32[]{:S(2)}, u32[]{:S(2)}) async-start(bf16[8,8,896]{2,1,0:T(8,128)(2,1)} %bitcast.12), calls=%async_computation | async-start | bytes 229376 | tf_op jit(solution)/shard_map/all_to_all | solution.py:58
  56.2 0.0 copy-done.3
  56.2 0.1 copy.21
  56.3 0.1 eq.18
  56.4 0.1 fusion.27
  56.5 0.2 select_reduce_fusion.1
  56.7 0.1 reshape.43
  56.8 0.1 copy.23
  56.9 0.1 fusion.28
  57.0 6.5 %all-to-all-done = bf16[8,8,896]{2,1,0:T(8,128)(2,1)S(1)} async-done(((bf16[8,8,896]{2,1,0:T(8,128)(2,1)}), bf16[8,8,896]{2,1,0:T(8,128)(2,1)S(1)}, u32[]{:S(2)}, u32[]{:S(2)}) %all-to-all-start) | async-done | bytes 114720 | tf_op jit(solution)/shard_map/all_to_all | solution.py:58
  63.5 0.0 copy-done.1
  63.5 0.2 fusion.20
  63.7 0.0 copy-done.2
  63.7 0.3 convolution_convert_fusion
  64.0 0.1 reshape.44
  64.1 0.2 broadcast_in_dim.29
  64.3 15.9 %all_to_all.29 = bf16[16,2,7168]{2,1,0:T(2,128)(2,1)S(1)} all-to-all(bf16[16,2,7168]{2,1,0:T(2,128)(2,1)S(1)} %bitcast.28), channel_id=1, replica_groups=mesh['groups'=2,'role'=8,'head'=2] {'role','head'}, dimensions={0} | all-to-all | bytes 917504 | tf_op jit(solution)/shard_map/all_to_all | solution.py:86
  80.2 0.2 reshape.46
  80.3 7.8 %fusion.33 = f32[32,1024]{1,0:T(8,128)S(1)} fusion(bf16[32,7168]{1,0:T(8,128)(2,1)S(1)} %reshape.46, bf16[7168,1024]{1,0:T(8,128)(2,1)} %param.21), kind=kOutput, calls=%fused_computation.48 | convolution fusion | flops 469762048 | bytes 15269888 | tf_op jit(solution)/shard_map/dot_general | solution.py:89
  88.1 0.0 copy-start.4
  88.1 14.5 %fusion.12 = f32[32,7168]{1,0:T(8,128)S(1)} fusion(bf16[1024,7168]{1,0:T(8,128)(2,1)} %param.23, bf16[32,7168]{1,0:T(8,128)(2,1)S(1)} %reshape.46, bf16[7168,1024]{1,0:T(8,128)(2,1)} %param.22, f32[32,1024]{1,0:T(8,128)S(1)} %fusion.33), kind=kOutput, calls=%fused_computation.16 | convolution fusion | flops 939720704 | bytes 30867456 | tf_op jit(solution)/shard_map/dot_general | solution.py:92
  102.7 1.5 %reshape.47 = f32[16,2,7168]{2,1,0:T(2,128)} reshape(f32[32,7168]{1,0:T(8,128)S(1)} %fusion.12) | data formatting | bytes 1835008 | tf_op jit(solution)/shard_map/reshape | solution.py:92
  104.2 3.8 %all-to-all-start.2 = ((f32[16,2,7168]{2,1,0:T(2,128)}), f32[16,2,7168]{2,1,0:T(2,128)S(1)}, u32[]{:S(2)}, u32[]{:S(2)}) async-start(f32[16,2,7168]{2,1,0:T(2,128)} %reshape.47), calls=%async_computation.2 | async-start | bytes 1835008 | tf_op jit(solution)/shard_map/all_to_all | solution.py:95
  108.0 0.0 copy-done.4
  108.0 0.1 select_reduce_fusion
  108.1 20.7 %all-to-all-done.2 = f32[16,2,7168]{2,1,0:T(2,128)S(1)} async-done(((f32[16,2,7168]{2,1,0:T(2,128)}), f32[16,2,7168]{2,1,0:T(2,128)S(1)}, u32[]{:S(2)}, u32[]{:S(2)}) %all-to-all-start.2) | async-done | bytes 917536 | tf_op jit(solution)/shard_map/all_to_all | solution.py:95
  128.8 0.4 bitcast_reduce_fusion
  129.2 0.3 reshape.49
  129.5 1.0 fusion.1
  (3 shorter events, 0.0 us)
Async XLA Ops:
  0.0 1.0 copy-start
  5.6 50.6 %copy-start.3 = (s32[4,2]{0,1:T(2,128)S(1)}, s32[4,2]{0,1:T(2,128)}, u32[]{:S(2)}) copy-start(s32[4,2]{0,1:T(2,128)} %param.19) | copy-start | bytes 100
  5.6 57.9 %copy-start.1 = (bf16[4,7168]{1,0:T(4,128)(2,1)S(1)}, bf16[4,7168]{1,0:T(4,128)(2,1)}, u32[]{:S(2)}) copy-start(bf16[4,7168]{1,0:T(4,128)(2,1)} %param.17) | copy-start | bytes 172036
  5.7 58.0 %copy-start.2 = (f32[7168]{0:T(1024)S(1)}, f32[7168]{0:T(1024)}, u32[]{:S(2)}) copy-start(f32[7168]{0:T(1024)} %param.18) | copy-start | bytes 86020
  50.5 13.0 %all-to-all-start = ((bf16[8,8,896]{2,1,0:T(8,128)(2,1)}), bf16[8,8,896]{2,1,0:T(8,128)(2,1)S(1)}, u32[]{:S(2)}, u32[]{:S(2)}) async-start(bf16[8,8,896]{2,1,0:T(8,128)(2,1)} %bitcast.12), calls=%async_computation | async-start | bytes 229376 | tf_op jit(solution)/shard_map/all_to_all | solution.py:58
  88.1 19.8 %copy-start.4 = (f32[4,2]{0,1:T(2,128)S(1)}, f32[4,2]{0,1:T(2,128)}, u32[]{:S(2)}) copy-start(f32[4,2]{0,1:T(2,128)} %param.20) | copy-start | bytes 100
  104.2 24.6 %all-to-all-start.2 = ((f32[16,2,7168]{2,1,0:T(2,128)}), f32[16,2,7168]{2,1,0:T(2,128)S(1)}, u32[]{:S(2)}, u32[]{:S(2)}) async-start(f32[16,2,7168]{2,1,0:T(2,128)} %reshape.47), calls=%async_computation.2 | async-start | bytes 1835008 | tf_op jit(solution)/shard_map/all_to_all | solution.py:95
where the time goes:
time: 132 us; the launch traced here: 131 us
  blocking collectives  53.4 us (40%)
  matrix products  35.3 us (27%)
  waiting for transfers between devices  27.2 us (21%)
  starting transfers between devices  9.53 us (7%)
  local copies, waits for them, and re-layouts  3.66 us (3%)
    all_gather x1, blocking collectives, on_device(): lax.all_gather(head_out, 'role', axis=0, tiled=True)  33 us
    all_to_all x1, waiting for transfers between devices, on_device(): lax.all_to_all(expert_part, ('role', 'head'), split_axis=0, concat_axis=0...  20.7 us
    all_to_all x1, blocking collectives, on_device(): lax.all_to_all(outgoing, ('role', 'head'), split_axis=0, concat_axis=0, t...  15.9 us
    dot_general x1, matrix products, on_device(): jnp.dot(act_val, down_weight, preferred_element_type=jnp.float32)  14.5 us
    dot_general x1, matrix products, on_device(): jnp.dot(token_rows, gate_weight, preferred_element_type=jnp.float32)  7.79 us
    all_to_all x1, waiting for transfers between devices, on_device(): lax.all_to_all(summed_cols, 'role', split_axis=0, concat_axis=1, tiled=True)  6.51 us
    all_to_all x1, starting transfers between devices, on_device(): lax.all_to_all(summed_cols, 'role', split_axis=0, concat_axis=1, tiled=True)  5.72 us
    psum x1, blocking collectives, on_device(): summed_cols = lax.psum(partial_value, 'head').astype(jnp.bfloat16)  4.55 us
  transfers between devices with their start and end apart: 2, of which 2 were waited for; matrix products, arithmetic and copies ran while one was open for 1% of the time, Pallas kernels for 0%

commit v1 on v0

--- a/solution.py
+++ b/solution.py
@@ -1,6 +1,10 @@
+import functools
+
 import jax
 import jax.numpy as jnp
 from jax import lax
+from jax.experimental import pallas as pl
+from jax.experimental.pallas import tpu as pltpu
 from jax.sharding import PartitionSpec as P
 
 LATENT = 512
@@ -8,6 +12,9 @@
 VDIM = 128
 EXPERTS = 8
 CAP = 2
+F32 = jnp.float32
+BF16 = jnp.bfloat16
+VMEM = pltpu.VMEM
 
 
 def attend(queries, kv_cache, cache_lengths, uv_weight):
@@ -30,7 +37,159 @@
     return head_out.reshape(head_out.shape[0], -1)
 
 
-def on_device(
+def slot_positions(expert_ids):
+    flat_ids = expert_ids.reshape(-1)
+    n = flat_ids.shape[0]
+    earlier = lax.broadcasted_iota(jnp.int32, (n, n), 1) < lax.broadcasted_iota(
+        jnp.int32, (n, n), 0
+    )
+    same = flat_ids[:, None] == flat_ids[None, :]
+    rank = jnp.sum((earlier & same).astype(jnp.int32), axis=1)
+    return (flat_ids * CAP + rank).reshape(expert_ids.shape)
+
+
+def expert_kernel(mine_ref, other_ref, gate_ref, up_ref, down_ref, keep_ref, send_ref, x_ref, act_ref, *, wide, deep):
+    half = mine_ref.shape[0]
+    x_ref[:half, :] = mine_ref[...]
+    x_ref[half:, :] = other_ref[...]
+
+    def hidden_units(i, _):
+        cols = pl.ds(pl.multiple_of(i * wide, wide), wide)
+        gate = jnp.dot(x_ref[...], gate_ref[:, cols], preferred_element_type=F32)
+        up = jnp.dot(x_ref[...], up_ref[:, cols], preferred_element_type=F32)
+        act_ref[:, cols] = (gate / (1.0 + jnp.exp(-gate)) * up).astype(BF16)
+        return 0
+
+    lax.fori_loop(0, gate_ref.shape[1] // wide, hidden_units, 0)
+
+    def model_columns(i, _):
+        cols = pl.ds(pl.multiple_of(i * deep, deep), deep)
+        part = jnp.dot(act_ref[...], down_ref[:, cols], preferred_element_type=F32)
+        keep_ref[:, cols] = part[:half]
+        send_ref[:, cols] = part[half:].astype(send_ref.dtype)
+        return 0
+
+    lax.fori_loop(0, down_ref.shape[1] // deep, model_columns, 0)
+
+
+def run_experts(mine, other, gate, up, down):
+    rows, width = mine.shape
+    units = gate.shape[1]
+    gate, up, down = [pltpu.with_memory_space_constraint(w, VMEM) for w in (gate, up, down)]
+    whole = pl.BlockSpec(memory_space=VMEM)
+    return pl.pallas_call(
+        functools.partial(expert_kernel, wide=512, deep=1024),
+        out_shape=(
+            jax.ShapeDtypeStruct((rows, width), F32),
+            jax.ShapeDtypeStruct((rows, width), F32),
+        ),
+        in_specs=[whole] * 5,
+        out_specs=(whole, whole),
+        scratch_shapes=[VMEM((2 * rows, width), BF16), VMEM((2 * rows, units), BF16)],
+        compiler_params=pltpu.CompilerParams(vmem_limit_bytes=8 << 20),
+        name="experts",
+    )(mine, other, gate, up, down)
+
+
+def fast(
+    queries,
+    kv_cache,
+    cache_lengths,
+    uv_weight,
+    out_weight,
+    residual,
+    norm_gain,
+    expert_ids,
+    route_weights,
+    gate_weight,
+    up_weight,
+    down_weight,
+):
+    roles = lax.axis_size("role")
+    role = lax.axis_index("role")
+    core = lax.axis_index("head")
+    share = residual.shape[0]
+    width = residual.shape[1]
+    cols = width // roles
+    tokens = 2 * share
+    left = 4 * 128
+    head_out = attend(queries, kv_cache, cache_lengths, uv_weight)
+    positions = slot_positions(expert_ids)
+    by_role = residual.reshape(share, roles, cols).transpose(1, 0, 2)
+    note = jnp.pad(positions.astype(BF16), ((0, 0), (0, 126)))
+    note = jnp.broadcast_to(note[None], (roles, share, 128))
+    extra = jnp.concatenate(
+        [by_role[:, :, :left], jnp.concatenate([by_role[:, :, left:], note], axis=2)], axis=1
+    )
+    messages = []
+    for step in range(roles):
+        block = jnp.concatenate(
+            [head_out, lax.dynamic_index_in_dim(extra, role ^ step, 0, keepdims=False)], axis=1
+        )
+        if step:
+            block = lax.ppermute(block, "role", [(i, i ^ step) for i in range(roles)])
+        messages.append(block)
+    gathered = jnp.concatenate(messages, axis=0)
+    wide = head_out.shape[1]
+    partial_value = jnp.dot(gathered[:, :wide], out_weight, preferred_element_type=F32)
+    other_value = lax.ppermute(partial_value, "head", [(0, 1), (1, 0)])
+    attn_out = (partial_value + other_value).astype(BF16)
+    sides = gathered[:, wide:].reshape(roles, 2, share, left)
+    resid = jnp.concatenate([sides[:, 0], sides[:, 1, :, : cols - left]], axis=2)
+    own_pos = sides[:, 1, :, cols - left : cols - left + 2].astype(jnp.int32)
+    own_attn = lax.dynamic_slice_in_dim(
+        attn_out.reshape(roles, tokens, cols), core * share, share, 1
+    )
+    hidden = (resid.astype(F32) + own_attn.astype(F32)).astype(BF16).reshape(roles * share, cols)
+    own_pos = own_pos.reshape(roles * share, 2)
+    source = role ^ (lax.broadcasted_iota(jnp.int32, (1, 1, roles * share), 2) // share)
+    dest = lax.broadcasted_iota(jnp.int32, (roles, 1, 1), 0)
+    slot = lax.broadcasted_iota(jnp.int32, (1, roles * CAP, 1), 1)
+    want = dest * CAP + slot % CAP
+    placing = (slot // CAP == source) & (
+        (own_pos[None, None, :, 0] == want) | (own_pos[None, None, :, 1] == want)
+    )
+    slots = jnp.einsum("djt,tc->djc", placing.astype(BF16), hidden, preferred_element_type=F32)
+    slots = slots.astype(BF16)
+    own = lax.broadcasted_iota(jnp.int32, (1, share, 1), 1)
+    member = lax.broadcasted_iota(jnp.int32, (1, 1, roles * share), 2) % share
+    keeping = ((source == dest) & (member == own)).astype(BF16)
+    kept = jnp.einsum("dit,tc->dic", keeping, hidden, preferred_element_type=F32).astype(BF16)
+    kept = jnp.pad(kept, ((0, 0), (0, 0), (0, 1024 - cols))).reshape(roles, share, 4, 256)
+    kept = kept.transpose(0, 2, 1, 3).reshape(roles, 4 * share, 256)
+    outgoing = jnp.concatenate([slots, kept], axis=2)
+    received = lax.all_to_all(outgoing, "role", split_axis=0, concat_axis=0, tiled=True)
+    x = received[:, :, :cols].transpose(1, 0, 2).reshape(roles * CAP, width).astype(F32)
+    inverse = lax.rsqrt(jnp.mean(x * x, axis=1, keepdims=True) + 1e-06)
+    normed = (x * inverse * norm_gain[None, :]).astype(BF16)
+    hidden_own = (
+        received[:, :, cols:]
+        .reshape(roles, 4, share, 256)
+        .transpose(2, 0, 1, 3)
+        .reshape(share, roles, 1024)[:, :, :cols]
+        .reshape(share, width)
+    )
+    other = lax.ppermute(normed, "head", [(0, 1), (1, 0)])
+    keep, send = run_experts(normed, other, gate_weight, up_weight, down_weight)
+    summed = (keep + lax.ppermute(send, "head", [(0, 1), (1, 0)])).astype(BF16)
+    returned = lax.all_to_all(
+        summed.reshape(roles, CAP, width), "role", split_axis=0, concat_axis=0, tiled=True
+    )
+    slot_grid = lax.broadcasted_iota(jnp.int32, (share, EXPERTS * CAP), 1)
+    mixing = sum(
+        jnp.where(slot_grid == positions[:, k : k + 1], route_weights[:, k : k + 1], 0.0)
+        for k in range(2)
+    )
+    combined = jnp.dot(
+        mixing,
+        returned.reshape(EXPERTS * CAP, width).astype(F32),
+        precision=lax.Precision.HIGHEST,
+        preferred_element_type=F32,
+    )
+    return (hidden_own.astype(F32) + combined).astype(BF16)
+
+
+def general(
     queries,
     kv_cache,
     cache_lengths,
@@ -105,6 +264,13 @@
     return (hidden_f + combined).astype(jnp.bfloat16)
 
 
+def on_device(*arrays):
+    residual = arrays[5]
+    roles = lax.axis_size("role")
+    fits = roles == EXPERTS and lax.axis_size("head") == 2 and residual.shape[0] == 4
+    return (fast if fits and residual.shape[1] == roles * 896 else general)(*arrays)
+
+
 def solution(mesh):
     return jax.shard_map(
         on_device,

time: 132 us -> 95.3 us (0.72)
  blocking collectives: 53.4 us -> 15.4 us
  matrix products: 35.3 us -> 13.2 us
  local copies, waits for them, and re-layouts: 3.66 us -> 19.8 us
  Pallas kernels: 0 us -> 8.59 us
  waiting for transfers between devices: 27.2 us -> 19.9 us
  starting transfers between devices: 9.53 us -> 16.3 us
    all_gather x1 -> x0, blocking collectives: 33 us -> none  [on_device(): lax.all_gather(head_out, 'role', axis=0, tiled=True)]
    dot_general x5 -> x4, matrix products: 27.9 us -> 5.78 us  [the longest x1 4.44 us: fast(): jnp.dot(gathered[:, :wide], out_weight, preferred_element_type=F32)]
    all_to_all x2 -> x1, waiting for transfers between devices: 27.2 us -> 8.76 us  [fast(): lax.all_to_all(summed.reshape(roles, CAP, width), 'role', split_axis=0, c...]
    unnamed x11 -> x21, local copies, waits for them, and re-layouts: 1.1 us -> 16.5 us
    ppermute x0 -> x10, starting transfers between devices: none -> 12.9 us  [the longest x7 12.6 us: fast(): block = lax.ppermute(block, 'role', [(i, i ^ step) for i in range(roles)])]
    ppermute x0 -> x10, waiting for transfers between devices: none -> 11.2 us  [the longest x7 7.06 us: fast(): block = lax.ppermute(block, 'role', [(i, i ^ step) for i in range(roles)])]
    pallas_call x0 -> x1, Pallas kernels: none -> 8.59 us  [run_experts(): pl.pallas_call(functools.partial(expert_kernel, wide=512, deep=1024), out...]
    all_to_all x2 -> x1, starting transfers between devices: 9.53 us -> 3.4 us  [fast(): lax.all_to_all(summed.reshape(roles, CAP, width), 'role', split_axis=0, c...]
  transfers between devices with their start and end apart: 2 -> 11, of which waited for: 2 -> 6; matrix products, arithmetic and copies ran while one was open for 1% -> 1% of each run, Pallas kernels for 0% -> 0%
where the time goes in v1:
time: 95.3 us; the launch traced here: 94.7 us
  waiting for transfers between devices  19.9 us (21%)
  local copies, waits for them, and re-layouts  19.8 us (21%)
  starting transfers between devices  16.3 us (17%)
  blocking collectives  15.4 us (16%)
  matrix products  13.2 us (14%)
  Pallas kernels  8.59 us (9%)
  other arithmetic  1.17 us (1%)
    unnamed x21, local copies, waits for them, and re-layouts  16.5 us
    all_to_all x1, blocking collectives, fast(): lax.all_to_all(outgoing, 'role', split_axis=0, concat_axis=0, tiled=True)  15.4 us
    ppermute x7, starting transfers between devices, fast(): block = lax.ppermute(block, 'role', [(i, i ^ step) for i in range(roles)])  12.6 us
    all_to_all x1, waiting for transfers between devices, fast(): lax.all_to_all(summed.reshape(roles, CAP, width), 'role', split_axis=0, c...  8.76 us
    pallas_call x1, Pallas kernels, run_experts(): pl.pallas_call(functools.partial(expert_kernel, wide=512, deep=1024), out...  8.59 us
    ppermute x7, waiting for transfers between devices, fast(): block = lax.ppermute(block, 'role', [(i, i ^ step) for i in range(roles)])  7.06 us
    dot_general x1, matrix products, fast(): jnp.dot(gathered[:, :wide], out_weight, preferred_element_type=F32)  4.44 us
    all_to_all x1, starting transfers between devices, fast(): lax.all_to_all(summed.reshape(roles, CAP, width), 'role', split_axis=0, c...  3.4 us
  transfers between devices with their start and end apart: 11, of which 6 were waited for; matrix products, arithmetic and copies ran while one was open for 1% of the time, Pallas kernels for 0%

profile of v1, /device:TPU:0, one launch (start us, length us, event | category | flops | bytes accessed | tf_op | source)
XLA Modules:
  0.0 94.7 jit_solution(2029151277063650192)
XLA Ops:
  0.0 0.8 slice.68
  0.8 0.8 slice.69
  1.6 0.8 copy.36
  2.3 0.1 eq.126
  2.4 0.2 convert_reduce_fusion
  2.6 0.1 reduce_sum.31
  2.7 2.1 %fusion.9 = f32[8,32,256]{2,1,0:T(8,128)S(1)} fusion(bf16[8,32,576]{2,1,0:T(8,128)(2,1)S(1)} %copy-done, bf16[8,256,576]{1,2,0:T(8,128)(2,1)} %param.13, s32[8]{0:T(128)} %param.14), kind=kOutput, calls=%fused_computation.10 | convolution fusion | flops 75694080 | bytes 2916384 | tf_op jit(solution)/shard_map/thc,tsc->ths/dot_general | solution.py:23
  4.9 0.2 fusion.44
  5.1 2.3 %fusion.5 = bf16[8,32,512]{2,1,0:T(8,128)(2,1)S(1)} fusion(bf16[8,256,576]{1,2,0:T(8,128)(2,1)} %param.13, f32[8,32]{1,0:T(8,128)S(1)} %fusion.44, f32[8,32,256]{2,1,0:T(8,128)S(1)} %fusion.9), kind=kOutput, calls=%fused_computation.6 | convolution fusion | flops 67437056 | bytes 2887680 | tf_op jit(solution)/shard_map/ths,tsc->thc/dot_general | solution.py:31
  7.4 2.9 %fusion.10 = bf16[8,4096]{1,0:T(8,128)(2,1)S(1)} fusion(bf16[32,512,128]{2,1,0:T(8,128)(2,1)} %param.15, bf16[8,32,512]{2,1,0:T(8,128)(2,1)S(1)} %fusion.5), kind=kOutput, calls=%fused_computation.12 | convolution fusion | flops 33587200 | bytes 4521984 | tf_op jit(solution)/shard_map/thc,hcv->thv/dot_general | solution.py:34
  10.5 3.0 %collective-permute-start = (bf16[8,4608]{1,0:T(8,128)(2,1)S(1)}, bf16[8,4608]{1,0:T(8,128)(2,1)S(1)}, u32[]{:S(2)}, u32[]{:S(2)}) collective-permute-start(bf16[8,4608]{1,0:T(8,128)(2,1)S(1)} %get-tuple-element.14), channel_id=1, source_target_pairs={{0,2},{2,0},{4,6},{6,4},{8,10},{10,8},{12,14},{14,12},{1,3},{3,1},... | collective-permute-start | bytes 221192 | tf_op jit(solution)/shard_map/ppermute | solution.py:130
  13.5 1.6 %collective-permute-start.1 = (bf16[8,4608]{1,0:T(8,128)(2,1)S(1)}, bf16[8,4608]{1,0:T(8,128)(2,1)S(1)}, u32[]{:S(2)}, u32[]{:S(2)}) collective-permute-start(bf16[8,4608]{1,0:T(8,128)(2,1)S(1)} %get-tuple-element.15), channel_id=1, source_target_pairs={{0,4},{2,6},{4,0},{6,2},{8,12},{10,14},{12,8},{14,10},{1,5},{3,7},... | collective-permute-start | bytes 221192 | tf_op jit(solution)/shard_map/ppermute | solution.py:130
  15.1 3.0 %collective-permute-start.3 = (bf16[8,4608]{1,0:T(8,128)(2,1)S(1)}, bf16[8,4608]{1,0:T(8,128)(2,1)S(1)}, u32[]{:S(2)}, u32[]{:S(2)}) collective-permute-start(bf16[8,4608]{1,0:T(8,128)(2,1)S(1)} %get-tuple-element.17), channel_id=1, source_target_pairs={{0,8},{2,10},{4,12},{6,14},{8,0},{10,2},{12,4},{14,6},{1,9},{3,11}... | collective-permute-start | bytes 221192 | tf_op jit(solution)/shard_map/ppermute | solution.py:130
  18.1 1.3 %collective-permute-start.4 = (bf16[8,4608]{1,0:T(8,128)(2,1)S(1)}, bf16[8,4608]{1,0:T(8,128)(2,1)S(1)}, u32[]{:S(2)}, u32[]{:S(2)}) collective-permute-start(bf16[8,4608]{1,0:T(8,128)(2,1)S(1)} %get-tuple-element.18), channel_id=1, source_target_pairs={{0,10},{2,8},{4,14},{6,12},{8,2},{10,0},{12,6},{14,4},{1,11},{3,9}... | collective-permute-start | bytes 221192 | tf_op jit(solution)/shard_map/ppermute | solution.py:130
  19.4 0.1 broadcast_compare_fusion
  19.4 0.1 broadcast_add_fusion
  19.5 3.7 %collective-permute-start.5 = (bf16[8,4608]{1,0:T(8,128)(2,1)S(1)}, bf16[8,4608]{1,0:T(8,128)(2,1)S(1)}, u32[]{:S(2)}, u32[]{:S(2)}) collective-permute-start(bf16[8,4608]{1,0:T(8,128)(2,1)S(1)} %get-tuple-element.19), channel_id=1, source_target_pairs={{0,12},{2,14},{4,8},{6,10},{8,4},{10,6},{12,0},{14,2},{1,13},{3,15... | collective-permute-start | bytes 221192 | tf_op jit(solution)/shard_map/ppermute | solution.py:130
  23.2 0.1 collective-permute-start.6
  23.4 6.0 %collective-permute-done.4 = bf16[8,4608]{1,0:T(8,128)(2,1)S(1)} collective-permute-done((bf16[8,4608]{1,0:T(8,128)(2,1)S(1)}, bf16[8,4608]{1,0:T(8,128)(2,1)S(1)}, u32[]{:S(2)}, u32[]{:S(2)}) %collective-permute-start.4) | collective-permute-done | bytes 73760 | tf_op jit(solution)/shard_map/ppermute | solution.py:130
  29.3 1.1 %collective-permute-done.6 = bf16[8,4608]{1,0:T(8,128)(2,1)S(1)} collective-permute-done((bf16[8,4608]{1,0:T(8,128)(2,1)S(1)}, bf16[8,4608]{1,0:T(8,128)(2,1)S(1)}, u32[]{:S(2)}, u32[]{:S(2)}) %collective-permute-start.6) | collective-permute-done | bytes 73760 | tf_op jit(solution)/shard_map/ppermute | solution.py:130
  30.5 4.4 %fusion.11 = f32[64,896]{1,0:T(8,128)S(1)} fusion(bf16[4096,896]{1,0:T(8,128)(2,1)} %param.16, bf16[64,4608]{1,0:T(8,128)(2,1)S(1)} %constant_dynamic-update-slice_fusion), kind=kOutput, calls=%fused_computation.16 | convolution fusion | flops 469762048 | bytes 8093696 | tf_op jit(solution)/shard_map/dot_general | solution.py:134
  34.9 0.0 copy-start.4
  35.0 0.1 collective-permute-start.7
  35.0 0.1 copy.44
  35.2 0.1 copy.39
  35.2 0.1 reshape.295
  35.4 1.1 %collective-permute-done.7 = f32[64,896]{1,0:T(8,128)S(1)} collective-permute-done((f32[64,896]{1,0:T(8,128)S(1)}, f32[64,896]{1,0:T(8,128)S(1)}, u32[]{:S(2)}, u32[]{:S(2)}) %collective-permute-start.7) | collective-permute-done | bytes 229408 | tf_op jit(solution)/shard_map/ppermute | solution.py:135
  36.5 0.1 add_convert_fusion.2
  36.6 0.1 convolution_convert_fusion.2
  36.8 0.1 copy.52
  36.9 0.3 convolution_convert_fusion
  37.2 15.4 %all_to_all.10 = bf16[8,16,1152]{2,1,0:T(8,128)(2,1)S(1)} all-to-all(bf16[8,16,1152]{2,1,0:T(8,128)(2,1)S(1)} %pad_maximum_fusion), channel_id=1, replica_groups=mesh['groups'=2,'role'=8,'head'=2] {'role'}, dimensions={0} | all-to-all | bytes 589824 | tf_op jit(solution)/shard_map/all_to_all | solution.py:161
  52.7 0.2 fusion.13
  52.9 0.1 multiply_convert_fusion.mine_ref
  53.0 0.1 collective-permute-start.8
  53.1 1.5 %collective-permute-done.8.other_ref = bf16[16,7168]{1,0:T(8,128)(2,1)S(1)} collective-permute-done((bf16[16,7168]{1,0:T(8,128)(2,1)S(1)}, bf16[16,7168]{1,0:T(8,128)(2,1)S(1)}, u32[]{:S(2)}, u32[]{:S(2)}) %collective-permute-start.8) | collective-permute-done | bytes 229408 | tf_op jit(solution)/shard_map/ppermute | solution.py:172
  54.6 5.2 %copy-done.1 = bf16[7168,1024]{1,0:T(8,128)(2,1)S(1)} copy-done((bf16[7168,1024]{1,0:T(8,128)(2,1)S(1)}, bf16[7168,1024]{1,0:T(8,128)(2,1)}, u32[]{:S(2)}) %copy-start.1) | copy-done | bytes 14680088
  59.8 5.2 %copy-done.2 = bf16[7168,1024]{1,0:T(8,128)(2,1)S(1)} copy-done((bf16[7168,1024]{1,0:T(8,128)(2,1)S(1)}, bf16[7168,1024]{1,0:T(8,128)(2,1)}, u32[]{:S(2)}) %copy-start.2) | copy-done | bytes 14680088
  64.9 5.2 %copy-done.3 = bf16[1024,7168]{1,0:T(8,128)(2,1)S(1)} copy-done((bf16[1024,7168]{1,0:T(8,128)(2,1)S(1)}, bf16[1024,7168]{1,0:T(8,128)(2,1)}, u32[]{:S(2)}) %copy-start.3) | copy-done | bytes 14680088
  70.1 8.6 %experts.1 = (f32[16,7168]{1,0:T(8,128)S(1)}, f32[16,7168]{1,0:T(8,128)S(1)}) custom-call(bf16[16,7168]{1,0:T(8,128)(2,1)S(1)} %multiply_convert_fusion.mine_ref, bf16[16,7168]{1,0:T(8,128)(2,1)S(1)} %collective-permute-done.8.other_ref, bf16[7168,1024]{1,0:T(8,128)(2,1)S(1)} %copy-done.1, bf16[7168,1024]{1,0:T(8,128)(2,1)S(1)} %copy-done.2, ...), custom_call_target="tpu_custom_call" | custom-call | tf_op jit(solution)/shard_map/experts/pallas_call | solution.py:80
  78.7 0.2 collective-permute-start.9
  78.8 0.2 slice_reduce_fusion.1
  79.0 1.5 %collective-permute-done.9 = f32[16,7168]{1,0:T(8,128)S(1)} collective-permute-done((f32[16,7168]{1,0:T(8,128)S(1)}, f32[16,7168]{1,0:T(8,128)S(1)}, u32[]{:S(2)}, u32[]{:S(2)}) %collective-permute-start.9) | collective-permute-done | bytes 458784 | tf_op jit(solution)/shard_map/ppermute | solution.py:174
  80.6 0.8 reshape.293
  81.3 3.4 %all-to-all-start.1 = ((bf16[8,2,7168]{2,1,0:T(2,128)(2,1)}), bf16[8,2,7168]{2,1,0:T(2,128)(2,1)S(1)}, u32[]{:S(2)}, u32[]{:S(2)}) async-start(bf16[8,2,7168]{2,1,0:T(2,128)(2,1)} %reshape.293), calls=%async_computation.1 | async-start | bytes 458752 | tf_op jit(solution)/shard_map/all_to_all | solution.py:175
  84.9 8.8 %all-to-all-done.1 = bf16[8,2,7168]{2,1,0:T(2,128)(2,1)S(1)} async-done(((bf16[8,2,7168]{2,1,0:T(2,128)(2,1)}), bf16[8,2,7168]{2,1,0:T(2,128)(2,1)S(1)}, u32[]{:S(2)}, u32[]{:S(2)}) %all-to-all-start.1) | async-done | bytes 229408 | tf_op jit(solution)/shard_map/all_to_all | solution.py:175
  93.7 0.1 reshape.294
  93.8 0.9 fusion.1
  (54 shorter events, 0.7 us)
Async XLA Ops:
  0.0 2.7 %copy-start = (bf16[8,32,576]{2,1,0:T(8,128)(2,1)S(1)}, bf16[8,32,576]{2,1,0:T(8,128)(2,1)}, u32[]{:S(2)}) copy-start(bf16[8,32,576]{2,1,0:T(8,128)(2,1)} %param.12) | copy-start | bytes 884740
  10.5 9.1 %collective-permute-start = (bf16[8,4608]{1,0:T(8,128)(2,1)S(1)}, bf16[8,4608]{1,0:T(8,128)(2,1)S(1)}, u32[]{:S(2)}, u32[]{:S(2)}) collective-permute-start(bf16[8,4608]{1,0:T(8,128)(2,1)S(1)} %get-tuple-element.14), channel_id=1, source_target_pairs={{0,2},{2,0},{4,6},{6,4},{8,10},{10,8},{12,14},{14,12},{1,3},{3,1},... | collective-permute-start | bytes 221192 | tf_op jit(solution)/shard_map/ppermute | solution.py:130
  13.5 9.7 %collective-permute-start.1 = (bf16[8,4608]{1,0:T(8,128)(2,1)S(1)}, bf16[8,4608]{1,0:T(8,128)(2,1)S(1)}, u32[]{:S(2)}, u32[]{:S(2)}) collective-permute-start(bf16[8,4608]{1,0:T(8,128)(2,1)S(1)} %get-tuple-element.15), channel_id=1, source_target_pairs={{0,4},{2,6},{4,0},{6,2},{8,12},{10,14},{12,8},{14,10},{1,5},{3,7},... | collective-permute-start | bytes 221192 | tf_op jit(solution)/shard_map/ppermute | solution.py:130
  15.1 8.2 %collective-permute-start.2 = (bf16[8,4608]{1,0:T(8,128)(2,1)S(1)}, bf16[8,4608]{1,0:T(8,128)(2,1)S(1)}, u32[]{:S(2)}, u32[]{:S(2)}) collective-permute-start(bf16[8,4608]{1,0:T(8,128)(2,1)S(1)} %get-tuple-element.16), channel_id=1, source_target_pairs={{0,6},{2,4},{4,2},{6,0},{8,14},{10,12},{12,10},{14,8},{1,7},{3,5},... | collective-permute-start | bytes 221192 | tf_op jit(solution)/shard_map/ppermute | solution.py:130
  15.1 8.3 %collective-permute-start.3 = (bf16[8,4608]{1,0:T(8,128)(2,1)S(1)}, bf16[8,4608]{1,0:T(8,128)(2,1)S(1)}, u32[]{:S(2)}, u32[]{:S(2)}) collective-permute-start(bf16[8,4608]{1,0:T(8,128)(2,1)S(1)} %get-tuple-element.17), channel_id=1, source_target_pairs={{0,8},{2,10},{4,12},{6,14},{8,0},{10,2},{12,4},{14,6},{1,9},{3,11}... | collective-permute-start | bytes 221192 | tf_op jit(solution)/shard_map/ppermute | solution.py:130
  18.1 11.3 %collective-permute-start.4 = (bf16[8,4608]{1,0:T(8,128)(2,1)S(1)}, bf16[8,4608]{1,0:T(8,128)(2,1)S(1)}, u32[]{:S(2)}, u32[]{:S(2)}) collective-permute-start(bf16[8,4608]{1,0:T(8,128)(2,1)S(1)} %get-tuple-element.18), channel_id=1, source_target_pairs={{0,10},{2,8},{4,14},{6,12},{8,2},{10,0},{12,6},{14,4},{1,11},{3,9}... | collective-permute-start | bytes 221192 | tf_op jit(solution)/shard_map/ppermute | solution.py:130
  19.5 9.8 %collective-permute-start.5 = (bf16[8,4608]{1,0:T(8,128)(2,1)S(1)}, bf16[8,4608]{1,0:T(8,128)(2,1)S(1)}, u32[]{:S(2)}, u32[]{:S(2)}) collective-permute-start(bf16[8,4608]{1,0:T(8,128)(2,1)S(1)} %get-tuple-element.19), channel_id=1, source_target_pairs={{0,12},{2,14},{4,8},{6,10},{8,4},{10,6},{12,0},{14,2},{1,13},{3,15... | collective-permute-start | bytes 221192 | tf_op jit(solution)/shard_map/ppermute | solution.py:130
  23.2 7.2 %collective-permute-start.6 = (bf16[8,4608]{1,0:T(8,128)(2,1)S(1)}, bf16[8,4608]{1,0:T(8,128)(2,1)S(1)}, u32[]{:S(2)}, u32[]{:S(2)}) collective-permute-start(bf16[8,4608]{1,0:T(8,128)(2,1)S(1)} %get-tuple-element.13), channel_id=1, source_target_pairs={{0,14},{2,12},{4,10},{6,8},{8,6},{10,4},{12,2},{14,0},{1,15},{3,13... | collective-permute-start | bytes 221192 | tf_op jit(solution)/shard_map/ppermute | solution.py:130
  34.9 18.0 %copy-start.4 = (f32[7168]{0:T(1024)S(1)}, f32[7168]{0:T(1024)}, u32[]{:S(2)}) copy-start(f32[7168]{0:T(1024)} %param.18) | copy-start | bytes 86020
  35.0 1.6 %collective-permute-start.7 = (f32[64,896]{1,0:T(8,128)S(1)}, f32[64,896]{1,0:T(8,128)S(1)}, u32[]{:S(2)}, u32[]{:S(2)}) collective-permute-start(f32[64,896]{1,0:T(8,128)S(1)} %fusion.11), channel_id=1, source_target_pairs={{0,1},{1,0},{2,3},{3,2},{4,5},{5,4},{6,7},{7,6},{8,9},{9,8},{10,11... | collective-permute-start | bytes 688136 | tf_op jit(solution)/shard_map/ppermute | solution.py:135
  52.9 31.9 %copy-start.5 = (f32[4,2]{0,1:T(2,128)S(1)}, f32[4,2]{0,1:T(2,128)}, u32[]{:S(2)}) copy-start(f32[4,2]{0,1:T(2,128)} %param.20) | copy-start | bytes 100
  53.0 1.6 %collective-permute-start.8 = (bf16[16,7168]{1,0:T(8,128)(2,1)S(1)}, bf16[16,7168]{1,0:T(8,128)(2,1)S(1)}, u32[]{:S(2)}, u32[]{:S(2)}) collective-permute-start(bf16[16,7168]{1,0:T(8,128)(2,1)S(1)} %multiply_convert_fusion.mine_ref), channel_id=1, source_target_pairs={{0,1},{1,0},{2,3},{3,2},{4,5},{5,4},{6,7},{7,6},{8,9},{9,8},{10,11... | collective-permute-start | bytes 688136 | tf_op jit(solution)/shard_map/ppermute | solution.py:172
  54.6 5.2 %copy-start.1 = (bf16[7168,1024]{1,0:T(8,128)(2,1)S(1)}, bf16[7168,1024]{1,0:T(8,128)(2,1)}, u32[]{:S(2)}) copy-start(bf16[7168,1024]{1,0:T(8,128)(2,1)} %gate_ref.1) | copy-start | bytes 44040196
  59.8 5.2 %copy-start.2 = (bf16[7168,1024]{1,0:T(8,128)(2,1)S(1)}, bf16[7168,1024]{1,0:T(8,128)(2,1)}, u32[]{:S(2)}) copy-start(bf16[7168,1024]{1,0:T(8,128)(2,1)} %up_ref.1) | copy-start | bytes 44040196
  64.9 5.2 %copy-start.3 = (bf16[1024,7168]{1,0:T(8,128)(2,1)S(1)}, bf16[1024,7168]{1,0:T(8,128)(2,1)}, u32[]{:S(2)}) copy-start(bf16[1024,7168]{1,0:T(8,128)(2,1)} %down_ref.1) | copy-start | bytes 44040196
  78.7 1.8 %collective-permute-start.9 = (f32[16,7168]{1,0:T(8,128)S(1)}, f32[16,7168]{1,0:T(8,128)S(1)}, u32[]{:S(2)}, u32[]{:S(2)}) collective-permute-start(f32[16,7168]{1,0:T(8,128)S(1)} %get-tuple-element.8), channel_id=1, source_target_pairs={{0,1},{1,0},{2,3},{3,2},{4,5},{5,4},{6,7},{7,6},{8,9},{9,8},{10,11... | collective-permute-start | bytes 1376264 | tf_op jit(solution)/shard_map/ppermute | solution.py:174
  81.3 12.4 %all-to-all-start.1 = ((bf16[8,2,7168]{2,1,0:T(2,128)(2,1)}), bf16[8,2,7168]{2,1,0:T(2,128)(2,1)S(1)}, u32[]{:S(2)}, u32[]{:S(2)}) async-start(bf16[8,2,7168]{2,1,0:T(2,128)(2,1)} %reshape.293), calls=%async_computation.1 | async-start | bytes 458752 | tf_op jit(solution)/shard_map/all_to_all | solution.py:175

commit v2 on v1

--- a/solution.py
+++ b/solution.py
@@ -48,47 +48,199 @@
     return (flat_ids * CAP + rank).reshape(expert_ids.shape)
 
 
-def expert_kernel(mine_ref, other_ref, gate_ref, up_ref, down_ref, keep_ref, send_ref, x_ref, act_ref, *, wide, deep):
-    half = mine_ref.shape[0]
+def load_kernel(gate_hbm, up_hbm, after_ref, both_ref, sems):
+    copies = (
+        pltpu.make_async_copy(gate_hbm, both_ref.at[0], sems.at[0]),
+        pltpu.make_async_copy(up_hbm, both_ref.at[1], sems.at[1]),
+    )
+    for copy in copies:
+        copy.start()
+    for copy in copies:
+        copy.wait()
+
+
+def load(gate, up, after):
+    gate, up = [pltpu.with_memory_space_constraint(w, pltpu.HBM) for w in (gate, up)]
+    return pl.pallas_call(
+        load_kernel,
+        out_shape=VMEM((2,) + gate.shape, gate.dtype),
+        in_specs=[pl.BlockSpec(memory_space=pltpu.HBM)] * 2 + [pl.BlockSpec(memory_space=pl.ANY)],
+        out_specs=pl.BlockSpec(memory_space=VMEM),
+        scratch_shapes=[pltpu.SemaphoreType.DMA((2,))],
+        compiler_params=pltpu.CompilerParams(vmem_limit_bytes=1 << 20),
+        cost_estimate=pl.CostEstimate(
+            flops=0, bytes_accessed=2 * (gate.size + up.size), transcendentals=0
+        ),
+        name="load",
+    )(gate, up, after)
+
+
+def project_kernel(*refs):
+    messages, (weight_hbm, out_ref, weight_ref, sems) = refs[:-4], refs[-4:]
+    chunks, deep, _ = weight_ref.shape
+
+    def fetch(i):
+        return pltpu.make_async_copy(
+            weight_hbm.at[pl.ds(i * deep, deep), :], weight_ref.at[i], sems.at[i]
+        )
+
+    for i in range(chunks):
+        fetch(i).start()
+    for i in range(chunks):
+        rows = jnp.concatenate(
+            [m[:, i * deep : (i + 1) * deep].astype(F32) for m in messages], axis=0
+        ).astype(BF16)
+        fetch(i).wait()
+        part = jnp.dot(rows, weight_ref[i], preferred_element_type=F32)
+        if i:
+            out_ref[...] += part
+        else:
+            out_ref[...] = part
+
+
+def project(messages, weight):
+    depth, cols = weight.shape
+    tokens = sum(m.shape[0] for m in messages)
+    chunks = 4
+    whole = pl.BlockSpec(memory_space=VMEM)
+    return pl.pallas_call(
+        project_kernel,
+        out_shape=jax.ShapeDtypeStruct((tokens, cols), F32),
+        in_specs=[whole] * len(messages) + [pl.BlockSpec(memory_space=pltpu.HBM)],
+        out_specs=whole,
+        scratch_shapes=[
+            VMEM((chunks, depth // chunks, cols), BF16),
+            pltpu.SemaphoreType.DMA((chunks,)),
+        ],
+        compiler_params=pltpu.CompilerParams(vmem_limit_bytes=12 << 20),
+        cost_estimate=pl.CostEstimate(
+            flops=2 * tokens * depth * cols, bytes_accessed=2 * depth * cols, transcendentals=0
+        ),
+        name="project",
+    )(*messages, pltpu.with_memory_space_constraint(weight, pltpu.HBM))
+
+
+def dispatch_kernel(place_ref, mine_ref, other_ref, *refs):
+    messages, out_ref = refs[:-1], refs[-1]
+    role, core = place_ref[0], place_ref[1]
+    roles = len(messages)
+    tokens, cols = mine_ref.shape
+    each = tokens // roles
+    share = each // 2
+    wide = messages[0].shape[1]
+    left = 4 * 128
+    slots = roles * CAP
+    firsts, seconds = [], []
+    for m in messages:
+        side = m[:, wide - left :].astype(F32)
+        turned = pltpu.roll(side, share, 0)
+        firsts.append(jnp.where(core == 0, side, turned))
+        seconds.append(jnp.where(core == 0, turned, side))
+    second = jnp.concatenate(seconds, axis=0)
+    resid = jnp.concatenate([jnp.concatenate(firsts, axis=0), second[:, : cols - left]], axis=1)
+    notes = second[:, cols - left :].T
+    attn_out = (mine_ref[...] + other_ref[...]).astype(BF16)
+    hidden = (resid + attn_out.astype(F32)).astype(BF16)
+    token = lax.broadcasted_iota(jnp.int32, (1, tokens), 1)
+    source = role ^ (token // each)
+    member = token % each
+    row = lax.broadcasted_iota(jnp.int32, (roles * slots, 1), 0)
+    dest, slot = row // slots, row % slots
+    want = (dest * CAP + slot % CAP).astype(F32)
+    placing = (
+        (slot // CAP == source)
+        & (member // share == core)
+        & ((notes[0:1, :] == want) | (notes[1:2, :] == want))
+    )
+    keeping = (dest == source) & (member == core * share + slot % share)
+    placed = jnp.dot(
+        jnp.where(placing, 1.0, 0.0).astype(BF16), hidden, preferred_element_type=F32
+    ).astype(BF16)
+    kept = jnp.dot(jnp.where(keeping, 1.0, 0.0).astype(BF16), hidden, preferred_element_type=F32)
+    kept = jnp.concatenate([kept, jnp.zeros((roles * slots, 1024 - cols), F32)], axis=1)
+    group = slot // share
+    extra = kept[:, :256]
+    for g in range(1, 4):
+        extra = jnp.where(group == g, kept[:, g * 256 : (g + 1) * 256], extra)
+    extra = extra.astype(BF16)
+    for d in range(roles):
+        out_ref[d, :, :cols] = placed[d * slots : (d + 1) * slots]
+        out_ref[d, :, cols:] = extra[d * slots : (d + 1) * slots]
+
+
+def dispatch(place, mine, other, messages):
+    roles = len(messages)
+    cols = mine.shape[1]
+    whole = pl.BlockSpec(memory_space=VMEM)
+    return pl.pallas_call(
+        dispatch_kernel,
+        out_shape=jax.ShapeDtypeStruct((roles, roles * CAP, cols + 256), BF16),
+        in_specs=[pl.BlockSpec(memory_space=pltpu.SMEM)] + [whole] * (2 + roles),
+        out_specs=whole,
+        compiler_params=pltpu.CompilerParams(vmem_limit_bytes=6 << 20),
+        name="dispatch",
+    )(place, mine, other, *messages)
+
+
+def expert_kernel(
+    mine_ref, other_ref, both_ref, down_hbm, keep_ref, send_ref,
+    x_ref, act_ref, down_ref, out_sems
+):
+    half, width = mine_ref.shape
+    outs, _, broad = down_ref.shape
+
+    def fetch_down(i):
+        cols = pl.ds(i * broad, broad)
+        return pltpu.make_async_copy(down_hbm.at[:, cols], down_ref.at[i], out_sems.at[i])
+
+    for i in range(outs):
+        fetch_down(i).start()
     x_ref[:half, :] = mine_ref[...]
     x_ref[half:, :] = other_ref[...]
+    wide = 512
 
     def hidden_units(i, _):
         cols = pl.ds(pl.multiple_of(i * wide, wide), wide)
-        gate = jnp.dot(x_ref[...], gate_ref[:, cols], preferred_element_type=F32)
-        up = jnp.dot(x_ref[...], up_ref[:, cols], preferred_element_type=F32)
+        gate = jnp.dot(x_ref[...], both_ref[0, :, cols], preferred_element_type=F32)
+        up = jnp.dot(x_ref[...], both_ref[1, :, cols], preferred_element_type=F32)
         act_ref[:, cols] = (gate / (1.0 + jnp.exp(-gate)) * up).astype(BF16)
         return 0
 
-    lax.fori_loop(0, gate_ref.shape[1] // wide, hidden_units, 0)
-
-    def model_columns(i, _):
-        cols = pl.ds(pl.multiple_of(i * deep, deep), deep)
-        part = jnp.dot(act_ref[...], down_ref[:, cols], preferred_element_type=F32)
-        keep_ref[:, cols] = part[:half]
-        send_ref[:, cols] = part[half:].astype(send_ref.dtype)
-        return 0
-
-    lax.fori_loop(0, down_ref.shape[1] // deep, model_columns, 0)
-
-
-def run_experts(mine, other, gate, up, down):
+    lax.fori_loop(0, both_ref.shape[2] // wide, hidden_units, 0)
+    for i in range(outs):
+        fetch_down(i).wait()
+        part = jnp.dot(act_ref[...], down_ref[i], preferred_element_type=F32)
+        keep_ref[:, i * broad : (i + 1) * broad] = part[:half]
+        send_ref[:, i * broad : (i + 1) * broad] = part[half:].astype(send_ref.dtype)
+
+
+def run_experts(mine, other, both, down):
     rows, width = mine.shape
-    units = gate.shape[1]
-    gate, up, down = [pltpu.with_memory_space_constraint(w, VMEM) for w in (gate, up, down)]
+    units = both.shape[2]
+    outs = 7
+    both = pltpu.with_memory_space_constraint(both, VMEM)
+    down = pltpu.with_memory_space_constraint(down, pltpu.HBM)
     whole = pl.BlockSpec(memory_space=VMEM)
     return pl.pallas_call(
-        functools.partial(expert_kernel, wide=512, deep=1024),
+        expert_kernel,
         out_shape=(
             jax.ShapeDtypeStruct((rows, width), F32),
             jax.ShapeDtypeStruct((rows, width), F32),
         ),
-        in_specs=[whole] * 5,
+        in_specs=[whole] * 3 + [pl.BlockSpec(memory_space=pltpu.HBM)],
         out_specs=(whole, whole),
-        scratch_shapes=[VMEM((2 * rows, width), BF16), VMEM((2 * rows, units), BF16)],
-        compiler_params=pltpu.CompilerParams(vmem_limit_bytes=8 << 20),
+        scratch_shapes=[
+            VMEM((2 * rows, width), BF16),
+            VMEM((2 * rows, units), BF16),
+            VMEM((outs, units, width // outs), BF16),
+            pltpu.SemaphoreType.DMA((outs,)),
+        ],
+        compiler_params=pltpu.CompilerParams(vmem_limit_bytes=18 << 20),
+        cost_estimate=pl.CostEstimate(
+            flops=12 * rows * width * units, bytes_accessed=2 * width * units, transcendentals=0
+        ),
         name="experts",
-    )(mine, other, gate, up, down)
+    )(mine, other, both, down)
 
 
 def fast(
@@ -114,6 +266,7 @@
     tokens = 2 * share
     left = 4 * 128
     head_out = attend(queries, kv_cache, cache_lengths, uv_weight)
+    place, head_out = lax.optimization_barrier((jnp.stack([role, core]), head_out))
     positions = slot_positions(expert_ids)
     by_role = residual.reshape(share, roles, cols).transpose(1, 0, 2)
     note = jnp.pad(positions.astype(BF16), ((0, 0), (0, 126)))
@@ -129,35 +282,11 @@
         if step:
             block = lax.ppermute(block, "role", [(i, i ^ step) for i in range(roles)])
         messages.append(block)
-    gathered = jnp.concatenate(messages, axis=0)
-    wide = head_out.shape[1]
-    partial_value = jnp.dot(gathered[:, :wide], out_weight, preferred_element_type=F32)
+    both_weights = load(gate_weight, up_weight, head_out)
+    messages, both_weights = lax.optimization_barrier((messages, both_weights))
+    partial_value = project(messages, out_weight)
     other_value = lax.ppermute(partial_value, "head", [(0, 1), (1, 0)])
-    attn_out = (partial_value + other_value).astype(BF16)
-    sides = gathered[:, wide:].reshape(roles, 2, share, left)
-    resid = jnp.concatenate([sides[:, 0], sides[:, 1, :, : cols - left]], axis=2)
-    own_pos = sides[:, 1, :, cols - left : cols - left + 2].astype(jnp.int32)
-    own_attn = lax.dynamic_slice_in_dim(
-        attn_out.reshape(roles, tokens, cols), core * share, share, 1
-    )
-    hidden = (resid.astype(F32) + own_attn.astype(F32)).astype(BF16).reshape(roles * share, cols)
-    own_pos = own_pos.reshape(roles * share, 2)
-    source = role ^ (lax.broadcasted_iota(jnp.int32, (1, 1, roles * share), 2) // share)
-    dest = lax.broadcasted_iota(jnp.int32, (roles, 1, 1), 0)
-    slot = lax.broadcasted_iota(jnp.int32, (1, roles * CAP, 1), 1)
-    want = dest * CAP + slot % CAP
-    placing = (slot // CAP == source) & (
-        (own_pos[None, None, :, 0] == want) | (own_pos[None, None, :, 1] == want)
-    )
-    slots = jnp.einsum("djt,tc->djc", placing.astype(BF16), hidden, preferred_element_type=F32)
-    slots = slots.astype(BF16)
-    own = lax.broadcasted_iota(jnp.int32, (1, share, 1), 1)
-    member = lax.broadcasted_iota(jnp.int32, (1, 1, roles * share), 2) % share
-    keeping = ((source == dest) & (member == own)).astype(BF16)
-    kept = jnp.einsum("dit,tc->dic", keeping, hidden, preferred_element_type=F32).astype(BF16)
-    kept = jnp.pad(kept, ((0, 0), (0, 0), (0, 1024 - cols))).reshape(roles, share, 4, 256)
-    kept = kept.transpose(0, 2, 1, 3).reshape(roles, 4 * share, 256)
-    outgoing = jnp.concatenate([slots, kept], axis=2)
+    outgoing = dispatch(place, partial_value, other_value, messages)
     received = lax.all_to_all(outgoing, "role", split_axis=0, concat_axis=0, tiled=True)
     x = received[:, :, :cols].transpose(1, 0, 2).reshape(roles * CAP, width).astype(F32)
     inverse = lax.rsqrt(jnp.mean(x * x, axis=1, keepdims=True) + 1e-06)
@@ -170,7 +299,7 @@
         .reshape(share, width)
     )
     other = lax.ppermute(normed, "head", [(0, 1), (1, 0)])
-    keep, send = run_experts(normed, other, gate_weight, up_weight, down_weight)
+    keep, send = run_experts(normed, other, both_weights, down_weight)
     summed = (keep + lax.ppermute(send, "head", [(0, 1), (1, 0)])).astype(BF16)
     returned = lax.all_to_all(
         summed.reshape(roles, CAP, width), "role", split_axis=0, concat_axis=0, tiled=True

time: 95.3 us -> 82.2 us (0.86)
  local copies, waits for them, and re-layouts: 19.8 us -> 3.73 us
  Pallas kernels: 8.59 us -> 22.6 us
  waiting for transfers between devices: 19.9 us -> 13.2 us
  matrix products: 13.2 us -> 8.3 us
    unnamed x21 -> x10, local copies, waits for them, and re-layouts: 16.5 us -> 0.82 us
    pallas_call x1 -> x4, Pallas kernels: 8.59 us -> 22.6 us  [the longest x1 9.37 us: load(): pl.pallas_call(load_kernel, out_shape=VMEM((2,) + gate.shape, gate.dtype)...]
    ppermute x7, waiting for transfers between devices: 7.06 us -> 0.02 us  [fast(): block = lax.ppermute(block, 'role', [(i, i ^ step) for i in range(roles)])]
    dot_general x3 -> x0, matrix products: 4.84 us -> none  [the longest x1 4.44 us: fast(): jnp.dot(gathered[:, :wide], out_weight, preferred_element_type=F32)]
  transfers between devices with their start and end apart: 11 -> 11, of which waited for: 6 -> 4; matrix products, arithmetic and copies ran while one was open for 1% -> 0% of each run, Pallas kernels for 0% -> 11%
where the time goes in v2:
time: 82.2 us; the launch traced here: 81.7 us
  Pallas kernels  22.6 us (27%)
  starting transfers between devices  16.6 us (20%)
  blocking collectives  16.1 us (20%)
  waiting for transfers between devices  13.2 us (16%)
  matrix products  8.3 us (10%)
  local copies, waits for them, and re-layouts  3.73 us (5%)
  other arithmetic  0.96 us (1%)
    all_to_all x1, blocking collectives, fast(): lax.all_to_all(outgoing, 'role', split_axis=0, concat_axis=0, tiled=True)  16.1 us
    ppermute x7, starting transfers between devices, fast(): block = lax.ppermute(block, 'role', [(i, i ^ step) for i in range(roles)])  12.8 us
    pallas_call x1, Pallas kernels, load(): pl.pallas_call(load_kernel, out_shape=VMEM((2,) + gate.shape, gate.dtype)...  9.37 us
    all_to_all x1, waiting for transfers between devices, fast(): lax.all_to_all(summed.reshape(roles, CAP, width), 'role', split_axis=0, c...  8.76 us
    pallas_call x1, Pallas kernels, run_experts(): pl.pallas_call(expert_kernel, out_shape=(jax.ShapeDtypeStruct((rows, widt...  8.66 us
    pallas_call x1, Pallas kernels, project(): pl.pallas_call(project_kernel, out_shape=jax.ShapeDtypeStruct((tokens, co...  3.65 us
    all_to_all x1, starting transfers between devices, fast(): lax.all_to_all(summed.reshape(roles, CAP, width), 'role', split_axis=0, c...  3.4 us
    dot_general x1, matrix products, attend(): jnp.einsum('thc,hcv->thv', latent_out, uv_weight, preferred_element_type=...  2.91 us
  transfers between devices with their start and end apart: 11, of which 4 were waited for; matrix products, arithmetic and copies ran while one was open for 0% of the time, Pallas kernels for 11%

profile of v2, /device:TPU:0, one launch (start us, length us, event | category | flops | bytes accessed | tf_op | source)
XLA Modules:
  0.0 81.7 jit_solution(1140463485281371551)
XLA Ops:
  0.0 0.8 slice.41
  0.8 0.8 slice.40
  1.6 0.8 copy.25
  2.3 0.1 eq.35
  2.4 0.2 convert_reduce_fusion
  2.6 0.1 reduce_sum.31
  2.7 0.0 copy-done
  2.7 2.1 %fusion.9 = f32[8,32,256]{2,1,0:T(8,128)S(1)} fusion(bf16[8,32,576]{2,1,0:T(8,128)(2,1)S(1)} %copy-done, bf16[8,256,576]{1,2,0:T(8,128)(2,1)} %param.13, s32[8]{0:T(128)} %param.14), kind=kOutput, calls=%fused_computation.9 | convolution fusion | flops 75694080 | bytes 2916384 | tf_op jit(solution)/shard_map/thc,tsc->ths/dot_general | solution.py:23
  4.9 0.2 fusion.29
  5.1 2.3 %fusion.5 = bf16[8,32,512]{2,1,0:T(8,128)(2,1)S(1)} fusion(bf16[8,256,576]{1,2,0:T(8,128)(2,1)} %param.13, f32[8,32]{1,0:T(8,128)S(1)} %fusion.29, f32[8,32,256]{2,1,0:T(8,128)S(1)} %fusion.9), kind=kOutput, calls=%fused_computation.6 | convolution fusion | flops 67437056 | bytes 2887680 | tf_op jit(solution)/shard_map/ths,tsc->thc/dot_general | solution.py:31
  7.4 0.1 pad_add_fusion.place_ref
  7.5 2.9 %fusion.10.after_ref = bf16[8,4096]{1,0:T(8,128)(2,1)S(1)} fusion(bf16[32,512,128]{2,1,0:T(8,128)(2,1)} %param.15, bf16[8,32,512]{2,1,0:T(8,128)(2,1)S(1)} %fusion.5), kind=kOutput, calls=%fused_computation.11 | convolution fusion | flops 33587200 | bytes 4521984 | tf_op jit(solution)/shard_map/thc,hcv->thv/dot_general | solution.py:34
  10.5 6.1 %collective-permute-start.6 = (bf16[8,4608]{1,0:T(8,128)(2,1)S(1)}, bf16[8,4608]{1,0:T(8,128)(2,1)S(1)}, u32[]{:S(2)}, u32[]{:S(2)}) collective-permute-start(bf16[8,4608]{1,0:T(8,128)(2,1)S(1)} %get-tuple-element.35), channel_id=1, source_target_pairs={{0,14},{2,12},{4,10},{6,8},{8,6},{10,4},{12,2},{14,0},{1,15},{3,13... | collective-permute-start | bytes 221192 | tf_op jit(solution)/shard_map/ppermute | solution.py:283
  16.6 0.5 collective-permute-start
  17.1 0.0 collective-permute-start.1
  17.1 3.0 %collective-permute-start.2 = (bf16[8,4608]{1,0:T(8,128)(2,1)S(1)}, bf16[8,4608]{1,0:T(8,128)(2,1)S(1)}, u32[]{:S(2)}, u32[]{:S(2)}) collective-permute-start(bf16[8,4608]{1,0:T(8,128)(2,1)S(1)} %get-tuple-element.38), channel_id=1, source_target_pairs={{0,6},{2,4},{4,2},{6,0},{8,14},{10,12},{12,10},{14,8},{1,7},{3,5},... | collective-permute-start | bytes 221192 | tf_op jit(solution)/shard_map/ppermute | solution.py:283
  20.1 0.0 collective-permute-start.3
  20.1 0.0 collective-permute-done.6.refs_7_
  20.1 2.9 %collective-permute-start.4 = (bf16[8,4608]{1,0:T(8,128)(2,1)S(1)}, bf16[8,4608]{1,0:T(8,128)(2,1)S(1)}, u32[]{:S(2)}, u32[]{:S(2)}) collective-permute-start(bf16[8,4608]{1,0:T(8,128)(2,1)S(1)} %get-tuple-element.40), channel_id=1, source_target_pairs={{0,10},{2,8},{4,14},{6,12},{8,2},{10,0},{12,6},{14,4},{1,11},{3,9}... | collective-permute-start | bytes 221192 | tf_op jit(solution)/shard_map/ppermute | solution.py:283
  23.0 0.0 collective-permute-done.refs_1_
  23.0 0.4 collective-permute-start.5
  23.4 9.4 %load.1.both_ref = bf16[2,7168,1024]{2,1,0:T(8,128)(2,1)S(1)} custom-call(bf16[7168,1024]{1,0:T(8,128)(2,1)} %gate_hbm.1, bf16[7168,1024]{1,0:T(8,128)(2,1)} %up_hbm.1, bf16[8,4096]{1,0:T(8,128)(2,1)S(1)} %fusion.10.after_ref), custom_call_target="tpu_custom_call" | custom-call | bytes 29360128 | tf_op jit(solution)/shard_map/load/pallas_call | solution.py:64
  32.8 0.0 collective-permute-done.1.refs_2_
  32.8 0.0 collective-permute-done.2.refs_3_
  32.8 0.0 collective-permute-done.3.refs_4_
  32.8 0.0 collective-permute-done.4.refs_5_
  32.8 0.0 collective-permute-done.5.refs_6_
  32.8 0.0 copy-start.2
  32.8 3.7 %project.1.mine_ref = f32[64,896]{1,0:T(8,128)S(1)} custom-call(bf16[8,4608]{1,0:T(8,128)(2,1)S(1)} %get-tuple-element.20.refs_0_, bf16[8,4608]{1,0:T(8,128)(2,1)S(1)} %collective-permute-done.refs_1_, bf16[8,4608]{1,0:T(8,128)(2,1)S(1)} %collective-permute-done.1.refs_2_, bf16[8,4608]{1,0:T(8,128)(2,1)S(1)} %collective-permute-done.2.refs_3_, ...), custom_call_target="tpu_custom_call" | custom-call | flops 469762048 | bytes 7340032 | tf_op jit(solution)/shard_map/project/pallas_call | solution.py:106
  36.5 0.1 collective-permute-start.7
  36.6 1.5 %collective-permute-done.7.other_ref = f32[64,896]{1,0:T(8,128)S(1)} collective-permute-done((f32[64,896]{1,0:T(8,128)S(1)}, f32[64,896]{1,0:T(8,128)S(1)}, u32[]{:S(2)}, u32[]{:S(2)}) %collective-permute-start.7) | collective-permute-done | bytes 229408 | tf_op jit(solution)/shard_map/ppermute | solution.py:288
  38.1 0.9 %dispatch.1 = bf16[8,16,1152]{2,1,0:T(8,128)(2,1)S(1)} custom-call(s32[2]{0:T(128)S(1)} %pad_add_fusion.place_ref, f32[64,896]{1,0:T(8,128)S(1)} %project.1.mine_ref, f32[64,896]{1,0:T(8,128)S(1)} %collective-permute-done.7.other_ref, bf16[8,4608]{1,0:T(8,128)(2,1)S(1)} %get-tuple-element.20.refs_0_, bf16[8,4608]{1,0:T(8,128)(2,1)S(1)} %collective-permute-done.refs_1_, ...), custom_call_target="tpu_custom_call" | custom-call | tf_op jit(solution)/shard_map/dispatch/pallas_call | solution.py:175
  38.9 16.1 %all_to_all.10 = bf16[8,16,1152]{2,1,0:T(8,128)(2,1)S(1)} all-to-all(bf16[8,16,1152]{2,1,0:T(8,128)(2,1)S(1)} %dispatch.1), channel_id=1, replica_groups=mesh['groups'=2,'role'=8,'head'=2] {'role'}, dimensions={0} | all-to-all | bytes 589824 | tf_op jit(solution)/shard_map/all_to_all | solution.py:290
  55.0 0.2 fusion.11
  55.3 0.0 copy-done.2
  55.3 0.1 multiply_convert_fusion.mine_ref
  55.4 0.0 copy-start.3
  55.4 0.1 collective-permute-start.8
  55.5 1.5 %collective-permute-done.8.other_ref = bf16[16,7168]{1,0:T(8,128)(2,1)S(1)} collective-permute-done((bf16[16,7168]{1,0:T(8,128)(2,1)S(1)}, bf16[16,7168]{1,0:T(8,128)(2,1)S(1)}, u32[]{:S(2)}, u32[]{:S(2)}) %collective-permute-start.8) | collective-permute-done | bytes 229408 | tf_op jit(solution)/shard_map/ppermute | solution.py:301
  57.0 8.7 %experts.1 = (f32[16,7168]{1,0:T(8,128)S(1)}, f32[16,7168]{1,0:T(8,128)S(1)}) custom-call(bf16[16,7168]{1,0:T(8,128)(2,1)S(1)} %multiply_convert_fusion.mine_ref, bf16[16,7168]{1,0:T(8,128)(2,1)S(1)} %collective-permute-done.8.other_ref, bf16[2,7168,1024]{2,1,0:T(8,128)(2,1)S(1)} %load.1.both_ref, bf16[1024,7168]{1,0:T(8,128)(2,1)} %down_hbm.1), custom_call_target="tpu_custom_call" | custom-call | flops 1409286144 | bytes 14680064 | tf_op jit(solution)/shard_map/experts/pallas_call | solution.py:224
  65.6 0.2 collective-permute-start.9
  65.9 0.2 slice_reduce_fusion.1
  66.0 1.5 %collective-permute-done.9 = f32[16,7168]{1,0:T(8,128)S(1)} collective-permute-done((f32[16,7168]{1,0:T(8,128)S(1)}, f32[16,7168]{1,0:T(8,128)S(1)}, u32[]{:S(2)}, u32[]{:S(2)}) %collective-permute-start.9) | collective-permute-done | bytes 458784 | tf_op jit(solution)/shard_map/ppermute | solution.py:303
  67.6 0.8 reshape.46
  68.3 3.4 %all-to-all-start.1 = ((bf16[8,2,7168]{2,1,0:T(2,128)(2,1)}), bf16[8,2,7168]{2,1,0:T(2,128)(2,1)S(1)}, u32[]{:S(2)}, u32[]{:S(2)}) async-start(bf16[8,2,7168]{2,1,0:T(2,128)(2,1)} %reshape.46), calls=%async_computation.1 | async-start | bytes 458752 | tf_op jit(solution)/shard_map/all_to_all | solution.py:304
  72.0 8.8 %all-to-all-done.1 = bf16[8,2,7168]{2,1,0:T(2,128)(2,1)S(1)} async-done(((bf16[8,2,7168]{2,1,0:T(2,128)(2,1)}), bf16[8,2,7168]{2,1,0:T(2,128)(2,1)S(1)}, u32[]{:S(2)}, u32[]{:S(2)}) %all-to-all-start.1) | async-done | bytes 229408 | tf_op jit(solution)/shard_map/all_to_all | solution.py:304
  80.7 0.1 reshape.47
  80.8 0.9 %fusion.1 = bf16[4,7168]{1,0:T(4,128)(2,1)} fusion(f32[4,7168]{1,0:T(4,128)S(1)} %bitcast.47, bf16[16,7168]{1,0:T(8,128)(2,1)S(1)} %reshape.47, f32[4]{0:T(128)S(1)} %get-tuple-element.52, s32[4]{0:T(128)S(1)} %get-tuple-element.32, f32[4]{0:T(128)S(1)} %get-tuple-element.51, s32[4]{0:T(128)S(1)} %get-tuple-element.31), kind=kOutput, calls=%fused_computation.2 | convolution fusion | flops 5562688 | bytes 401472 | tf_op jit(solution)/shard_map/dot_general | solution.py:312
  (20 shorter events, 0.4 us)
Async XLA Ops:
  0.0 2.7 %copy-start = (bf16[8,32,576]{2,1,0:T(8,128)(2,1)S(1)}, bf16[8,32,576]{2,1,0:T(8,128)(2,1)}, u32[]{:S(2)}) copy-start(bf16[8,32,576]{2,1,0:T(8,128)(2,1)} %param.12) | copy-start | bytes 884740
  10.5 9.6 %collective-permute-start.6 = (bf16[8,4608]{1,0:T(8,128)(2,1)S(1)}, bf16[8,4608]{1,0:T(8,128)(2,1)S(1)}, u32[]{:S(2)}, u32[]{:S(2)}) collective-permute-start(bf16[8,4608]{1,0:T(8,128)(2,1)S(1)} %get-tuple-element.35), channel_id=1, source_target_pairs={{0,14},{2,12},{4,10},{6,8},{8,6},{10,4},{12,2},{14,0},{1,15},{3,13... | collective-permute-start | bytes 221192 | tf_op jit(solution)/shard_map/ppermute | solution.py:283
  16.6 6.4 %collective-permute-start = (bf16[8,4608]{1,0:T(8,128)(2,1)S(1)}, bf16[8,4608]{1,0:T(8,128)(2,1)S(1)}, u32[]{:S(2)}, u32[]{:S(2)}) collective-permute-start(bf16[8,4608]{1,0:T(8,128)(2,1)S(1)} %get-tuple-element.36), channel_id=1, source_target_pairs={{0,2},{2,0},{4,6},{6,4},{8,10},{10,8},{12,14},{14,12},{1,3},{3,1},... | collective-permute-start | bytes 221192 | tf_op jit(solution)/shard_map/ppermute | solution.py:283
  17.1 15.7 %collective-permute-start.1 = (bf16[8,4608]{1,0:T(8,128)(2,1)S(1)}, bf16[8,4608]{1,0:T(8,128)(2,1)S(1)}, u32[]{:S(2)}, u32[]{:S(2)}) collective-permute-start(bf16[8,4608]{1,0:T(8,128)(2,1)S(1)} %get-tuple-element.37), channel_id=1, source_target_pairs={{0,4},{2,6},{4,0},{6,2},{8,12},{10,14},{12,8},{14,10},{1,5},{3,7},... | collective-permute-start | bytes 221192 | tf_op jit(solution)/shard_map/ppermute | solution.py:283
  17.1 15.7 %collective-permute-start.2 = (bf16[8,4608]{1,0:T(8,128)(2,1)S(1)}, bf16[8,4608]{1,0:T(8,128)(2,1)S(1)}, u32[]{:S(2)}, u32[]{:S(2)}) collective-permute-start(bf16[8,4608]{1,0:T(8,128)(2,1)S(1)} %get-tuple-element.38), channel_id=1, source_target_pairs={{0,6},{2,4},{4,2},{6,0},{8,14},{10,12},{12,10},{14,8},{1,7},{3,5},... | collective-permute-start | bytes 221192 | tf_op jit(solution)/shard_map/ppermute | solution.py:283
  20.1 12.7 %collective-permute-start.3 = (bf16[8,4608]{1,0:T(8,128)(2,1)S(1)}, bf16[8,4608]{1,0:T(8,128)(2,1)S(1)}, u32[]{:S(2)}, u32[]{:S(2)}) collective-permute-start(bf16[8,4608]{1,0:T(8,128)(2,1)S(1)} %get-tuple-element.39), channel_id=1, source_target_pairs={{0,8},{2,10},{4,12},{6,14},{8,0},{10,2},{12,4},{14,6},{1,9},{3,11}... | collective-permute-start | bytes 221192 | tf_op jit(solution)/shard_map/ppermute | solution.py:283
  20.1 12.7 %collective-permute-start.4 = (bf16[8,4608]{1,0:T(8,128)(2,1)S(1)}, bf16[8,4608]{1,0:T(8,128)(2,1)S(1)}, u32[]{:S(2)}, u32[]{:S(2)}) collective-permute-start(bf16[8,4608]{1,0:T(8,128)(2,1)S(1)} %get-tuple-element.40), channel_id=1, source_target_pairs={{0,10},{2,8},{4,14},{6,12},{8,2},{10,0},{12,6},{14,4},{1,11},{3,9}... | collective-permute-start | bytes 221192 | tf_op jit(solution)/shard_map/ppermute | solution.py:283
  23.0 9.8 %collective-permute-start.5 = (bf16[8,4608]{1,0:T(8,128)(2,1)S(1)}, bf16[8,4608]{1,0:T(8,128)(2,1)S(1)}, u32[]{:S(2)}, u32[]{:S(2)}) collective-permute-start(bf16[8,4608]{1,0:T(8,128)(2,1)S(1)} %get-tuple-element.41), channel_id=1, source_target_pairs={{0,12},{2,14},{4,8},{6,10},{8,4},{10,6},{12,0},{14,2},{1,13},{3,15... | collective-permute-start | bytes 221192 | tf_op jit(solution)/shard_map/ppermute | solution.py:283
  32.8 22.5 %copy-start.2 = (f32[7168]{0:T(1024)S(1)}, f32[7168]{0:T(1024)}, u32[]{:S(2)}) copy-start(f32[7168]{0:T(1024)} %param.18) | copy-start | bytes 86020
  36.5 1.6 %collective-permute-start.7 = (f32[64,896]{1,0:T(8,128)S(1)}, f32[64,896]{1,0:T(8,128)S(1)}, u32[]{:S(2)}, u32[]{:S(2)}) collective-permute-start(f32[64,896]{1,0:T(8,128)S(1)} %project.1.mine_ref), channel_id=1, source_target_pairs={{0,1},{1,0},{2,3},{3,2},{4,5},{5,4},{6,7},{7,6},{8,9},{9,8},{10,11... | collective-permute-start | bytes 688136 | tf_op jit(solution)/shard_map/ppermute | solution.py:288
  55.4 16.4 %copy-start.3 = (f32[4,2]{0,1:T(2,128)S(1)}, f32[4,2]{0,1:T(2,128)}, u32[]{:S(2)}) copy-start(f32[4,2]{0,1:T(2,128)} %param.20) | copy-start | bytes 100
  55.4 1.6 %collective-permute-start.8 = (bf16[16,7168]{1,0:T(8,128)(2,1)S(1)}, bf16[16,7168]{1,0:T(8,128)(2,1)S(1)}, u32[]{:S(2)}, u32[]{:S(2)}) collective-permute-start(bf16[16,7168]{1,0:T(8,128)(2,1)S(1)} %multiply_convert_fusion.mine_ref), channel_id=1, source_target_pairs={{0,1},{1,0},{2,3},{3,2},{4,5},{5,4},{6,7},{7,6},{8,9},{9,8},{10,11... | collective-permute-start | bytes 688136 | tf_op jit(solution)/shard_map/ppermute | solution.py:301
  57.0 24.8 %copy-start.1 = (bf16[8,32,576]{2,1,0:T(8,128)(2,1)S(1)}, bf16[8,32,576]{2,1,0:T(8,128)(2,1)}, u32[]{:S(2)}) copy-start(bf16[8,32,576]{2,1,0:T(8,128)(2,1)} %param.12) | copy-start | bytes 884740
  65.6 1.9 %collective-permute-start.9 = (f32[16,7168]{1,0:T(8,128)S(1)}, f32[16,7168]{1,0:T(8,128)S(1)}, u32[]{:S(2)}, u32[]{:S(2)}) collective-permute-start(f32[16,7168]{1,0:T(8,128)S(1)} %get-tuple-element.30), channel_id=1, source_target_pairs={{0,1},{1,0},{2,3},{3,2},{4,5},{5,4},{6,7},{7,6},{8,9},{9,8},{10,11... | collective-permute-start | bytes 1376264 | tf_op jit(solution)/shard_map/ppermute | solution.py:303
  68.3 12.4 %all-to-all-start.1 = ((bf16[8,2,7168]{2,1,0:T(2,128)(2,1)}), bf16[8,2,7168]{2,1,0:T(2,128)(2,1)S(1)}, u32[]{:S(2)}, u32[]{:S(2)}) async-start(bf16[8,2,7168]{2,1,0:T(2,128)(2,1)} %reshape.46), calls=%async_computation.1 | async-start | bytes 458752 | tf_op jit(solution)/shard_map/all_to_all | solution.py:304

commit v3 on v2

--- a/solution.py
+++ b/solution.py
@@ -17,35 +17,172 @@
 VMEM = pltpu.VMEM
 
 
-def attend(queries, kv_cache, cache_lengths, uv_weight):
-    scale_factor = (VDIM + ROPE) ** (-0.5)
-    scores = (
-        jnp.einsum("thc,tsc->ths", queries, kv_cache, preferred_element_type=jnp.float32)
-        * scale_factor
-    )
-    position = lax.broadcasted_iota(jnp.int32, scores.shape, 2)
-    scores = jnp.where(position < cache_lengths[:, None, None], scores, -jnp.inf)
-    top_score = jnp.max(scores, axis=2, keepdims=True)
-    weights = jnp.exp(scores - top_score)
-    attn_probs = (weights / jnp.sum(weights, axis=2, keepdims=True)).astype(jnp.bfloat16)
-    latent_out = jnp.einsum(
-        "ths,tsc->thc", attn_probs, kv_cache[:, :, :LATENT], preferred_element_type=jnp.float32
-    ).astype(jnp.bfloat16)
-    head_out = jnp.einsum(
-        "thc,hcv->thv", latent_out, uv_weight, preferred_element_type=jnp.float32
-    ).astype(jnp.bfloat16)
-    return head_out.reshape(head_out.shape[0], -1)
-
-
-def slot_positions(expert_ids):
-    flat_ids = expert_ids.reshape(-1)
-    n = flat_ids.shape[0]
-    earlier = lax.broadcasted_iota(jnp.int32, (n, n), 1) < lax.broadcasted_iota(
-        jnp.int32, (n, n), 0
-    )
-    same = flat_ids[:, None] == flat_ids[None, :]
-    rank = jnp.sum((earlier & same).astype(jnp.int32), axis=1)
-    return (flat_ids * CAP + rank).reshape(expert_ids.shape)
+def slot_of(ids_ref, token, choice):
+    mine = ids_ref[choice, token]
+    rank = jnp.int32(0)
+    choices = ids_ref.shape[0]
+    for earlier in range(token * choices + choice):
+        rank += (ids_ref[earlier % choices, earlier // choices] == mine).astype(jnp.int32)
+    return mine * CAP + rank
+
+
+def attend_kernel(
+    resid_ref, length_hbm, ids_hbm, query_hbm, cache_hbm, value_hbm, weight_hbm, weight_ref, *refs
+):
+    outs, refs = refs[:-11], refs[-11:]
+    query_ref, cache_ref, value_ref, latent_ref, head_ref, side_ref, length_ref, ids_ref = refs[:8]
+    cache_sems, value_sems, other_sems = refs[8:]
+    requests, heads, _ = query_ref.shape
+    groups = value_ref.shape[0]
+    per = value_ref.shape[1]
+    share, width = resid_ref.shape
+    cols = width // len(outs)
+    wide = heads * VDIM
+    left = outs[0].shape[1] - wide
+    role = lax.axis_index("role")
+    scalars = [
+        pltpu.make_async_copy(ids_hbm, ids_ref, other_sems.at[0]),
+        pltpu.make_async_copy(length_hbm, length_ref, other_sems.at[1]),
+    ]
+    last = pltpu.make_async_copy(weight_hbm, weight_ref, other_sems.at[2])
+    copies = [pltpu.make_async_copy(query_hbm, query_ref, other_sems.at[3])]
+    for t in range(requests):
+        copies.append(pltpu.make_async_copy(cache_hbm.at[t], cache_ref.at[t], cache_sems.at[t]))
+    for g in range(groups):
+        copies.append(
+            pltpu.make_async_copy(
+                value_hbm.at[pl.ds(g * per, per)], value_ref.at[g], value_sems.at[g]
+            )
+        )
+    for copy in (*scalars, *copies, last):
+        copy.start()
+    for copy in scalars:
+        copy.wait()
+
+    side_ref[0:share, :width] = resid_ref[...].astype(F32)
+    side_ref[share:, :width] = resid_ref[...].astype(F32)
+    side_ref[:, width:] = jnp.zeros((2 * share, 128), F32)
+    row = lax.broadcasted_iota(jnp.int32, (2 * share, 128), 0)
+    lane = lax.broadcasted_iota(jnp.int32, (2 * share, 128), 1)
+    notes = jnp.zeros((2 * share, 128), F32)
+    for t in range(share):
+        for k in range(2):
+            slot = slot_of(ids_ref, t, k).astype(F32)
+            notes = jnp.where((row == share + t) & (lane == k), slot, notes)
+    upper = lax.broadcasted_iota(jnp.int32, (2 * share, left), 0) < share
+    for step, out in enumerate(outs):
+        start = pl.multiple_of((role ^ step) * cols, 128)
+        first = side_ref[:, pl.ds(start, left)]
+        second = side_ref[:, pl.ds(start + left, cols - left)]
+        second = jnp.concatenate([second, notes], axis=1)
+        out[:, wide:] = jnp.where(upper, first, second).astype(BF16)
+
+    scale = (VDIM + ROPE) ** (-0.5)
+    for copy in copies[: 1 + requests]:
+        copy.wait()
+    scores = [
+        jnp.dot(query_ref[t], cache_ref[t], preferred_element_type=F32) for t in range(requests)
+    ]
+    position = lax.broadcasted_iota(jnp.int32, scores[0].shape, 1)
+    scores = [
+        jnp.where(position < length_ref[t], scores[t] * scale, -jnp.inf) for t in range(requests)
+    ]
+    tops = [jnp.max(v, axis=1, keepdims=True) for v in scores]
+    weights = [jnp.exp(v - top) for v, top in zip(scores, tops)]
+    sums = [jnp.sum(v, axis=1, keepdims=True) for v in weights]
+    probs = [(v / total).astype(BF16) for v, total in zip(weights, sums)]
+    for t in range(requests):
+        latent = lax.dot_general(
+            probs[t], cache_ref[t, :LATENT], (((1,), (1,)), ((), ())), preferred_element_type=F32
+        )
+        latent = latent.astype(BF16).astype(F32)
+        for c in range(LATENT // 128):
+            latent_ref[c, t * heads : (t + 1) * heads, :] = latent[:, c * 128 : (c + 1) * 128]
+    for copy in copies[1 + requests :]:
+        copy.wait()
+    for g in range(groups):
+        for i in range(per):
+            h = g * per + i
+            latent = jnp.concatenate(
+                [
+                    latent_ref[c, pl.ds(h, requests, stride=heads), :]
+                    for c in range(LATENT // 128)
+                ],
+                axis=1,
+            ).astype(BF16)
+            head = jnp.dot(latent, value_ref[g, i], preferred_element_type=F32)
+            head_ref[:, h * VDIM : (h + 1) * VDIM] = head.astype(BF16)
+    for out in outs:
+        out[:, :wide] = head_ref[...]
+    last.wait()
+
+
+def attend(lengths, ids, residual, queries, cache, values, weight, roles):
+    requests, heads, width = queries.shape
+    groups = 4
+    hbm = [
+        pltpu.with_memory_space_constraint(w, pltpu.HBM)
+        for w in (lengths, ids, queries, cache, values, weight)
+    ]
+    whole = pl.BlockSpec(memory_space=VMEM)
+    return pl.pallas_call(
+        attend_kernel,
+        out_shape=(VMEM(weight.shape, weight.dtype),)
+        + (jax.ShapeDtypeStruct((requests, heads * VDIM + 512), BF16),) * roles,
+        in_specs=[whole] + [pl.BlockSpec(memory_space=pltpu.HBM)] * 6,
+        out_specs=(whole,) * (1 + roles),
+        scratch_shapes=[
+            VMEM(queries.shape, BF16),
+            VMEM(cache.shape, BF16),
+            VMEM((groups, heads // groups) + values.shape[1:], BF16),
+            VMEM((LATENT // 128, requests * heads, 128), F32),
+            VMEM((requests, heads * VDIM), BF16),
+            VMEM((2 * residual.shape[0], residual.shape[1] + 128), F32),
+            pltpu.SMEM(lengths.shape, jnp.int32),
+            pltpu.SMEM(ids.shape, jnp.int32),
+            pltpu.SemaphoreType.DMA((requests,)),
+            pltpu.SemaphoreType.DMA((groups,)),
+            pltpu.SemaphoreType.DMA((4,)),
+        ],
+        compiler_params=pltpu.CompilerParams(vmem_limit_bytes=24 << 20),
+        name="attend",
+    )(residual, *hbm)
+
+
+def combine_kernel(ids_ref, route_ref, received_ref, returned_ref, out_ref, sum_ref):
+    roles, slots, _ = received_ref.shape
+    share, width = out_ref.shape
+    cols = width // roles
+    for r in range(roles):
+        kept = received_ref[r, :, cols:].astype(F32)
+        for g in range(4):
+            reach = min(256, cols - g * 256)
+            start = r * cols + g * 256
+            sum_ref[:, start : start + reach] = kept[g * share : (g + 1) * share, :reach]
+    for t in range(share):
+        extra = []
+        for k in range(2):
+            slot = slot_of(ids_ref, t, k)
+            both = returned_ref[ids_ref[k, t]].astype(F32)
+            one = jnp.where(slot % CAP == 0, both[0:1], both[1:2])
+            extra.append(route_ref[k, t] * one)
+        sum_ref[t : t + 1, :] += extra[0] + extra[1]
+    out_ref[...] = sum_ref[...].astype(BF16)
+
+
+def combine(ids, route, received, returned, share):
+    width = returned.shape[2]
+    whole = pl.BlockSpec(memory_space=VMEM)
+    scalars = pl.BlockSpec(memory_space=pltpu.SMEM)
+    return pl.pallas_call(
+        combine_kernel,
+        out_shape=jax.ShapeDtypeStruct((share, width), BF16),
+        in_specs=[scalars] * 2 + [whole] * 2,
+        out_specs=whole,
+        scratch_shapes=[VMEM((share, width), F32)],
+        compiler_params=pltpu.CompilerParams(vmem_limit_bytes=6 << 20),
+        name="combine",
+    )(ids, route, received, returned)
 
 
 def load_kernel(gate_hbm, up_hbm, after_ref, both_ref, sems):
@@ -75,54 +212,30 @@
     )(gate, up, after)
 
 
-def project_kernel(*refs):
-    messages, (weight_hbm, out_ref, weight_ref, sems) = refs[:-4], refs[-4:]
-    chunks, deep, _ = weight_ref.shape
-
-    def fetch(i):
-        return pltpu.make_async_copy(
-            weight_hbm.at[pl.ds(i * deep, deep), :], weight_ref.at[i], sems.at[i]
-        )
-
-    for i in range(chunks):
-        fetch(i).start()
-    for i in range(chunks):
-        rows = jnp.concatenate(
-            [m[:, i * deep : (i + 1) * deep].astype(F32) for m in messages], axis=0
-        ).astype(BF16)
-        fetch(i).wait()
-        part = jnp.dot(rows, weight_ref[i], preferred_element_type=F32)
-        if i:
-            out_ref[...] += part
-        else:
-            out_ref[...] = part
+def project_kernel(weight_ref, *refs):
+    messages, out_ref = refs[:-1], refs[-1]
+    depth = weight_ref.shape[0]
+    rows = jnp.concatenate([m[:, :depth].astype(F32) for m in messages], axis=0).astype(BF16)
+    out_ref[...] = jnp.dot(rows, weight_ref[...], preferred_element_type=F32)
 
 
 def project(messages, weight):
-    depth, cols = weight.shape
+    cols = weight.shape[1]
     tokens = sum(m.shape[0] for m in messages)
-    chunks = 4
     whole = pl.BlockSpec(memory_space=VMEM)
     return pl.pallas_call(
         project_kernel,
         out_shape=jax.ShapeDtypeStruct((tokens, cols), F32),
-        in_specs=[whole] * len(messages) + [pl.BlockSpec(memory_space=pltpu.HBM)],
+        in_specs=[whole] * (1 + len(messages)),
         out_specs=whole,
-        scratch_shapes=[
-            VMEM((chunks, depth // chunks, cols), BF16),
-            pltpu.SemaphoreType.DMA((chunks,)),
-        ],
-        compiler_params=pltpu.CompilerParams(vmem_limit_bytes=12 << 20),
-        cost_estimate=pl.CostEstimate(
-            flops=2 * tokens * depth * cols, bytes_accessed=2 * depth * cols, transcendentals=0
-        ),
+        compiler_params=pltpu.CompilerParams(vmem_limit_bytes=6 << 20),
         name="project",
-    )(*messages, pltpu.with_memory_space_constraint(weight, pltpu.HBM))
-
-
-def dispatch_kernel(place_ref, mine_ref, other_ref, *refs):
+    )(pltpu.with_memory_space_constraint(weight, VMEM), *messages)
+
+
+def dispatch_kernel(mine_ref, other_ref, *refs):
     messages, out_ref = refs[:-1], refs[-1]
-    role, core = place_ref[0], place_ref[1]
+    role, core = lax.axis_index("role"), lax.axis_index("head")
     roles = len(messages)
     tokens, cols = mine_ref.shape
     each = tokens // roles
@@ -168,18 +281,18 @@
         out_ref[d, :, cols:] = extra[d * slots : (d + 1) * slots]
 
 
-def dispatch(place, mine, other, messages):
+def dispatch(mine, other, messages):
     roles = len(messages)
     cols = mine.shape[1]
     whole = pl.BlockSpec(memory_space=VMEM)
     return pl.pallas_call(
         dispatch_kernel,
         out_shape=jax.ShapeDtypeStruct((roles, roles * CAP, cols + 256), BF16),
-        in_specs=[pl.BlockSpec(memory_space=pltpu.SMEM)] + [whole] * (2 + roles),
+        in_specs=[whole] * (2 + roles),
         out_specs=whole,
         compiler_params=pltpu.CompilerParams(vmem_limit_bytes=6 << 20),
         name="dispatch",
-    )(place, mine, other, *messages)
+    )(mine, other, *messages)
 
 
 def expert_kernel(
@@ -258,64 +371,54 @@
     down_weight,
 ):
     roles = lax.axis_size("role")
-    role = lax.axis_index("role")
-    core = lax.axis_index("head")
     share = residual.shape[0]
     width = residual.shape[1]
     cols = width // roles
-    tokens = 2 * share
-    left = 4 * 128
-    head_out = attend(queries, kv_cache, cache_lengths, uv_weight)
-    place, head_out = lax.optimization_barrier((jnp.stack([role, core]), head_out))
-    positions = slot_positions(expert_ids)
-    by_role = residual.reshape(share, roles, cols).transpose(1, 0, 2)
-    note = jnp.pad(positions.astype(BF16), ((0, 0), (0, 126)))
-    note = jnp.broadcast_to(note[None], (roles, share, 128))
-    extra = jnp.concatenate(
-        [by_role[:, :, :left], jnp.concatenate([by_role[:, :, left:], note], axis=2)], axis=1
-    )
-    messages = []
-    for step in range(roles):
-        block = jnp.concatenate(
-            [head_out, lax.dynamic_index_in_dim(extra, role ^ step, 0, keepdims=False)], axis=1
-        )
-        if step:
-            block = lax.ppermute(block, "role", [(i, i ^ step) for i in range(roles)])
-        messages.append(block)
-    both_weights = load(gate_weight, up_weight, head_out)
+    ids = expert_ids.T
+    cache = kv_cache.transpose(0, 2, 1)
+    out_weight, *messages = attend(
+        cache_lengths, ids, residual, queries, cache, uv_weight, out_weight, roles
+    )
+    both_weights = load(gate_weight, up_weight, messages[0])
+    messages = [messages[0]] + [
+        lax.ppermute(messages[step], "role", [(i, i ^ step) for i in range(roles)])
+        for step in range(1, roles)
+    ]
     messages, both_weights = lax.optimization_barrier((messages, both_weights))
     partial_value = project(messages, out_weight)
     other_value = lax.ppermute(partial_value, "head", [(0, 1), (1, 0)])
-    outgoing = dispatch(place, partial_value, other_value, messages)
+    outgoing = dispatch(partial_value, other_value, messages)
     received = lax.all_to_all(outgoing, "role", split_axis=0, concat_axis=0, tiled=True)
     x = received[:, :, :cols].transpose(1, 0, 2).reshape(roles * CAP, width).astype(F32)
     inverse = lax.rsqrt(jnp.mean(x * x, axis=1, keepdims=True) + 1e-06)
     normed = (x * inverse * norm_gain[None, :]).astype(BF16)
-    hidden_own = (
-        received[:, :, cols:]
-        .reshape(roles, 4, share, 256)
-        .transpose(2, 0, 1, 3)
-        .reshape(share, roles, 1024)[:, :, :cols]
-        .reshape(share, width)
-    )
     other = lax.ppermute(normed, "head", [(0, 1), (1, 0)])
     keep, send = run_experts(normed, other, both_weights, down_weight)
     summed = (keep + lax.ppermute(send, "head", [(0, 1), (1, 0)])).astype(BF16)
     returned = lax.all_to_all(
         summed.reshape(roles, CAP, width), "role", split_axis=0, concat_axis=0, tiled=True
     )
-    slot_grid = lax.broadcasted_iota(jnp.int32, (share, EXPERTS * CAP), 1)
-    mixing = sum(
-        jnp.where(slot_grid == positions[:, k : k + 1], route_weights[:, k : k + 1], 0.0)
-        for k in range(2)
-    )
-    combined = jnp.dot(
-        mixing,
-        returned.reshape(EXPERTS * CAP, width).astype(F32),
-        precision=lax.Precision.HIGHEST,
-        preferred_element_type=F32,
-    )
-    return (hidden_own.astype(F32) + combined).astype(BF16)
+    return combine(ids, route_weights.T, received, returned, share)
+
+
+def attend_general(queries, kv_cache, cache_lengths, uv_weight):
+    scale_factor = (VDIM + ROPE) ** (-0.5)
+    scores = (
+        jnp.einsum("thc,tsc->ths", queries, kv_cache, preferred_element_type=jnp.float32)
+        * scale_factor
+    )
+    position = lax.broadcasted_iota(jnp.int32, scores.shape, 2)
+    scores = jnp.where(position < cache_lengths[:, None, None], scores, -jnp.inf)
+    top_score = jnp.max(scores, axis=2, keepdims=True)
+    weights = jnp.exp(scores - top_score)
+    attn_probs = (weights / jnp.sum(weights, axis=2, keepdims=True)).astype(jnp.bfloat16)
+    latent_out = jnp.einsum(
+        "ths,tsc->thc", attn_probs, kv_cache[:, :, :LATENT], preferred_element_type=jnp.float32
+    ).astype(jnp.bfloat16)
+    head_out = jnp.einsum(
+        "thc,hcv->thv", latent_out, uv_weight, preferred_element_type=jnp.float32
+    ).astype(jnp.bfloat16)
+    return head_out.reshape(head_out.shape[0], -1)
 
 
 def general(
@@ -336,7 +439,7 @@
     head_n = lax.axis_size("head")
     share_rows = residual.shape[0]
     model_width = residual.shape[1]
-    head_out = attend(queries, kv_cache, cache_lengths, uv_weight)
+    head_out = attend_general(queries, kv_cache, cache_lengths, uv_weight)
     partial_value = jnp.dot(
         lax.all_gather(head_out, "role", axis=0, tiled=True),
         out_weight,

time: 82.2 us -> 73.4 us (0.89)
  blocking collectives: 16.1 us -> 27.9 us
  waiting for transfers between devices: 13.2 us -> 4.65 us
  matrix products: 8.3 us -> 0 us
  starting transfers between devices: 16.6 us -> 12.8 us
  Pallas kernels: 22.6 us -> 26.3 us
  local copies, waits for them, and re-layouts: 3.73 us -> 0.95 us
    all_to_all x0 -> x1, blocking collectives: none -> 11.4 us  [fast(): lax.all_to_all(summed.reshape(roles, CAP, width), 'role', split_axis=0, c...]
    all_to_all x1 -> x0, waiting for transfers between devices: 8.76 us -> none  [fast(): lax.all_to_all(summed.reshape(roles, CAP, width), 'role', split_axis=0, c...]
    dot_general x4 -> x0, matrix products: 8.3 us -> none  [the longest x1 2.91 us: attend(): jnp.einsum('thc,hcv->thv', latent_out, uv_weight, preferred_element_type=...]
    pallas_call x0 -> x2, Pallas kernels: none -> 6.59 us  [the longest x1 5.3 us: attend(): pl.pallas_call(attend_kernel, out_shape=(VMEM(weight.shape, weight.dtype)...]
    all_to_all x1 -> x0, starting transfers between devices: 3.4 us -> none  [fast(): lax.all_to_all(summed.reshape(roles, CAP, width), 'role', split_axis=0, c...]
    pallas_call x1, Pallas kernels: 3.65 us -> 1.35 us  [project(): pl.pallas_call(project_kernel, out_shape=jax.ShapeDtypeStruct((tokens, co...]
    slice x4 -> x0, local copies, waits for them, and re-layouts: 1.74 us -> none  [the longest x1 0.79 us: fast(): by_role[:, :, left:]]
  transfers between devices with their start and end apart: 11 -> 10, of which waited for: 4 -> 3; matrix products, arithmetic and copies ran while one was open for 0% -> 0% of each run, Pallas kernels for 11% -> 13%
where the time goes in v3:
time: 73.4 us; the launch traced here: 73.2 us
  blocking collectives  27.9 us (38%)
  Pallas kernels  26.3 us (36%)
  starting transfers between devices  12.8 us (17%)
  waiting for transfers between devices  4.65 us (6%)
  local copies, waits for them, and re-layouts  0.95 us (1%)
    all_to_all x1, blocking collectives, fast(): lax.all_to_all(outgoing, 'role', split_axis=0, concat_axis=0, tiled=True)  16.4 us
    ppermute x7, starting transfers between devices, fast(): lax.ppermute(messages[step], 'role', [(i, i ^ step) for i in range(roles)])  12.5 us
    all_to_all x1, blocking collectives, fast(): lax.all_to_all(summed.reshape(roles, CAP, width), 'role', split_axis=0, c...  11.4 us
    pallas_call x1, Pallas kernels, load(): pl.pallas_call(load_kernel, out_shape=VMEM((2,) + gate.shape, gate.dtype)...  9.37 us
    pallas_call x1, Pallas kernels, run_experts(): pl.pallas_call(expert_kernel, out_shape=(jax.ShapeDtypeStruct((rows, widt...  8.66 us
    pallas_call x1, Pallas kernels, attend(): pl.pallas_call(attend_kernel, out_shape=(VMEM(weight.shape, weight.dtype)...  5.3 us
    ppermute x1, waiting for transfers between devices, fast(): summed = (keep + lax.ppermute(send, 'head', [(0, 1), (1, 0)])).astype(BF16)  1.68 us
    ppermute x1, waiting for transfers between devices, fast(): other_value = lax.ppermute(partial_value, 'head', [(0, 1), (1, 0)])  1.48 us
  transfers between devices with their start and end apart: 10, of which 3 were waited for; matrix products, arithmetic and copies ran while one was open for 0% of the time, Pallas kernels for 13%

profile of v3, /device:TPU:0, one launch (start us, length us, event | category | flops | bytes accessed | tf_op | source)
XLA Modules:
  0.0 73.2 jit_solution(13151540398383785082)
XLA Ops:
  0.0 0.0 copy-start
  0.0 0.8 %copy-done = bf16[4,7168]{1,0:T(4,128)(2,1)S(1)} copy-done((bf16[4,7168]{1,0:T(4,128)(2,1)S(1)}, bf16[4,7168]{1,0:T(4,128)(2,1)}, u32[]{:S(2)}) %copy-start) | copy-done | bytes 57368
  0.8 5.3 %attend.1 = (bf16[4096,896]{1,0:T(8,128)(2,1)S(1)}, bf16[8,4608]{1,0:T(8,128)(2,1)S(1)}, bf16[8,4608]{1,0:T(8,128)(2,1)S(1)}, bf16[8,4608]{1,0:T(8,128)(2,1)S(1)...) custom-call(bf16[4,7168]{1,0:T(4,128)(2,1)S(1)} %copy-done, ...), custom_call_target="tpu_custom_call" | custom-call | tf_op jit(solution)/shard_map/attend/pallas_call | solution.py:128
  6.1 3.0 %collective-permute-start = (bf16[8,4608]{1,0:T(8,128)(2,1)S(1)}, bf16[8,4608]{1,0:T(8,128)(2,1)S(1)}, u32[]{:S(2)}, u32[]{:S(2)}) collective-permute-start(bf16[8,4608]{1,0:T(8,128)(2,1)S(1)} %get-tuple-element.27), channel_id=1, source_target_pairs={{0,2},{2,0},{4,6},{6,4},{8,10},{10,8},{12,14},{14,12},{1,3},{3,1},... | collective-permute-start | bytes 221192 | tf_op jit(solution)/shard_map/ppermute | solution.py:384
  9.2 1.6 %collective-permute-start.1 = (bf16[8,4608]{1,0:T(8,128)(2,1)S(1)}, bf16[8,4608]{1,0:T(8,128)(2,1)S(1)}, u32[]{:S(2)}, u32[]{:S(2)}) collective-permute-start(bf16[8,4608]{1,0:T(8,128)(2,1)S(1)} %get-tuple-element.28), channel_id=1, source_target_pairs={{0,4},{2,6},{4,0},{6,2},{8,12},{10,14},{12,8},{14,10},{1,5},{3,7},... | collective-permute-start | bytes 221192 | tf_op jit(solution)/shard_map/ppermute | solution.py:384
  10.7 0.0 collective-permute-start.2
  10.7 3.0 %collective-permute-start.3 = (bf16[8,4608]{1,0:T(8,128)(2,1)S(1)}, bf16[8,4608]{1,0:T(8,128)(2,1)S(1)}, u32[]{:S(2)}, u32[]{:S(2)}) collective-permute-start(bf16[8,4608]{1,0:T(8,128)(2,1)S(1)} %get-tuple-element.30), channel_id=1, source_target_pairs={{0,8},{2,10},{4,12},{6,14},{8,0},{10,2},{12,4},{14,6},{1,9},{3,11}... | collective-permute-start | bytes 221192 | tf_op jit(solution)/shard_map/ppermute | solution.py:384
  13.7 1.3 %collective-permute-start.4 = (bf16[8,4608]{1,0:T(8,128)(2,1)S(1)}, bf16[8,4608]{1,0:T(8,128)(2,1)S(1)}, u32[]{:S(2)}, u32[]{:S(2)}) collective-permute-start(bf16[8,4608]{1,0:T(8,128)(2,1)S(1)} %get-tuple-element.31), channel_id=1, source_target_pairs={{0,10},{2,8},{4,14},{6,12},{8,2},{10,0},{12,6},{14,4},{1,11},{3,9}... | collective-permute-start | bytes 221192 | tf_op jit(solution)/shard_map/ppermute | solution.py:384
  15.0 0.0 collective-permute-done.refs_1_
  15.0 3.6 %collective-permute-start.5 = (bf16[8,4608]{1,0:T(8,128)(2,1)S(1)}, bf16[8,4608]{1,0:T(8,128)(2,1)S(1)}, u32[]{:S(2)}, u32[]{:S(2)}) collective-permute-start(bf16[8,4608]{1,0:T(8,128)(2,1)S(1)} %get-tuple-element.32), channel_id=1, source_target_pairs={{0,12},{2,14},{4,8},{6,10},{8,4},{10,6},{12,0},{14,2},{1,13},{3,15... | collective-permute-start | bytes 221192 | tf_op jit(solution)/shard_map/ppermute | solution.py:384
  18.6 0.0 collective-permute-done.1.refs_2_
  18.6 0.0 collective-permute-start.6
  18.6 0.0 copy-start.3
  18.6 9.4 %load.1.both_ref = bf16[2,7168,1024]{2,1,0:T(8,128)(2,1)S(1)} custom-call(bf16[7168,1024]{1,0:T(8,128)(2,1)} %gate_hbm.1, bf16[7168,1024]{1,0:T(8,128)(2,1)} %up_hbm.1, bf16[8,4608]{1,0:T(8,128)(2,1)S(1)} %get-tuple-element.34.after_ref.refs_0_), custom_call_target="tpu_custom_call" | custom-call | bytes 29360128 | tf_op jit(solution)/shard_map/load/pallas_call | solution.py:201
  28.0 0.0 collective-permute-done.2.refs_3_
  28.0 0.0 collective-permute-done.3.refs_4_
  28.0 0.0 collective-permute-done.4.refs_5_
  28.0 0.0 collective-permute-done.5.refs_6_
  28.1 0.0 collective-permute-done.6.refs_7_
  28.1 1.4 %project.1.mine_ref = f32[64,896]{1,0:T(8,128)S(1)} custom-call(bf16[4096,896]{1,0:T(8,128)(2,1)S(1)} %get-tuple-element.25.weight_ref, bf16[8,4608]{1,0:T(8,128)(2,1)S(1)} %get-tuple-element.34.after_ref.refs_0_, bf16[8,4608]{1,0:T(8,128)(2,1)S(1)} %collective-permute-done.refs_1_, bf16[8,4608]{1,0:T(8,128)(2,1)S(1)} %collective-permute-done.1.refs_2_, ...), custom_call_target="tpu_custom_call" | custom-call | tf_op jit(solution)/shard_map/project/pallas_call | solution.py:226
  29.4 0.1 collective-permute-start.7
  29.5 1.5 %collective-permute-done.7.other_ref = f32[64,896]{1,0:T(8,128)S(1)} collective-permute-done((f32[64,896]{1,0:T(8,128)S(1)}, f32[64,896]{1,0:T(8,128)S(1)}, u32[]{:S(2)}, u32[]{:S(2)}) %collective-permute-start.7) | collective-permute-done | bytes 229408 | tf_op jit(solution)/shard_map/ppermute | solution.py:389
  31.0 0.3 dispatch.1
  31.3 16.4 %all_to_all.10.received_ref = bf16[8,16,1152]{2,1,0:T(8,128)(2,1)S(1)} all-to-all(bf16[8,16,1152]{2,1,0:T(8,128)(2,1)S(1)} %dispatch.1), channel_id=1, replica_groups=mesh['groups'=2,'role'=8,'head'=2] {'role'}, dimensions={0} | all-to-all | bytes 589824 | tf_op jit(solution)/shard_map/all_to_all | solution.py:391
  47.7 0.2 fusion
  48.0 0.0 copy-done.3
  48.0 0.1 multiply_convert_fusion.mine_ref
  48.1 0.0 copy-start.1
  48.2 0.0 copy-start.2
  48.2 0.1 collective-permute-start.8
  48.2 1.5 %collective-permute-done.8.other_ref = bf16[16,7168]{1,0:T(8,128)(2,1)S(1)} collective-permute-done((bf16[16,7168]{1,0:T(8,128)(2,1)S(1)}, bf16[16,7168]{1,0:T(8,128)(2,1)S(1)}, u32[]{:S(2)}, u32[]{:S(2)}) %collective-permute-start.8) | collective-permute-done | bytes 229408 | tf_op jit(solution)/shard_map/ppermute | solution.py:395
  49.7 8.7 %experts.1 = (f32[16,7168]{1,0:T(8,128)S(1)}, f32[16,7168]{1,0:T(8,128)S(1)}) custom-call(bf16[16,7168]{1,0:T(8,128)(2,1)S(1)} %multiply_convert_fusion.mine_ref, bf16[16,7168]{1,0:T(8,128)(2,1)S(1)} %collective-permute-done.8.other_ref, bf16[2,7168,1024]{2,1,0:T(8,128)(2,1)S(1)} %load.1.both_ref, bf16[1024,7168]{1,0:T(8,128)(2,1)} %down_hbm.1), custom_call_target="tpu_custom_call" | custom-call | flops 1409286144 | bytes 14680064 | tf_op jit(solution)/shard_map/experts/pallas_call | solution.py:337
  58.4 0.2 collective-permute-start.9
  58.6 1.7 %collective-permute-done.9 = f32[16,7168]{1,0:T(8,128)S(1)} collective-permute-done((f32[16,7168]{1,0:T(8,128)S(1)}, f32[16,7168]{1,0:T(8,128)S(1)}, u32[]{:S(2)}, u32[]{:S(2)}) %collective-permute-start.9) | collective-permute-done | bytes 458784 | tf_op jit(solution)/shard_map/ppermute | solution.py:397
  60.3 0.1 reshape.15
  60.4 11.4 %all_to_all.11.returned_ref = bf16[8,2,7168]{2,1,0:T(2,128)(2,1)S(1)} all-to-all(bf16[8,2,7168]{2,1,0:T(2,128)(2,1)S(1)} %reshape.15), channel_id=1, replica_groups=mesh['groups'=2,'role'=8,'head'=2] {'role'}, dimensions={0} | all-to-all | bytes 458752 | tf_op jit(solution)/shard_map/all_to_all | solution.py:398
  71.9 0.0 copy-done.1
  71.9 0.0 copy-done.2
  71.9 1.3 %combine.1 = bf16[4,7168]{1,0:T(4,128)(2,1)} custom-call(s32[2,4]{1,0:T(2,128)S(1)} %bitcast.8, f32[2,4]{1,0:T(2,128)S(1)} %bitcast.9, bf16[8,16,1152]{2,1,0:T(8,128)(2,1)S(1)} %all_to_all.10.received_ref, bf16[8,2,7168]{2,1,0:T(2,128)(2,1)S(1)} %all_to_all.11.returned_ref), custom_call_target="tpu_custom_call" | custom-call | tf_op jit(solution)/shard_map/combine/pallas_call | solution.py:177
  (4 shorter events, 0.1 us)
Async XLA Ops:
  0.0 0.8 %copy-start = (bf16[4,7168]{1,0:T(4,128)(2,1)S(1)}, bf16[4,7168]{1,0:T(4,128)(2,1)}, u32[]{:S(2)}) copy-start(bf16[4,7168]{1,0:T(4,128)(2,1)} %resid_ref.1) | copy-start | bytes 172036
  6.1 8.9 %collective-permute-start = (bf16[8,4608]{1,0:T(8,128)(2,1)S(1)}, bf16[8,4608]{1,0:T(8,128)(2,1)S(1)}, u32[]{:S(2)}, u32[]{:S(2)}) collective-permute-start(bf16[8,4608]{1,0:T(8,128)(2,1)S(1)} %get-tuple-element.27), channel_id=1, source_target_pairs={{0,2},{2,0},{4,6},{6,4},{8,10},{10,8},{12,14},{14,12},{1,3},{3,1},... | collective-permute-start | bytes 221192 | tf_op jit(solution)/shard_map/ppermute | solution.py:384
  9.2 9.5 %collective-permute-start.1 = (bf16[8,4608]{1,0:T(8,128)(2,1)S(1)}, bf16[8,4608]{1,0:T(8,128)(2,1)S(1)}, u32[]{:S(2)}, u32[]{:S(2)}) collective-permute-start(bf16[8,4608]{1,0:T(8,128)(2,1)S(1)} %get-tuple-element.28), channel_id=1, source_target_pairs={{0,4},{2,6},{4,0},{6,2},{8,12},{10,14},{12,8},{14,10},{1,5},{3,7},... | collective-permute-start | bytes 221192 | tf_op jit(solution)/shard_map/ppermute | solution.py:384
  10.7 17.3 %collective-permute-start.2 = (bf16[8,4608]{1,0:T(8,128)(2,1)S(1)}, bf16[8,4608]{1,0:T(8,128)(2,1)S(1)}, u32[]{:S(2)}, u32[]{:S(2)}) collective-permute-start(bf16[8,4608]{1,0:T(8,128)(2,1)S(1)} %get-tuple-element.29), channel_id=1, source_target_pairs={{0,6},{2,4},{4,2},{6,0},{8,14},{10,12},{12,10},{14,8},{1,7},{3,5},... | collective-permute-start | bytes 221192 | tf_op jit(solution)/shard_map/ppermute | solution.py:384
  10.7 17.3 %collective-permute-start.3 = (bf16[8,4608]{1,0:T(8,128)(2,1)S(1)}, bf16[8,4608]{1,0:T(8,128)(2,1)S(1)}, u32[]{:S(2)}, u32[]{:S(2)}) collective-permute-start(bf16[8,4608]{1,0:T(8,128)(2,1)S(1)} %get-tuple-element.30), channel_id=1, source_target_pairs={{0,8},{2,10},{4,12},{6,14},{8,0},{10,2},{12,4},{14,6},{1,9},{3,11}... | collective-permute-start | bytes 221192 | tf_op jit(solution)/shard_map/ppermute | solution.py:384
  13.7 14.3 %collective-permute-start.4 = (bf16[8,4608]{1,0:T(8,128)(2,1)S(1)}, bf16[8,4608]{1,0:T(8,128)(2,1)S(1)}, u32[]{:S(2)}, u32[]{:S(2)}) collective-permute-start(bf16[8,4608]{1,0:T(8,128)(2,1)S(1)} %get-tuple-element.31), channel_id=1, source_target_pairs={{0,10},{2,8},{4,14},{6,12},{8,2},{10,0},{12,6},{14,4},{1,11},{3,9}... | collective-permute-start | bytes 221192 | tf_op jit(solution)/shard_map/ppermute | solution.py:384
  15.0 13.0 %collective-permute-start.5 = (bf16[8,4608]{1,0:T(8,128)(2,1)S(1)}, bf16[8,4608]{1,0:T(8,128)(2,1)S(1)}, u32[]{:S(2)}, u32[]{:S(2)}) collective-permute-start(bf16[8,4608]{1,0:T(8,128)(2,1)S(1)} %get-tuple-element.32), channel_id=1, source_target_pairs={{0,12},{2,14},{4,8},{6,10},{8,4},{10,6},{12,0},{14,2},{1,13},{3,15... | collective-permute-start | bytes 221192 | tf_op jit(solution)/shard_map/ppermute | solution.py:384
  18.6 9.4 %collective-permute-start.6 = (bf16[8,4608]{1,0:T(8,128)(2,1)S(1)}, bf16[8,4608]{1,0:T(8,128)(2,1)S(1)}, u32[]{:S(2)}, u32[]{:S(2)}) collective-permute-start(bf16[8,4608]{1,0:T(8,128)(2,1)S(1)} %get-tuple-element.33), channel_id=1, source_target_pairs={{0,14},{2,12},{4,10},{6,8},{8,6},{10,4},{12,2},{14,0},{1,15},{3,13... | collective-permute-start | bytes 221192 | tf_op jit(solution)/shard_map/ppermute | solution.py:384
  18.6 29.4 %copy-start.3 = (f32[7168]{0:T(1024)S(1)}, f32[7168]{0:T(1024)}, u32[]{:S(2)}) copy-start(f32[7168]{0:T(1024)} %param.18) | copy-start | bytes 86020
  29.4 1.6 %collective-permute-start.7 = (f32[64,896]{1,0:T(8,128)S(1)}, f32[64,896]{1,0:T(8,128)S(1)}, u32[]{:S(2)}, u32[]{:S(2)}) collective-permute-start(f32[64,896]{1,0:T(8,128)S(1)} %project.1.mine_ref), channel_id=1, source_target_pairs={{0,1},{1,0},{2,3},{3,2},{4,5},{5,4},{6,7},{7,6},{8,9},{9,8},{10,11... | collective-permute-start | bytes 688136 | tf_op jit(solution)/shard_map/ppermute | solution.py:389
  48.1 23.7 %copy-start.1 = (s32[4,2]{0,1:T(2,128)S(1)}, s32[4,2]{0,1:T(2,128)}, u32[]{:S(2)}) copy-start(s32[4,2]{0,1:T(2,128)} %param.19) | copy-start | bytes 100
  48.2 23.7 %copy-start.2 = (f32[4,2]{0,1:T(2,128)S(1)}, f32[4,2]{0,1:T(2,128)}, u32[]{:S(2)}) copy-start(f32[4,2]{0,1:T(2,128)} %param.20) | copy-start | bytes 100
  48.2 1.6 %collective-permute-start.8 = (bf16[16,7168]{1,0:T(8,128)(2,1)S(1)}, bf16[16,7168]{1,0:T(8,128)(2,1)S(1)}, u32[]{:S(2)}, u32[]{:S(2)}) collective-permute-start(bf16[16,7168]{1,0:T(8,128)(2,1)S(1)} %multiply_convert_fusion.mine_ref), channel_id=1, source_target_pairs={{0,1},{1,0},{2,3},{3,2},{4,5},{5,4},{6,7},{7,6},{8,9},{9,8},{10,11... | collective-permute-start | bytes 688136 | tf_op jit(solution)/shard_map/ppermute | solution.py:395
  58.4 1.9 %collective-permute-start.9 = (f32[16,7168]{1,0:T(8,128)S(1)}, f32[16,7168]{1,0:T(8,128)S(1)}, u32[]{:S(2)}, u32[]{:S(2)}) collective-permute-start(f32[16,7168]{1,0:T(8,128)S(1)} %get-tuple-element.44), channel_id=1, source_target_pairs={{0,1},{1,0},{2,3},{3,2},{4,5},{5,4},{6,7},{7,6},{8,9},{9,8},{10,11... | collective-permute-start | bytes 1376264 | tf_op jit(solution)/shard_map/ppermute | solution.py:397

commit v4 on v3

--- a/solution.py
+++ b/solution.py
@@ -186,10 +186,12 @@
 
 
 def load_kernel(gate_hbm, up_hbm, after_ref, both_ref, sems):
-    copies = (
-        pltpu.make_async_copy(gate_hbm, both_ref.at[0], sems.at[0]),
-        pltpu.make_async_copy(up_hbm, both_ref.at[1], sems.at[1]),
-    )
+    half = both_ref.shape[2]
+    parts = ((gate_hbm, 0), (gate_hbm, half), (up_hbm, 0))
+    copies = [
+        pltpu.make_async_copy(src.at[:, pl.ds(start, half)], both_ref.at[i], sems.at[i])
+        for i, (src, start) in enumerate(parts)
+    ]
     for copy in copies:
         copy.start()
     for copy in copies:
@@ -200,13 +202,13 @@
     gate, up = [pltpu.with_memory_space_constraint(w, pltpu.HBM) for w in (gate, up)]
     return pl.pallas_call(
         load_kernel,
-        out_shape=VMEM((2,) + gate.shape, gate.dtype),
+        out_shape=VMEM((3, gate.shape[0], gate.shape[1] // 2), gate.dtype),
         in_specs=[pl.BlockSpec(memory_space=pltpu.HBM)] * 2 + [pl.BlockSpec(memory_space=pl.ANY)],
         out_specs=pl.BlockSpec(memory_space=VMEM),
-        scratch_shapes=[pltpu.SemaphoreType.DMA((2,))],
+        scratch_shapes=[pltpu.SemaphoreType.DMA((3,))],
         compiler_params=pltpu.CompilerParams(vmem_limit_bytes=1 << 20),
         cost_estimate=pl.CostEstimate(
-            flops=0, bytes_accessed=2 * (gate.size + up.size), transcendentals=0
+            flops=0, bytes_accessed=3 * gate.size, transcendentals=0
         ),
         name="load",
     )(gate, up, after)
@@ -296,43 +298,48 @@
 
 
 def expert_kernel(
-    mine_ref, other_ref, both_ref, down_hbm, keep_ref, send_ref,
-    x_ref, act_ref, down_ref, out_sems
+    mine_ref, other_ref, both_ref, up_hbm, down_hbm, keep_ref, send_ref,
+    x_ref, act_ref, up_ref, down_ref, sems
 ):
-    half, width = mine_ref.shape
+    rows = mine_ref.shape[0]
     outs, _, broad = down_ref.shape
-
-    def fetch_down(i):
+    half = both_ref.shape[2]
+
+    def fetch(i):
         cols = pl.ds(i * broad, broad)
-        return pltpu.make_async_copy(down_hbm.at[:, cols], down_ref.at[i], out_sems.at[i])
-
+        return pltpu.make_async_copy(down_hbm.at[:, cols], down_ref.at[i], sems.at[i])
+
+    rest = pltpu.make_async_copy(up_hbm.at[:, pl.ds(half, half)], up_ref, sems.at[outs])
+    rest.start()
+    fetch(0).start()
+    x_ref[:rows, :] = mine_ref[...]
+    x_ref[rows:, :] = other_ref[...]
+    for i in range(2):
+        gate = jnp.dot(x_ref[...], both_ref[i], preferred_element_type=F32)
+        if i:
+            for j in range(4, outs):
+                fetch(j).start()
+            up = jnp.dot(x_ref[...], up_ref[...], preferred_element_type=F32)
+        else:
+            up = jnp.dot(x_ref[...], both_ref[2], preferred_element_type=F32)
+            rest.wait()
+            for j in range(1, 4):
+                fetch(j).start()
+        act = (gate / (1.0 + jnp.exp(-gate)) * up).astype(BF16)
+        act_ref[:, i * half : (i + 1) * half] = act
     for i in range(outs):
-        fetch_down(i).start()
-    x_ref[:half, :] = mine_ref[...]
-    x_ref[half:, :] = other_ref[...]
-    wide = 512
-
-    def hidden_units(i, _):
-        cols = pl.ds(pl.multiple_of(i * wide, wide), wide)
-        gate = jnp.dot(x_ref[...], both_ref[0, :, cols], preferred_element_type=F32)
-        up = jnp.dot(x_ref[...], both_ref[1, :, cols], preferred_element_type=F32)
-        act_ref[:, cols] = (gate / (1.0 + jnp.exp(-gate)) * up).astype(BF16)
-        return 0
-
-    lax.fori_loop(0, both_ref.shape[2] // wide, hidden_units, 0)
-    for i in range(outs):
-        fetch_down(i).wait()
+        fetch(i).wait()
         part = jnp.dot(act_ref[...], down_ref[i], preferred_element_type=F32)
-        keep_ref[:, i * broad : (i + 1) * broad] = part[:half]
-        send_ref[:, i * broad : (i + 1) * broad] = part[half:].astype(send_ref.dtype)
-
-
-def run_experts(mine, other, both, down):
+        keep_ref[:, i * broad : (i + 1) * broad] = part[:rows]
+        send_ref[:, i * broad : (i + 1) * broad] = part[rows:].astype(send_ref.dtype)
+
+
+def run_experts(mine, other, both, up, down):
     rows, width = mine.shape
-    units = both.shape[2]
+    units = up.shape[1]
     outs = 7
     both = pltpu.with_memory_space_constraint(both, VMEM)
-    down = pltpu.with_memory_space_constraint(down, pltpu.HBM)
+    up, down = [pltpu.with_memory_space_constraint(w, pltpu.HBM) for w in (up, down)]
     whole = pl.BlockSpec(memory_space=VMEM)
     return pl.pallas_call(
         expert_kernel,
@@ -340,20 +347,48 @@
             jax.ShapeDtypeStruct((rows, width), F32),
             jax.ShapeDtypeStruct((rows, width), F32),
         ),
-        in_specs=[whole] * 3 + [pl.BlockSpec(memory_space=pltpu.HBM)],
+        in_specs=[whole] * 3 + [pl.BlockSpec(memory_space=pltpu.HBM)] * 2,
         out_specs=(whole, whole),
         scratch_shapes=[
             VMEM((2 * rows, width), BF16),
             VMEM((2 * rows, units), BF16),
+            VMEM((width, units // 2), BF16),
             VMEM((outs, units, width // outs), BF16),
-            pltpu.SemaphoreType.DMA((outs,)),
+            pltpu.SemaphoreType.DMA((outs + 1,)),
         ],
-        compiler_params=pltpu.CompilerParams(vmem_limit_bytes=18 << 20),
+        compiler_params=pltpu.CompilerParams(vmem_limit_bytes=26 << 20),
         cost_estimate=pl.CostEstimate(
-            flops=12 * rows * width * units, bytes_accessed=2 * width * units, transcendentals=0
+            flops=12 * rows * width * units, bytes_accessed=3 * width * units, transcendentals=0
         ),
         name="experts",
-    )(mine, other, both, down)
+    )(mine, other, both, up, down)
+
+
+def norm_kernel(received_ref, gain_ref, out_ref):
+    roles = received_ref.shape[0]
+    width = out_ref.shape[1]
+    cols = width // roles
+    total = jnp.float32(0.0)
+    for r in range(roles):
+        x = received_ref[r, :, :cols].astype(F32)
+        total += jnp.sum(x * x, axis=1, keepdims=True)
+    inverse = lax.rsqrt(total / width + 1e-06)
+    for r in range(roles):
+        x = received_ref[r, :, :cols].astype(F32)
+        here = slice(r * cols, (r + 1) * cols)
+        out_ref[:, here] = (x * inverse * gain_ref[:, here]).astype(BF16)
+
+
+def normalise(received, gain):
+    whole = pl.BlockSpec(memory_space=VMEM)
+    return pl.pallas_call(
+        norm_kernel,
+        out_shape=jax.ShapeDtypeStruct((received.shape[1], gain.shape[1]), BF16),
+        in_specs=[whole] * 2,
+        out_specs=whole,
+        compiler_params=pltpu.CompilerParams(vmem_limit_bytes=4 << 20),
+        name="normalise",
+    )(received, gain)
 
 
 def fast(
@@ -389,11 +424,9 @@
     other_value = lax.ppermute(partial_value, "head", [(0, 1), (1, 0)])
     outgoing = dispatch(partial_value, other_value, messages)
     received = lax.all_to_all(outgoing, "role", split_axis=0, concat_axis=0, tiled=True)
-    x = received[:, :, :cols].transpose(1, 0, 2).reshape(roles * CAP, width).astype(F32)
-    inverse = lax.rsqrt(jnp.mean(x * x, axis=1, keepdims=True) + 1e-06)
-    normed = (x * inverse * norm_gain[None, :]).astype(BF16)
+    normed = normalise(received, norm_gain.reshape(1, -1))
     other = lax.ppermute(normed, "head", [(0, 1), (1, 0)])
-    keep, send = run_experts(normed, other, both_weights, down_weight)
+    keep, send = run_experts(normed, other, both_weights, up_weight, down_weight)
     summed = (keep + lax.ppermute(send, "head", [(0, 1), (1, 0)])).astype(BF16)
     returned = lax.all_to_all(
         summed.reshape(roles, CAP, width), "role", split_axis=0, concat_axis=0, tiled=True

time: 73.4 us -> 71.6 us (0.975)
  Pallas kernels: 26.3 us -> 24.9 us
    pallas_call x1 -> x2, Pallas kernels: 9.37 us -> 7.57 us  [the longest x1 7.39 us: load(): pl.pallas_call(load_kernel, out_shape=VMEM((3, gate.shape[0], gate.shape[...]
  transfers between devices with their start and end apart: 10 -> 10, of which waited for: 3 -> 3; matrix products, arithmetic and copies ran while one was open for 0% -> 0% of each run, Pallas kernels for 13% -> 10%
where the time goes in v4:
time: 71.6 us; the launch traced here: 71.4 us
  blocking collectives  27.9 us (39%)
  Pallas kernels  24.9 us (35%)
  starting transfers between devices  12.8 us (18%)
  waiting for transfers between devices  4.65 us (6%)
  local copies, waits for them, and re-layouts  0.92 us (1%)
    all_to_all x1, blocking collectives, fast(): lax.all_to_all(outgoing, 'role', split_axis=0, concat_axis=0, tiled=True)  16.4 us
    ppermute x7, starting transfers between devices, fast(): lax.ppermute(messages[step], 'role', [(i, i ^ step) for i in range(roles)])  12.5 us
    all_to_all x1, blocking collectives, fast(): lax.all_to_all(summed.reshape(roles, CAP, width), 'role', split_axis=0, c...  11.4 us
    pallas_call x1, Pallas kernels, run_experts(): pl.pallas_call(expert_kernel, out_shape=(jax.ShapeDtypeStruct((rows, widt...  9.06 us
    pallas_call x1, Pallas kernels, load(): pl.pallas_call(load_kernel, out_shape=VMEM((3, gate.shape[0], gate.shape[...  7.39 us
    pallas_call x1, Pallas kernels, attend(): pl.pallas_call(attend_kernel, out_shape=(VMEM(weight.shape, weight.dtype)...  5.3 us
    ppermute x1, waiting for transfers between devices, fast(): summed = (keep + lax.ppermute(send, 'head', [(0, 1), (1, 0)])).astype(BF16)  1.68 us
    ppermute x1, waiting for transfers between devices, fast(): other = lax.ppermute(normed, 'head', [(0, 1), (1, 0)])  1.48 us
  transfers between devices with their start and end apart: 10, of which 3 were waited for; matrix products, arithmetic and copies ran while one was open for 0% of the time, Pallas kernels for 10%

profile of v4, /device:TPU:0, one launch (start us, length us, event | category | flops | bytes accessed | tf_op | source)
XLA Modules:
  0.0 71.4 jit_solution(14117336620811746170)
XLA Ops:
  0.0 0.0 copy-start
  0.0 0.8 %copy-done = bf16[4,7168]{1,0:T(4,128)(2,1)S(1)} copy-done((bf16[4,7168]{1,0:T(4,128)(2,1)S(1)}, bf16[4,7168]{1,0:T(4,128)(2,1)}, u32[]{:S(2)}) %copy-start) | copy-done | bytes 57368
  0.8 5.3 %attend.1 = (bf16[4096,896]{1,0:T(8,128)(2,1)S(1)}, bf16[8,4608]{1,0:T(8,128)(2,1)S(1)}, bf16[8,4608]{1,0:T(8,128)(2,1)S(1)}, bf16[8,4608]{1,0:T(8,128)(2,1)S(1)...) custom-call(bf16[4,7168]{1,0:T(4,128)(2,1)S(1)} %copy-done, ...), custom_call_target="tpu_custom_call" | custom-call | tf_op jit(solution)/shard_map/attend/pallas_call | solution.py:128
  6.1 3.0 %collective-permute-start = (bf16[8,4608]{1,0:T(8,128)(2,1)S(1)}, bf16[8,4608]{1,0:T(8,128)(2,1)S(1)}, u32[]{:S(2)}, u32[]{:S(2)}) collective-permute-start(bf16[8,4608]{1,0:T(8,128)(2,1)S(1)} %get-tuple-element.27), channel_id=1, source_target_pairs={{0,2},{2,0},{4,6},{6,4},{8,10},{10,8},{12,14},{14,12},{1,3},{3,1},... | collective-permute-start | bytes 221192 | tf_op jit(solution)/shard_map/ppermute | solution.py:419
  9.2 1.6 %collective-permute-start.1 = (bf16[8,4608]{1,0:T(8,128)(2,1)S(1)}, bf16[8,4608]{1,0:T(8,128)(2,1)S(1)}, u32[]{:S(2)}, u32[]{:S(2)}) collective-permute-start(bf16[8,4608]{1,0:T(8,128)(2,1)S(1)} %get-tuple-element.28), channel_id=1, source_target_pairs={{0,4},{2,6},{4,0},{6,2},{8,12},{10,14},{12,8},{14,10},{1,5},{3,7},... | collective-permute-start | bytes 221192 | tf_op jit(solution)/shard_map/ppermute | solution.py:419
  10.7 0.0 collective-permute-start.2
  10.7 3.0 %collective-permute-start.3 = (bf16[8,4608]{1,0:T(8,128)(2,1)S(1)}, bf16[8,4608]{1,0:T(8,128)(2,1)S(1)}, u32[]{:S(2)}, u32[]{:S(2)}) collective-permute-start(bf16[8,4608]{1,0:T(8,128)(2,1)S(1)} %get-tuple-element.30), channel_id=1, source_target_pairs={{0,8},{2,10},{4,12},{6,14},{8,0},{10,2},{12,4},{14,6},{1,9},{3,11}... | collective-permute-start | bytes 221192 | tf_op jit(solution)/shard_map/ppermute | solution.py:419
  13.7 1.3 %collective-permute-start.4 = (bf16[8,4608]{1,0:T(8,128)(2,1)S(1)}, bf16[8,4608]{1,0:T(8,128)(2,1)S(1)}, u32[]{:S(2)}, u32[]{:S(2)}) collective-permute-start(bf16[8,4608]{1,0:T(8,128)(2,1)S(1)} %get-tuple-element.31), channel_id=1, source_target_pairs={{0,10},{2,8},{4,14},{6,12},{8,2},{10,0},{12,6},{14,4},{1,11},{3,9}... | collective-permute-start | bytes 221192 | tf_op jit(solution)/shard_map/ppermute | solution.py:419
  15.0 0.0 collective-permute-done.refs_1_
  15.0 3.6 %collective-permute-start.5 = (bf16[8,4608]{1,0:T(8,128)(2,1)S(1)}, bf16[8,4608]{1,0:T(8,128)(2,1)S(1)}, u32[]{:S(2)}, u32[]{:S(2)}) collective-permute-start(bf16[8,4608]{1,0:T(8,128)(2,1)S(1)} %get-tuple-element.32), channel_id=1, source_target_pairs={{0,12},{2,14},{4,8},{6,10},{8,4},{10,6},{12,0},{14,2},{1,13},{3,15... | collective-permute-start | bytes 221192 | tf_op jit(solution)/shard_map/ppermute | solution.py:419
  18.6 0.0 collective-permute-done.1.refs_2_
  18.6 0.0 collective-permute-start.6
  18.6 0.0 copy-start.1
  18.6 7.4 %load.1.both_ref = bf16[3,7168,512]{2,1,0:T(8,128)(2,1)S(1)} custom-call(bf16[7168,1024]{1,0:T(8,128)(2,1)} %gate_hbm.1, bf16[7168,1024]{1,0:T(8,128)(2,1)} %up_hbm.3, bf16[8,4608]{1,0:T(8,128)(2,1)S(1)} %get-tuple-element.34.after_ref.refs_0_), custom_call_target="tpu_custom_call" | custom-call | bytes 22020096 | tf_op jit(solution)/shard_map/load/pallas_call | solution.py:203
  26.0 0.0 collective-permute-done.2.refs_3_
  26.0 0.0 collective-permute-done.3.refs_4_
  26.1 0.0 collective-permute-done.4.refs_5_
  26.1 0.0 collective-permute-done.5.refs_6_
  26.1 0.0 collective-permute-done.6.refs_7_
  26.1 1.4 %project.1.mine_ref = f32[64,896]{1,0:T(8,128)S(1)} custom-call(bf16[4096,896]{1,0:T(8,128)(2,1)S(1)} %get-tuple-element.25.weight_ref, bf16[8,4608]{1,0:T(8,128)(2,1)S(1)} %get-tuple-element.34.after_ref.refs_0_, bf16[8,4608]{1,0:T(8,128)(2,1)S(1)} %collective-permute-done.refs_1_, bf16[8,4608]{1,0:T(8,128)(2,1)S(1)} %collective-permute-done.1.refs_2_, ...), custom_call_target="tpu_custom_call" | custom-call | tf_op jit(solution)/shard_map/project/pallas_call | solution.py:228
  27.4 0.1 collective-permute-start.7
  27.5 1.5 %collective-permute-done.7.other_ref = f32[64,896]{1,0:T(8,128)S(1)} collective-permute-done((f32[64,896]{1,0:T(8,128)S(1)}, f32[64,896]{1,0:T(8,128)S(1)}, u32[]{:S(2)}, u32[]{:S(2)}) %collective-permute-start.7) | collective-permute-done | bytes 229408 | tf_op jit(solution)/shard_map/ppermute | solution.py:424
  29.0 0.3 dispatch.1
  29.3 16.4 %all_to_all.10.received_ref = bf16[8,16,1152]{2,1,0:T(8,128)(2,1)S(1)} all-to-all(bf16[8,16,1152]{2,1,0:T(8,128)(2,1)S(1)} %dispatch.1), channel_id=1, replica_groups=mesh['groups'=2,'role'=8,'head'=2] {'role'}, dimensions={0} | all-to-all | bytes 589824 | tf_op jit(solution)/shard_map/all_to_all | solution.py:426
  45.8 0.0 copy-done.1
  45.8 0.2 normalise.1.mine_ref
  46.0 0.0 copy-start.2
  46.0 0.0 copy-start.3
  46.0 0.1 collective-permute-start.8
  46.1 1.5 %collective-permute-done.8.other_ref = bf16[16,7168]{1,0:T(8,128)(2,1)S(1)} collective-permute-done((bf16[16,7168]{1,0:T(8,128)(2,1)S(1)}, bf16[16,7168]{1,0:T(8,128)(2,1)S(1)}, u32[]{:S(2)}, u32[]{:S(2)}) %collective-permute-start.8) | collective-permute-done | bytes 229408 | tf_op jit(solution)/shard_map/ppermute | solution.py:428
  47.5 9.1 %experts.1 = (f32[16,7168]{1,0:T(8,128)S(1)}, f32[16,7168]{1,0:T(8,128)S(1)}) custom-call(bf16[16,7168]{1,0:T(8,128)(2,1)S(1)} %normalise.1.mine_ref, bf16[16,7168]{1,0:T(8,128)(2,1)S(1)} %collective-permute-done.8.other_ref, bf16[3,7168,512]{2,1,0:T(8,128)(2,1)S(1)} %load.1.both_ref, bf16[7168,1024]{1,0:T(8,128)(2,1)} %up_hbm.3, bf16[1024,7168]{1,0:T(8,128)(2,1)} %down_hbm.1), custom_call_target="tpu_custom_call" | custom-call | flops 1409286144 | bytes 22020096 | tf_op jit(solution)/shard_map/experts/pallas_call | solution.py:344
  56.6 0.2 collective-permute-start.9
  56.8 1.7 %collective-permute-done.9 = f32[16,7168]{1,0:T(8,128)S(1)} collective-permute-done((f32[16,7168]{1,0:T(8,128)S(1)}, f32[16,7168]{1,0:T(8,128)S(1)}, u32[]{:S(2)}, u32[]{:S(2)}) %collective-permute-start.9) | collective-permute-done | bytes 458784 | tf_op jit(solution)/shard_map/ppermute | solution.py:430
  58.5 0.1 reshape.7
  58.6 11.4 %all_to_all.11.returned_ref = bf16[8,2,7168]{2,1,0:T(2,128)(2,1)S(1)} all-to-all(bf16[8,2,7168]{2,1,0:T(2,128)(2,1)S(1)} %reshape.7), channel_id=1, replica_groups=mesh['groups'=2,'role'=8,'head'=2] {'role'}, dimensions={0} | all-to-all | bytes 458752 | tf_op jit(solution)/shard_map/all_to_all | solution.py:431
  70.1 0.0 copy-done.2
  70.1 0.0 copy-done.3
  70.1 1.3 %combine.1 = bf16[4,7168]{1,0:T(4,128)(2,1)} custom-call(s32[2,4]{1,0:T(2,128)S(1)} %bitcast.6, f32[2,4]{1,0:T(2,128)S(1)} %bitcast.7, bf16[8,16,1152]{2,1,0:T(8,128)(2,1)S(1)} %all_to_all.10.received_ref, bf16[8,2,7168]{2,1,0:T(2,128)(2,1)S(1)} %all_to_all.11.returned_ref), custom_call_target="tpu_custom_call" | custom-call | tf_op jit(solution)/shard_map/combine/pallas_call | solution.py:177
  (1 shorter events, 0.0 us)
Async XLA Ops:
  0.0 0.8 %copy-start = (bf16[4,7168]{1,0:T(4,128)(2,1)S(1)}, bf16[4,7168]{1,0:T(4,128)(2,1)}, u32[]{:S(2)}) copy-start(bf16[4,7168]{1,0:T(4,128)(2,1)} %resid_ref.1) | copy-start | bytes 172036
  6.1 8.9 %collective-permute-start = (bf16[8,4608]{1,0:T(8,128)(2,1)S(1)}, bf16[8,4608]{1,0:T(8,128)(2,1)S(1)}, u32[]{:S(2)}, u32[]{:S(2)}) collective-permute-start(bf16[8,4608]{1,0:T(8,128)(2,1)S(1)} %get-tuple-element.27), channel_id=1, source_target_pairs={{0,2},{2,0},{4,6},{6,4},{8,10},{10,8},{12,14},{14,12},{1,3},{3,1},... | collective-permute-start | bytes 221192 | tf_op jit(solution)/shard_map/ppermute | solution.py:419
  9.2 9.5 %collective-permute-start.1 = (bf16[8,4608]{1,0:T(8,128)(2,1)S(1)}, bf16[8,4608]{1,0:T(8,128)(2,1)S(1)}, u32[]{:S(2)}, u32[]{:S(2)}) collective-permute-start(bf16[8,4608]{1,0:T(8,128)(2,1)S(1)} %get-tuple-element.28), channel_id=1, source_target_pairs={{0,4},{2,6},{4,0},{6,2},{8,12},{10,14},{12,8},{14,10},{1,5},{3,7},... | collective-permute-start | bytes 221192 | tf_op jit(solution)/shard_map/ppermute | solution.py:419
  10.7 15.3 %collective-permute-start.2 = (bf16[8,4608]{1,0:T(8,128)(2,1)S(1)}, bf16[8,4608]{1,0:T(8,128)(2,1)S(1)}, u32[]{:S(2)}, u32[]{:S(2)}) collective-permute-start(bf16[8,4608]{1,0:T(8,128)(2,1)S(1)} %get-tuple-element.29), channel_id=1, source_target_pairs={{0,6},{2,4},{4,2},{6,0},{8,14},{10,12},{12,10},{14,8},{1,7},{3,5},... | collective-permute-start | bytes 221192 | tf_op jit(solution)/shard_map/ppermute | solution.py:419
  10.7 15.3 %collective-permute-start.3 = (bf16[8,4608]{1,0:T(8,128)(2,1)S(1)}, bf16[8,4608]{1,0:T(8,128)(2,1)S(1)}, u32[]{:S(2)}, u32[]{:S(2)}) collective-permute-start(bf16[8,4608]{1,0:T(8,128)(2,1)S(1)} %get-tuple-element.30), channel_id=1, source_target_pairs={{0,8},{2,10},{4,12},{6,14},{8,0},{10,2},{12,4},{14,6},{1,9},{3,11}... | collective-permute-start | bytes 221192 | tf_op jit(solution)/shard_map/ppermute | solution.py:419
  13.7 12.3 %collective-permute-start.4 = (bf16[8,4608]{1,0:T(8,128)(2,1)S(1)}, bf16[8,4608]{1,0:T(8,128)(2,1)S(1)}, u32[]{:S(2)}, u32[]{:S(2)}) collective-permute-start(bf16[8,4608]{1,0:T(8,128)(2,1)S(1)} %get-tuple-element.31), channel_id=1, source_target_pairs={{0,10},{2,8},{4,14},{6,12},{8,2},{10,0},{12,6},{14,4},{1,11},{3,9}... | collective-permute-start | bytes 221192 | tf_op jit(solution)/shard_map/ppermute | solution.py:419
  15.0 11.1 %collective-permute-start.5 = (bf16[8,4608]{1,0:T(8,128)(2,1)S(1)}, bf16[8,4608]{1,0:T(8,128)(2,1)S(1)}, u32[]{:S(2)}, u32[]{:S(2)}) collective-permute-start(bf16[8,4608]{1,0:T(8,128)(2,1)S(1)} %get-tuple-element.32), channel_id=1, source_target_pairs={{0,12},{2,14},{4,8},{6,10},{8,4},{10,6},{12,0},{14,2},{1,13},{3,15... | collective-permute-start | bytes 221192 | tf_op jit(solution)/shard_map/ppermute | solution.py:419
  18.6 7.5 %collective-permute-start.6 = (bf16[8,4608]{1,0:T(8,128)(2,1)S(1)}, bf16[8,4608]{1,0:T(8,128)(2,1)S(1)}, u32[]{:S(2)}, u32[]{:S(2)}) collective-permute-start(bf16[8,4608]{1,0:T(8,128)(2,1)S(1)} %get-tuple-element.33), channel_id=1, source_target_pairs={{0,14},{2,12},{4,10},{6,8},{8,6},{10,4},{12,2},{14,0},{1,15},{3,13... | collective-permute-start | bytes 221192 | tf_op jit(solution)/shard_map/ppermute | solution.py:419
  18.6 27.1 %copy-start.1 = (f32[7168]{0:T(1024)S(1)}, f32[7168]{0:T(1024)}, u32[]{:S(2)}) copy-start(f32[7168]{0:T(1024)} %param.18) | copy-start | bytes 86020
  27.4 1.6 %collective-permute-start.7 = (f32[64,896]{1,0:T(8,128)S(1)}, f32[64,896]{1,0:T(8,128)S(1)}, u32[]{:S(2)}, u32[]{:S(2)}) collective-permute-start(f32[64,896]{1,0:T(8,128)S(1)} %project.1.mine_ref), channel_id=1, source_target_pairs={{0,1},{1,0},{2,3},{3,2},{4,5},{5,4},{6,7},{7,6},{8,9},{9,8},{10,11... | collective-permute-start | bytes 688136 | tf_op jit(solution)/shard_map/ppermute | solution.py:424
  46.0 24.1 %copy-start.2 = (s32[4,2]{0,1:T(2,128)S(1)}, s32[4,2]{0,1:T(2,128)}, u32[]{:S(2)}) copy-start(s32[4,2]{0,1:T(2,128)} %param.19) | copy-start | bytes 100
  46.0 24.1 %copy-start.3 = (f32[4,2]{0,1:T(2,128)S(1)}, f32[4,2]{0,1:T(2,128)}, u32[]{:S(2)}) copy-start(f32[4,2]{0,1:T(2,128)} %param.20) | copy-start | bytes 100
  46.0 1.6 %collective-permute-start.8 = (bf16[16,7168]{1,0:T(8,128)(2,1)S(1)}, bf16[16,7168]{1,0:T(8,128)(2,1)S(1)}, u32[]{:S(2)}, u32[]{:S(2)}) collective-permute-start(bf16[16,7168]{1,0:T(8,128)(2,1)S(1)} %normalise.1.mine_ref), channel_id=1, source_target_pairs={{0,1},{1,0},{2,3},{3,2},{4,5},{5,4},{6,7},{7,6},{8,9},{9,8},{10,11... | collective-permute-start | bytes 688136 | tf_op jit(solution)/shard_map/ppermute | solution.py:428
  56.6 1.9 %collective-permute-start.9 = (f32[16,7168]{1,0:T(8,128)S(1)}, f32[16,7168]{1,0:T(8,128)S(1)}, u32[]{:S(2)}, u32[]{:S(2)}) collective-permute-start(f32[16,7168]{1,0:T(8,128)S(1)} %get-tuple-element.44), channel_id=1, source_target_pairs={{0,1},{1,0},{2,3},{3,2},{4,5},{5,4},{6,7},{7,6},{8,9},{9,8},{10,11... | collective-permute-start | bytes 1376264 | tf_op jit(solution)/shard_map/ppermute | solution.py:430

commit v5 on v4

--- a/solution.py
+++ b/solution.py
@@ -345,7 +345,7 @@
         expert_kernel,
         out_shape=(
             jax.ShapeDtypeStruct((rows, width), F32),
-            jax.ShapeDtypeStruct((rows, width), F32),
+            jax.ShapeDtypeStruct((rows, width), BF16),
         ),
         in_specs=[whole] * 3 + [pl.BlockSpec(memory_space=pltpu.HBM)] * 2,
         out_specs=(whole, whole),
@@ -415,10 +415,9 @@
         cache_lengths, ids, residual, queries, cache, uv_weight, out_weight, roles
     )
     both_weights = load(gate_weight, up_weight, messages[0])
-    messages = [messages[0]] + [
-        lax.ppermute(messages[step], "role", [(i, i ^ step) for i in range(roles)])
-        for step in range(1, roles)
-    ]
+    for step in sorted(range(1, roles), reverse=True):
+        pairs = [(i, i ^ step) for i in range(roles)]
+        messages[step] = lax.ppermute(messages[step], "role", pairs)
     messages, both_weights = lax.optimization_barrier((messages, both_weights))
     partial_value = project(messages, out_weight)
     other_value = lax.ppermute(partial_value, "head", [(0, 1), (1, 0)])
@@ -427,7 +426,8 @@
     normed = normalise(received, norm_gain.reshape(1, -1))
     other = lax.ppermute(normed, "head", [(0, 1), (1, 0)])
     keep, send = run_experts(normed, other, both_weights, up_weight, down_weight)
-    summed = (keep + lax.ppermute(send, "head", [(0, 1), (1, 0)])).astype(BF16)
+    sent = lax.ppermute(send, "head", [(0, 1), (1, 0)])
+    summed = (keep + sent.astype(F32)).astype(BF16)
     returned = lax.all_to_all(
         summed.reshape(roles, CAP, width), "role", split_axis=0, concat_axis=0, tiled=True
     )

time: 71.6 us -> 71.3 us (level)
  no operation moved by 1% of the time
where the time goes in v5:
time: 71.3 us; the launch traced here: 71 us
  blocking collectives  27.9 us (39%)
  Pallas kernels  24.9 us (35%)
  starting transfers between devices  12.8 us (18%)
  waiting for transfers between devices  4.32 us (6%)
  local copies, waits for them, and re-layouts  0.92 us (1%)
    all_to_all x1, blocking collectives, fast(): lax.all_to_all(outgoing, 'role', split_axis=0, concat_axis=0, tiled=True)  16.4 us
    ppermute x7, starting transfers between devices, fast(): messages[step] = lax.ppermute(messages[step], 'role', pairs)  12.5 us
    all_to_all x1, blocking collectives, fast(): lax.all_to_all(summed.reshape(roles, CAP, width), 'role', split_axis=0, c...  11.4 us
    pallas_call x1, Pallas kernels, run_experts(): pl.pallas_call(expert_kernel, out_shape=(jax.ShapeDtypeStruct((rows, widt...  9.07 us
    pallas_call x1, Pallas kernels, load(): pl.pallas_call(load_kernel, out_shape=VMEM((3, gate.shape[0], gate.shape[...  7.39 us
    pallas_call x1, Pallas kernels, attend(): pl.pallas_call(attend_kernel, out_shape=(VMEM(weight.shape, weight.dtype)...  5.3 us
    ppermute x1, waiting for transfers between devices, fast(): other_value = lax.ppermute(partial_value, 'head', [(0, 1), (1, 0)])  1.48 us
    ppermute x1, waiting for transfers between devices, fast(): other = lax.ppermute(normed, 'head', [(0, 1), (1, 0)])  1.48 us
  transfers between devices with their start and end apart: 10, of which 3 were waited for; matrix products, arithmetic and copies ran while one was open for 0% of the time, Pallas kernels for 10%

profile of v5, /device:TPU:0, one launch (start us, length us, event | category | flops | bytes accessed | tf_op | source)
XLA Modules:
  0.0 71.0 jit_solution(10460543922332769018)
XLA Ops:
  0.0 0.0 copy-start
  0.0 0.8 %copy-done = bf16[4,7168]{1,0:T(4,128)(2,1)S(1)} copy-done((bf16[4,7168]{1,0:T(4,128)(2,1)S(1)}, bf16[4,7168]{1,0:T(4,128)(2,1)}, u32[]{:S(2)}) %copy-start) | copy-done | bytes 57368
  0.8 5.3 %attend.1 = (bf16[4096,896]{1,0:T(8,128)(2,1)S(1)}, bf16[8,4608]{1,0:T(8,128)(2,1)S(1)}, bf16[8,4608]{1,0:T(8,128)(2,1)S(1)}, bf16[8,4608]{1,0:T(8,128)(2,1)S(1)...) custom-call(bf16[4,7168]{1,0:T(4,128)(2,1)S(1)} %copy-done, ...), custom_call_target="tpu_custom_call" | custom-call | tf_op jit(solution)/shard_map/attend/pallas_call | solution.py:128
  6.1 3.0 %collective-permute-start = (bf16[8,4608]{1,0:T(8,128)(2,1)S(1)}, bf16[8,4608]{1,0:T(8,128)(2,1)S(1)}, u32[]{:S(2)}, u32[]{:S(2)}) collective-permute-start(bf16[8,4608]{1,0:T(8,128)(2,1)S(1)} %get-tuple-element.27), channel_id=1, source_target_pairs={{0,2},{2,0},{4,6},{6,4},{8,10},{10,8},{12,14},{14,12},{1,3},{3,1},... | collective-permute-start | bytes 221192 | tf_op jit(solution)/shard_map/ppermute | solution.py:420
  9.2 1.6 %collective-permute-start.1 = (bf16[8,4608]{1,0:T(8,128)(2,1)S(1)}, bf16[8,4608]{1,0:T(8,128)(2,1)S(1)}, u32[]{:S(2)}, u32[]{:S(2)}) collective-permute-start(bf16[8,4608]{1,0:T(8,128)(2,1)S(1)} %get-tuple-element.28), channel_id=1, source_target_pairs={{0,4},{2,6},{4,0},{6,2},{8,12},{10,14},{12,8},{14,10},{1,5},{3,7},... | collective-permute-start | bytes 221192 | tf_op jit(solution)/shard_map/ppermute | solution.py:420
  10.7 0.0 collective-permute-start.2
  10.7 3.0 %collective-permute-start.3 = (bf16[8,4608]{1,0:T(8,128)(2,1)S(1)}, bf16[8,4608]{1,0:T(8,128)(2,1)S(1)}, u32[]{:S(2)}, u32[]{:S(2)}) collective-permute-start(bf16[8,4608]{1,0:T(8,128)(2,1)S(1)} %get-tuple-element.30), channel_id=1, source_target_pairs={{0,8},{2,10},{4,12},{6,14},{8,0},{10,2},{12,4},{14,6},{1,9},{3,11}... | collective-permute-start | bytes 221192 | tf_op jit(solution)/shard_map/ppermute | solution.py:420
  13.7 1.3 %collective-permute-start.4 = (bf16[8,4608]{1,0:T(8,128)(2,1)S(1)}, bf16[8,4608]{1,0:T(8,128)(2,1)S(1)}, u32[]{:S(2)}, u32[]{:S(2)}) collective-permute-start(bf16[8,4608]{1,0:T(8,128)(2,1)S(1)} %get-tuple-element.31), channel_id=1, source_target_pairs={{0,10},{2,8},{4,14},{6,12},{8,2},{10,0},{12,6},{14,4},{1,11},{3,9}... | collective-permute-start | bytes 221192 | tf_op jit(solution)/shard_map/ppermute | solution.py:420
  15.0 0.0 collective-permute-done.refs_1_
  15.0 3.6 %collective-permute-start.5 = (bf16[8,4608]{1,0:T(8,128)(2,1)S(1)}, bf16[8,4608]{1,0:T(8,128)(2,1)S(1)}, u32[]{:S(2)}, u32[]{:S(2)}) collective-permute-start(bf16[8,4608]{1,0:T(8,128)(2,1)S(1)} %get-tuple-element.32), channel_id=1, source_target_pairs={{0,12},{2,14},{4,8},{6,10},{8,4},{10,6},{12,0},{14,2},{1,13},{3,15... | collective-permute-start | bytes 221192 | tf_op jit(solution)/shard_map/ppermute | solution.py:420
  18.6 0.0 collective-permute-done.1.refs_2_
  18.6 0.0 collective-permute-start.6
  18.6 0.0 copy-start.1
  18.6 7.4 %load.1.both_ref = bf16[3,7168,512]{2,1,0:T(8,128)(2,1)S(1)} custom-call(bf16[7168,1024]{1,0:T(8,128)(2,1)} %gate_hbm.1, bf16[7168,1024]{1,0:T(8,128)(2,1)} %up_hbm.3, bf16[8,4608]{1,0:T(8,128)(2,1)S(1)} %get-tuple-element.34.after_ref.refs_0_), custom_call_target="tpu_custom_call" | custom-call | bytes 22020096 | tf_op jit(solution)/shard_map/load/pallas_call | solution.py:203
  26.0 0.0 collective-permute-done.2.refs_3_
  26.0 0.0 collective-permute-done.3.refs_4_
  26.1 0.0 collective-permute-done.4.refs_5_
  26.1 0.0 collective-permute-done.5.refs_6_
  26.1 0.0 collective-permute-done.6.refs_7_
  26.1 1.4 %project.1.mine_ref = f32[64,896]{1,0:T(8,128)S(1)} custom-call(bf16[4096,896]{1,0:T(8,128)(2,1)S(1)} %get-tuple-element.25.weight_ref, bf16[8,4608]{1,0:T(8,128)(2,1)S(1)} %get-tuple-element.34.after_ref.refs_0_, bf16[8,4608]{1,0:T(8,128)(2,1)S(1)} %collective-permute-done.refs_1_, bf16[8,4608]{1,0:T(8,128)(2,1)S(1)} %collective-permute-done.1.refs_2_, ...), custom_call_target="tpu_custom_call" | custom-call | tf_op jit(solution)/shard_map/project/pallas_call | solution.py:228
  27.4 0.1 collective-permute-start.7
  27.5 1.5 %collective-permute-done.7.other_ref = f32[64,896]{1,0:T(8,128)S(1)} collective-permute-done((f32[64,896]{1,0:T(8,128)S(1)}, f32[64,896]{1,0:T(8,128)S(1)}, u32[]{:S(2)}, u32[]{:S(2)}) %collective-permute-start.7) | collective-permute-done | bytes 229408 | tf_op jit(solution)/shard_map/ppermute | solution.py:423
  29.0 0.3 dispatch.1
  29.3 16.4 %all_to_all.10.received_ref = bf16[8,16,1152]{2,1,0:T(8,128)(2,1)S(1)} all-to-all(bf16[8,16,1152]{2,1,0:T(8,128)(2,1)S(1)} %dispatch.1), channel_id=1, replica_groups=mesh['groups'=2,'role'=8,'head'=2] {'role'}, dimensions={0} | all-to-all | bytes 589824 | tf_op jit(solution)/shard_map/all_to_all | solution.py:425
  45.8 0.0 copy-done.1
  45.8 0.2 normalise.1.mine_ref
  46.0 0.0 copy-start.2
  46.0 0.0 copy-start.3
  46.0 0.1 collective-permute-start.8
  46.1 1.5 %collective-permute-done.8.other_ref = bf16[16,7168]{1,0:T(8,128)(2,1)S(1)} collective-permute-done((bf16[16,7168]{1,0:T(8,128)(2,1)S(1)}, bf16[16,7168]{1,0:T(8,128)(2,1)S(1)}, u32[]{:S(2)}, u32[]{:S(2)}) %collective-permute-start.8) | collective-permute-done | bytes 229408 | tf_op jit(solution)/shard_map/ppermute | solution.py:427
  47.5 9.1 %experts.1 = (f32[16,7168]{1,0:T(8,128)S(1)}, bf16[16,7168]{1,0:T(8,128)(2,1)S(1)}) custom-call(bf16[16,7168]{1,0:T(8,128)(2,1)S(1)} %normalise.1.mine_ref, bf16[16,7168]{1,0:T(8,128)(2,1)S(1)} %collective-permute-done.8.other_ref, bf16[3,7168,512]{2,1,0:T(8,128)(2,1)S(1)} %load.1.both_ref, bf16[7168,1024]{1,0:T(8,128)(2,1)} %up_hbm.3, ...), custom_call_target="tpu_custom_call" | custom-call | flops 1409286144 | bytes 22020096 | tf_op jit(solution)/shard_map/experts/pallas_call | solution.py:344
  56.6 0.2 collective-permute-start.9
  56.8 1.4 %collective-permute-done.9 = bf16[16,7168]{1,0:T(8,128)(2,1)S(1)} collective-permute-done((bf16[16,7168]{1,0:T(8,128)(2,1)S(1)}, bf16[16,7168]{1,0:T(8,128)(2,1)S(1)}, u32[]{:S(2)}, u32[]{:S(2)}) %collective-permute-start.9) | collective-permute-done | bytes 229408 | tf_op jit(solution)/shard_map/ppermute | solution.py:429
  58.2 0.1 reshape.7
  58.3 11.4 %all_to_all.11.returned_ref = bf16[8,2,7168]{2,1,0:T(2,128)(2,1)S(1)} all-to-all(bf16[8,2,7168]{2,1,0:T(2,128)(2,1)S(1)} %reshape.7), channel_id=1, replica_groups=mesh['groups'=2,'role'=8,'head'=2] {'role'}, dimensions={0} | all-to-all | bytes 458752 | tf_op jit(solution)/shard_map/all_to_all | solution.py:431
  69.7 0.0 copy-done.2
  69.7 0.0 copy-done.3
  69.7 1.3 %combine.1 = bf16[4,7168]{1,0:T(4,128)(2,1)} custom-call(s32[2,4]{1,0:T(2,128)S(1)} %bitcast.6, f32[2,4]{1,0:T(2,128)S(1)} %bitcast.7, bf16[8,16,1152]{2,1,0:T(8,128)(2,1)S(1)} %all_to_all.10.received_ref, bf16[8,2,7168]{2,1,0:T(2,128)(2,1)S(1)} %all_to_all.11.returned_ref), custom_call_target="tpu_custom_call" | custom-call | tf_op jit(solution)/shard_map/combine/pallas_call | solution.py:177
  (1 shorter events, 0.0 us)
Async XLA Ops:
  0.0 0.8 %copy-start = (bf16[4,7168]{1,0:T(4,128)(2,1)S(1)}, bf16[4,7168]{1,0:T(4,128)(2,1)}, u32[]{:S(2)}) copy-start(bf16[4,7168]{1,0:T(4,128)(2,1)} %resid_ref.1) | copy-start | bytes 172036
  6.1 8.9 %collective-permute-start = (bf16[8,4608]{1,0:T(8,128)(2,1)S(1)}, bf16[8,4608]{1,0:T(8,128)(2,1)S(1)}, u32[]{:S(2)}, u32[]{:S(2)}) collective-permute-start(bf16[8,4608]{1,0:T(8,128)(2,1)S(1)} %get-tuple-element.27), channel_id=1, source_target_pairs={{0,2},{2,0},{4,6},{6,4},{8,10},{10,8},{12,14},{14,12},{1,3},{3,1},... | collective-permute-start | bytes 221192 | tf_op jit(solution)/shard_map/ppermute | solution.py:420
  9.2 9.5 %collective-permute-start.1 = (bf16[8,4608]{1,0:T(8,128)(2,1)S(1)}, bf16[8,4608]{1,0:T(8,128)(2,1)S(1)}, u32[]{:S(2)}, u32[]{:S(2)}) collective-permute-start(bf16[8,4608]{1,0:T(8,128)(2,1)S(1)} %get-tuple-element.28), channel_id=1, source_target_pairs={{0,4},{2,6},{4,0},{6,2},{8,12},{10,14},{12,8},{14,10},{1,5},{3,7},... | collective-permute-start | bytes 221192 | tf_op jit(solution)/shard_map/ppermute | solution.py:420
  10.7 15.3 %collective-permute-start.2 = (bf16[8,4608]{1,0:T(8,128)(2,1)S(1)}, bf16[8,4608]{1,0:T(8,128)(2,1)S(1)}, u32[]{:S(2)}, u32[]{:S(2)}) collective-permute-start(bf16[8,4608]{1,0:T(8,128)(2,1)S(1)} %get-tuple-element.29), channel_id=1, source_target_pairs={{0,6},{2,4},{4,2},{6,0},{8,14},{10,12},{12,10},{14,8},{1,7},{3,5},... | collective-permute-start | bytes 221192 | tf_op jit(solution)/shard_map/ppermute | solution.py:420
  10.7 15.3 %collective-permute-start.3 = (bf16[8,4608]{1,0:T(8,128)(2,1)S(1)}, bf16[8,4608]{1,0:T(8,128)(2,1)S(1)}, u32[]{:S(2)}, u32[]{:S(2)}) collective-permute-start(bf16[8,4608]{1,0:T(8,128)(2,1)S(1)} %get-tuple-element.30), channel_id=1, source_target_pairs={{0,8},{2,10},{4,12},{6,14},{8,0},{10,2},{12,4},{14,6},{1,9},{3,11}... | collective-permute-start | bytes 221192 | tf_op jit(solution)/shard_map/ppermute | solution.py:420
  13.7 12.3 %collective-permute-start.4 = (bf16[8,4608]{1,0:T(8,128)(2,1)S(1)}, bf16[8,4608]{1,0:T(8,128)(2,1)S(1)}, u32[]{:S(2)}, u32[]{:S(2)}) collective-permute-start(bf16[8,4608]{1,0:T(8,128)(2,1)S(1)} %get-tuple-element.31), channel_id=1, source_target_pairs={{0,10},{2,8},{4,14},{6,12},{8,2},{10,0},{12,6},{14,4},{1,11},{3,9}... | collective-permute-start | bytes 221192 | tf_op jit(solution)/shard_map/ppermute | solution.py:420
  15.0 11.1 %collective-permute-start.5 = (bf16[8,4608]{1,0:T(8,128)(2,1)S(1)}, bf16[8,4608]{1,0:T(8,128)(2,1)S(1)}, u32[]{:S(2)}, u32[]{:S(2)}) collective-permute-start(bf16[8,4608]{1,0:T(8,128)(2,1)S(1)} %get-tuple-element.32), channel_id=1, source_target_pairs={{0,12},{2,14},{4,8},{6,10},{8,4},{10,6},{12,0},{14,2},{1,13},{3,15... | collective-permute-start | bytes 221192 | tf_op jit(solution)/shard_map/ppermute | solution.py:420
  18.6 7.5 %collective-permute-start.6 = (bf16[8,4608]{1,0:T(8,128)(2,1)S(1)}, bf16[8,4608]{1,0:T(8,128)(2,1)S(1)}, u32[]{:S(2)}, u32[]{:S(2)}) collective-permute-start(bf16[8,4608]{1,0:T(8,128)(2,1)S(1)} %get-tuple-element.33), channel_id=1, source_target_pairs={{0,14},{2,12},{4,10},{6,8},{8,6},{10,4},{12,2},{14,0},{1,15},{3,13... | collective-permute-start | bytes 221192 | tf_op jit(solution)/shard_map/ppermute | solution.py:420
  18.6 27.1 %copy-start.1 = (f32[7168]{0:T(1024)S(1)}, f32[7168]{0:T(1024)}, u32[]{:S(2)}) copy-start(f32[7168]{0:T(1024)} %param.18) | copy-start | bytes 86020
  27.4 1.6 %collective-permute-start.7 = (f32[64,896]{1,0:T(8,128)S(1)}, f32[64,896]{1,0:T(8,128)S(1)}, u32[]{:S(2)}, u32[]{:S(2)}) collective-permute-start(f32[64,896]{1,0:T(8,128)S(1)} %project.1.mine_ref), channel_id=1, source_target_pairs={{0,1},{1,0},{2,3},{3,2},{4,5},{5,4},{6,7},{7,6},{8,9},{9,8},{10,11... | collective-permute-start | bytes 688136 | tf_op jit(solution)/shard_map/ppermute | solution.py:423
  46.0 23.8 %copy-start.2 = (s32[4,2]{0,1:T(2,128)S(1)}, s32[4,2]{0,1:T(2,128)}, u32[]{:S(2)}) copy-start(s32[4,2]{0,1:T(2,128)} %param.19) | copy-start | bytes 100
  46.0 23.8 %copy-start.3 = (f32[4,2]{0,1:T(2,128)S(1)}, f32[4,2]{0,1:T(2,128)}, u32[]{:S(2)}) copy-start(f32[4,2]{0,1:T(2,128)} %param.20) | copy-start | bytes 100
  46.0 1.6 %collective-permute-start.8 = (bf16[16,7168]{1,0:T(8,128)(2,1)S(1)}, bf16[16,7168]{1,0:T(8,128)(2,1)S(1)}, u32[]{:S(2)}, u32[]{:S(2)}) collective-permute-start(bf16[16,7168]{1,0:T(8,128)(2,1)S(1)} %normalise.1.mine_ref), channel_id=1, source_target_pairs={{0,1},{1,0},{2,3},{3,2},{4,5},{5,4},{6,7},{7,6},{8,9},{9,8},{10,11... | collective-permute-start | bytes 688136 | tf_op jit(solution)/shard_map/ppermute | solution.py:427
  56.6 1.6 %collective-permute-start.9 = (bf16[16,7168]{1,0:T(8,128)(2,1)S(1)}, bf16[16,7168]{1,0:T(8,128)(2,1)S(1)}, u32[]{:S(2)}, u32[]{:S(2)}) collective-permute-start(bf16[16,7168]{1,0:T(8,128)(2,1)S(1)} %get-tuple-element.44), channel_id=1, source_target_pairs={{0,1},{1,0},{2,3},{3,2},{4,5},{5,4},{6,7},{7,6},{8,9},{9,8},{10,11... | collective-permute-start | bytes 688136 | tf_op jit(solution)/shard_map/ppermute | solution.py:429

commit v6 on v5

--- a/solution.py
+++ b/solution.py
@@ -159,14 +159,15 @@
             reach = min(256, cols - g * 256)
             start = r * cols + g * 256
             sum_ref[:, start : start + reach] = kept[g * share : (g + 1) * share, :reach]
+    row = lax.broadcasted_iota(jnp.int32, (CAP, 1), 0)
     for t in range(share):
-        extra = []
+        pair = None
         for k in range(2):
             slot = slot_of(ids_ref, t, k)
-            both = returned_ref[ids_ref[k, t]].astype(F32)
-            one = jnp.where(slot % CAP == 0, both[0:1], both[1:2])
-            extra.append(route_ref[k, t] * one)
-        sum_ref[t : t + 1, :] += extra[0] + extra[1]
+            weight = jnp.where(row == slot % CAP, route_ref[k, t], 0.0)
+            term = weight * returned_ref[ids_ref[k, t]].astype(F32)
+            pair = term if pair is None else pair + term
+        sum_ref[t : t + 1, :] += pair[0:1] + pair[1:2]
     out_ref[...] = sum_ref[...].astype(BF16)
 
 

time: 71.3 us -> 71.5 us (level)
  no operation moved by 1% of the time
where the time goes in v6:
time: 71.5 us; the launch traced here: 71.3 us
  blocking collectives  27.9 us (39%)
  Pallas kernels  25.2 us (35%)
  starting transfers between devices  12.8 us (18%)
  waiting for transfers between devices  4.32 us (6%)
  local copies, waits for them, and re-layouts  0.92 us (1%)
    all_to_all x1, blocking collectives, fast(): lax.all_to_all(outgoing, 'role', split_axis=0, concat_axis=0, tiled=True)  16.4 us
    ppermute x7, starting transfers between devices, fast(): messages[step] = lax.ppermute(messages[step], 'role', pairs)  12.5 us
    all_to_all x1, blocking collectives, fast(): lax.all_to_all(summed.reshape(roles, CAP, width), 'role', split_axis=0, c...  11.4 us
    pallas_call x1, Pallas kernels, run_experts(): pl.pallas_call(expert_kernel, out_shape=(jax.ShapeDtypeStruct((rows, widt...  9.07 us
    pallas_call x1, Pallas kernels, load(): pl.pallas_call(load_kernel, out_shape=VMEM((3, gate.shape[0], gate.shape[...  7.39 us
    pallas_call x1, Pallas kernels, attend(): pl.pallas_call(attend_kernel, out_shape=(VMEM(weight.shape, weight.dtype)...  5.3 us
    pallas_call x1, Pallas kernels, combine(): pl.pallas_call(combine_kernel, out_shape=jax.ShapeDtypeStruct((share, wid...  1.57 us
    ppermute x1, waiting for transfers between devices, fast(): other_value = lax.ppermute(partial_value, 'head', [(0, 1), (1, 0)])  1.48 us
  transfers between devices with their start and end apart: 10, of which 3 were waited for; matrix products, arithmetic and copies ran while one was open for 0% of the time, Pallas kernels for 10%

profile of v6, /device:TPU:0, one launch (start us, length us, event | category | flops | bytes accessed | tf_op | source)
XLA Modules:
  0.0 71.3 jit_solution(16748117130117498581)
XLA Ops:
  0.0 0.0 copy-start
  0.0 0.8 %copy-done = bf16[4,7168]{1,0:T(4,128)(2,1)S(1)} copy-done((bf16[4,7168]{1,0:T(4,128)(2,1)S(1)}, bf16[4,7168]{1,0:T(4,128)(2,1)}, u32[]{:S(2)}) %copy-start) | copy-done | bytes 57368
  0.8 5.3 %attend.1 = (bf16[4096,896]{1,0:T(8,128)(2,1)S(1)}, bf16[8,4608]{1,0:T(8,128)(2,1)S(1)}, bf16[8,4608]{1,0:T(8,128)(2,1)S(1)}, bf16[8,4608]{1,0:T(8,128)(2,1)S(1)...) custom-call(bf16[4,7168]{1,0:T(4,128)(2,1)S(1)} %copy-done, ...), custom_call_target="tpu_custom_call" | custom-call | tf_op jit(solution)/shard_map/attend/pallas_call | solution.py:128
  6.1 3.0 %collective-permute-start = (bf16[8,4608]{1,0:T(8,128)(2,1)S(1)}, bf16[8,4608]{1,0:T(8,128)(2,1)S(1)}, u32[]{:S(2)}, u32[]{:S(2)}) collective-permute-start(bf16[8,4608]{1,0:T(8,128)(2,1)S(1)} %get-tuple-element.27), channel_id=1, source_target_pairs={{0,2},{2,0},{4,6},{6,4},{8,10},{10,8},{12,14},{14,12},{1,3},{3,1},... | collective-permute-start | bytes 221192 | tf_op jit(solution)/shard_map/ppermute | solution.py:421
  9.2 1.6 %collective-permute-start.1 = (bf16[8,4608]{1,0:T(8,128)(2,1)S(1)}, bf16[8,4608]{1,0:T(8,128)(2,1)S(1)}, u32[]{:S(2)}, u32[]{:S(2)}) collective-permute-start(bf16[8,4608]{1,0:T(8,128)(2,1)S(1)} %get-tuple-element.28), channel_id=1, source_target_pairs={{0,4},{2,6},{4,0},{6,2},{8,12},{10,14},{12,8},{14,10},{1,5},{3,7},... | collective-permute-start | bytes 221192 | tf_op jit(solution)/shard_map/ppermute | solution.py:421
  10.7 0.0 collective-permute-start.2
  10.7 3.0 %collective-permute-start.3 = (bf16[8,4608]{1,0:T(8,128)(2,1)S(1)}, bf16[8,4608]{1,0:T(8,128)(2,1)S(1)}, u32[]{:S(2)}, u32[]{:S(2)}) collective-permute-start(bf16[8,4608]{1,0:T(8,128)(2,1)S(1)} %get-tuple-element.30), channel_id=1, source_target_pairs={{0,8},{2,10},{4,12},{6,14},{8,0},{10,2},{12,4},{14,6},{1,9},{3,11}... | collective-permute-start | bytes 221192 | tf_op jit(solution)/shard_map/ppermute | solution.py:421
  13.7 1.3 %collective-permute-start.4 = (bf16[8,4608]{1,0:T(8,128)(2,1)S(1)}, bf16[8,4608]{1,0:T(8,128)(2,1)S(1)}, u32[]{:S(2)}, u32[]{:S(2)}) collective-permute-start(bf16[8,4608]{1,0:T(8,128)(2,1)S(1)} %get-tuple-element.31), channel_id=1, source_target_pairs={{0,10},{2,8},{4,14},{6,12},{8,2},{10,0},{12,6},{14,4},{1,11},{3,9}... | collective-permute-start | bytes 221192 | tf_op jit(solution)/shard_map/ppermute | solution.py:421
  15.0 0.0 collective-permute-done.refs_1_
  15.0 3.6 %collective-permute-start.5 = (bf16[8,4608]{1,0:T(8,128)(2,1)S(1)}, bf16[8,4608]{1,0:T(8,128)(2,1)S(1)}, u32[]{:S(2)}, u32[]{:S(2)}) collective-permute-start(bf16[8,4608]{1,0:T(8,128)(2,1)S(1)} %get-tuple-element.32), channel_id=1, source_target_pairs={{0,12},{2,14},{4,8},{6,10},{8,4},{10,6},{12,0},{14,2},{1,13},{3,15... | collective-permute-start | bytes 221192 | tf_op jit(solution)/shard_map/ppermute | solution.py:421
  18.6 0.0 collective-permute-done.1.refs_2_
  18.6 0.0 collective-permute-start.6
  18.6 0.0 copy-start.1
  18.6 7.4 %load.1.both_ref = bf16[3,7168,512]{2,1,0:T(8,128)(2,1)S(1)} custom-call(bf16[7168,1024]{1,0:T(8,128)(2,1)} %gate_hbm.1, bf16[7168,1024]{1,0:T(8,128)(2,1)} %up_hbm.3, bf16[8,4608]{1,0:T(8,128)(2,1)S(1)} %get-tuple-element.34.after_ref.refs_0_), custom_call_target="tpu_custom_call" | custom-call | bytes 22020096 | tf_op jit(solution)/shard_map/load/pallas_call | solution.py:204
  26.0 0.0 collective-permute-done.2.refs_3_
  26.0 0.0 collective-permute-done.3.refs_4_
  26.1 0.0 collective-permute-done.4.refs_5_
  26.1 0.0 collective-permute-done.5.refs_6_
  26.1 0.0 collective-permute-done.6.refs_7_
  26.1 1.4 %project.1.mine_ref = f32[64,896]{1,0:T(8,128)S(1)} custom-call(bf16[4096,896]{1,0:T(8,128)(2,1)S(1)} %get-tuple-element.25.weight_ref, bf16[8,4608]{1,0:T(8,128)(2,1)S(1)} %get-tuple-element.34.after_ref.refs_0_, bf16[8,4608]{1,0:T(8,128)(2,1)S(1)} %collective-permute-done.refs_1_, bf16[8,4608]{1,0:T(8,128)(2,1)S(1)} %collective-permute-done.1.refs_2_, ...), custom_call_target="tpu_custom_call" | custom-call | tf_op jit(solution)/shard_map/project/pallas_call | solution.py:229
  27.4 0.1 collective-permute-start.7
  27.5 1.5 %collective-permute-done.7.other_ref = f32[64,896]{1,0:T(8,128)S(1)} collective-permute-done((f32[64,896]{1,0:T(8,128)S(1)}, f32[64,896]{1,0:T(8,128)S(1)}, u32[]{:S(2)}, u32[]{:S(2)}) %collective-permute-start.7) | collective-permute-done | bytes 229408 | tf_op jit(solution)/shard_map/ppermute | solution.py:424
  29.0 0.3 dispatch.1
  29.3 16.4 %all_to_all.10.received_ref = bf16[8,16,1152]{2,1,0:T(8,128)(2,1)S(1)} all-to-all(bf16[8,16,1152]{2,1,0:T(8,128)(2,1)S(1)} %dispatch.1), channel_id=1, replica_groups=mesh['groups'=2,'role'=8,'head'=2] {'role'}, dimensions={0} | all-to-all | bytes 589824 | tf_op jit(solution)/shard_map/all_to_all | solution.py:426
  45.8 0.0 copy-done.1
  45.8 0.2 normalise.1.mine_ref
  46.0 0.0 copy-start.2
  46.0 0.0 copy-start.3
  46.0 0.1 collective-permute-start.8
  46.1 1.5 %collective-permute-done.8.other_ref = bf16[16,7168]{1,0:T(8,128)(2,1)S(1)} collective-permute-done((bf16[16,7168]{1,0:T(8,128)(2,1)S(1)}, bf16[16,7168]{1,0:T(8,128)(2,1)S(1)}, u32[]{:S(2)}, u32[]{:S(2)}) %collective-permute-start.8) | collective-permute-done | bytes 229408 | tf_op jit(solution)/shard_map/ppermute | solution.py:428
  47.5 9.1 %experts.1 = (f32[16,7168]{1,0:T(8,128)S(1)}, bf16[16,7168]{1,0:T(8,128)(2,1)S(1)}) custom-call(bf16[16,7168]{1,0:T(8,128)(2,1)S(1)} %normalise.1.mine_ref, bf16[16,7168]{1,0:T(8,128)(2,1)S(1)} %collective-permute-done.8.other_ref, bf16[3,7168,512]{2,1,0:T(8,128)(2,1)S(1)} %load.1.both_ref, bf16[7168,1024]{1,0:T(8,128)(2,1)} %up_hbm.3, ...), custom_call_target="tpu_custom_call" | custom-call | flops 1409286144 | bytes 22020096 | tf_op jit(solution)/shard_map/experts/pallas_call | solution.py:345
  56.6 0.2 collective-permute-start.9
  56.8 1.4 %collective-permute-done.9 = bf16[16,7168]{1,0:T(8,128)(2,1)S(1)} collective-permute-done((bf16[16,7168]{1,0:T(8,128)(2,1)S(1)}, bf16[16,7168]{1,0:T(8,128)(2,1)S(1)}, u32[]{:S(2)}, u32[]{:S(2)}) %collective-permute-start.9) | collective-permute-done | bytes 229408 | tf_op jit(solution)/shard_map/ppermute | solution.py:430
  58.2 0.1 reshape.7
  58.3 11.4 %all_to_all.11.returned_ref = bf16[8,2,7168]{2,1,0:T(2,128)(2,1)S(1)} all-to-all(bf16[8,2,7168]{2,1,0:T(2,128)(2,1)S(1)} %reshape.7), channel_id=1, replica_groups=mesh['groups'=2,'role'=8,'head'=2] {'role'}, dimensions={0} | all-to-all | bytes 458752 | tf_op jit(solution)/shard_map/all_to_all | solution.py:432
  69.7 0.0 copy-done.2
  69.7 0.0 copy-done.3
  69.7 1.6 %combine.1 = bf16[4,7168]{1,0:T(4,128)(2,1)} custom-call(s32[2,4]{1,0:T(2,128)S(1)} %bitcast.6, f32[2,4]{1,0:T(2,128)S(1)} %bitcast.7, bf16[8,16,1152]{2,1,0:T(8,128)(2,1)S(1)} %all_to_all.10.received_ref, bf16[8,2,7168]{2,1,0:T(2,128)(2,1)S(1)} %all_to_all.11.returned_ref), custom_call_target="tpu_custom_call" | custom-call | tf_op jit(solution)/shard_map/combine/pallas_call | solution.py:178
  (1 shorter events, 0.0 us)
Async XLA Ops:
  0.0 0.8 %copy-start = (bf16[4,7168]{1,0:T(4,128)(2,1)S(1)}, bf16[4,7168]{1,0:T(4,128)(2,1)}, u32[]{:S(2)}) copy-start(bf16[4,7168]{1,0:T(4,128)(2,1)} %resid_ref.1) | copy-start | bytes 172036
  6.1 8.9 %collective-permute-start = (bf16[8,4608]{1,0:T(8,128)(2,1)S(1)}, bf16[8,4608]{1,0:T(8,128)(2,1)S(1)}, u32[]{:S(2)}, u32[]{:S(2)}) collective-permute-start(bf16[8,4608]{1,0:T(8,128)(2,1)S(1)} %get-tuple-element.27), channel_id=1, source_target_pairs={{0,2},{2,0},{4,6},{6,4},{8,10},{10,8},{12,14},{14,12},{1,3},{3,1},... | collective-permute-start | bytes 221192 | tf_op jit(solution)/shard_map/ppermute | solution.py:421
  9.2 9.5 %collective-permute-start.1 = (bf16[8,4608]{1,0:T(8,128)(2,1)S(1)}, bf16[8,4608]{1,0:T(8,128)(2,1)S(1)}, u32[]{:S(2)}, u32[]{:S(2)}) collective-permute-start(bf16[8,4608]{1,0:T(8,128)(2,1)S(1)} %get-tuple-element.28), channel_id=1, source_target_pairs={{0,4},{2,6},{4,0},{6,2},{8,12},{10,14},{12,8},{14,10},{1,5},{3,7},... | collective-permute-start | bytes 221192 | tf_op jit(solution)/shard_map/ppermute | solution.py:421
  10.7 15.3 %collective-permute-start.2 = (bf16[8,4608]{1,0:T(8,128)(2,1)S(1)}, bf16[8,4608]{1,0:T(8,128)(2,1)S(1)}, u32[]{:S(2)}, u32[]{:S(2)}) collective-permute-start(bf16[8,4608]{1,0:T(8,128)(2,1)S(1)} %get-tuple-element.29), channel_id=1, source_target_pairs={{0,6},{2,4},{4,2},{6,0},{8,14},{10,12},{12,10},{14,8},{1,7},{3,5},... | collective-permute-start | bytes 221192 | tf_op jit(solution)/shard_map/ppermute | solution.py:421
  10.7 15.3 %collective-permute-start.3 = (bf16[8,4608]{1,0:T(8,128)(2,1)S(1)}, bf16[8,4608]{1,0:T(8,128)(2,1)S(1)}, u32[]{:S(2)}, u32[]{:S(2)}) collective-permute-start(bf16[8,4608]{1,0:T(8,128)(2,1)S(1)} %get-tuple-element.30), channel_id=1, source_target_pairs={{0,8},{2,10},{4,12},{6,14},{8,0},{10,2},{12,4},{14,6},{1,9},{3,11}... | collective-permute-start | bytes 221192 | tf_op jit(solution)/shard_map/ppermute | solution.py:421
  13.7 12.3 %collective-permute-start.4 = (bf16[8,4608]{1,0:T(8,128)(2,1)S(1)}, bf16[8,4608]{1,0:T(8,128)(2,1)S(1)}, u32[]{:S(2)}, u32[]{:S(2)}) collective-permute-start(bf16[8,4608]{1,0:T(8,128)(2,1)S(1)} %get-tuple-element.31), channel_id=1, source_target_pairs={{0,10},{2,8},{4,14},{6,12},{8,2},{10,0},{12,6},{14,4},{1,11},{3,9}... | collective-permute-start | bytes 221192 | tf_op jit(solution)/shard_map/ppermute | solution.py:421
  15.0 11.1 %collective-permute-start.5 = (bf16[8,4608]{1,0:T(8,128)(2,1)S(1)}, bf16[8,4608]{1,0:T(8,128)(2,1)S(1)}, u32[]{:S(2)}, u32[]{:S(2)}) collective-permute-start(bf16[8,4608]{1,0:T(8,128)(2,1)S(1)} %get-tuple-element.32), channel_id=1, source_target_pairs={{0,12},{2,14},{4,8},{6,10},{8,4},{10,6},{12,0},{14,2},{1,13},{3,15... | collective-permute-start | bytes 221192 | tf_op jit(solution)/shard_map/ppermute | solution.py:421
  18.6 7.5 %collective-permute-start.6 = (bf16[8,4608]{1,0:T(8,128)(2,1)S(1)}, bf16[8,4608]{1,0:T(8,128)(2,1)S(1)}, u32[]{:S(2)}, u32[]{:S(2)}) collective-permute-start(bf16[8,4608]{1,0:T(8,128)(2,1)S(1)} %get-tuple-element.33), channel_id=1, source_target_pairs={{0,14},{2,12},{4,10},{6,8},{8,6},{10,4},{12,2},{14,0},{1,15},{3,13... | collective-permute-start | bytes 221192 | tf_op jit(solution)/shard_map/ppermute | solution.py:421
  18.6 27.1 %copy-start.1 = (f32[7168]{0:T(1024)S(1)}, f32[7168]{0:T(1024)}, u32[]{:S(2)}) copy-start(f32[7168]{0:T(1024)} %param.18) | copy-start | bytes 86020
  27.4 1.6 %collective-permute-start.7 = (f32[64,896]{1,0:T(8,128)S(1)}, f32[64,896]{1,0:T(8,128)S(1)}, u32[]{:S(2)}, u32[]{:S(2)}) collective-permute-start(f32[64,896]{1,0:T(8,128)S(1)} %project.1.mine_ref), channel_id=1, source_target_pairs={{0,1},{1,0},{2,3},{3,2},{4,5},{5,4},{6,7},{7,6},{8,9},{9,8},{10,11... | collective-permute-start | bytes 688136 | tf_op jit(solution)/shard_map/ppermute | solution.py:424
  46.0 23.8 %copy-start.2 = (s32[4,2]{0,1:T(2,128)S(1)}, s32[4,2]{0,1:T(2,128)}, u32[]{:S(2)}) copy-start(s32[4,2]{0,1:T(2,128)} %param.19) | copy-start | bytes 100
  46.0 23.8 %copy-start.3 = (f32[4,2]{0,1:T(2,128)S(1)}, f32[4,2]{0,1:T(2,128)}, u32[]{:S(2)}) copy-start(f32[4,2]{0,1:T(2,128)} %param.20) | copy-start | bytes 100
  46.0 1.6 %collective-permute-start.8 = (bf16[16,7168]{1,0:T(8,128)(2,1)S(1)}, bf16[16,7168]{1,0:T(8,128)(2,1)S(1)}, u32[]{:S(2)}, u32[]{:S(2)}) collective-permute-start(bf16[16,7168]{1,0:T(8,128)(2,1)S(1)} %normalise.1.mine_ref), channel_id=1, source_target_pairs={{0,1},{1,0},{2,3},{3,2},{4,5},{5,4},{6,7},{7,6},{8,9},{9,8},{10,11... | collective-permute-start | bytes 688136 | tf_op jit(solution)/shard_map/ppermute | solution.py:428
  56.6 1.6 %collective-permute-start.9 = (bf16[16,7168]{1,0:T(8,128)(2,1)S(1)}, bf16[16,7168]{1,0:T(8,128)(2,1)S(1)}, u32[]{:S(2)}, u32[]{:S(2)}) collective-permute-start(bf16[16,7168]{1,0:T(8,128)(2,1)S(1)} %get-tuple-element.44), channel_id=1, source_target_pairs={{0,1},{1,0},{2,3},{3,2},{4,5},{5,4},{6,7},{7,6},{8,9},{9,8},{10,11... | collective-permute-start | bytes 688136 | tf_op jit(solution)/shard_map/ppermute | solution.py:430

commit v7 on v5

--- a/solution.py
+++ b/solution.py
@@ -319,10 +319,10 @@
         if i:
             for j in range(4, outs):
                 fetch(j).start()
+            rest.wait()
             up = jnp.dot(x_ref[...], up_ref[...], preferred_element_type=F32)
         else:
             up = jnp.dot(x_ref[...], both_ref[2], preferred_element_type=F32)
-            rest.wait()
             for j in range(1, 4):
                 fetch(j).start()
         act = (gate / (1.0 + jnp.exp(-gate)) * up).astype(BF16)

time: 71.3 us -> 73.8 us (1.035)
  Pallas kernels: 24.9 us -> 27.4 us
    pallas_call x1, Pallas kernels: 9.07 us -> 11.6 us  [run_experts(): pl.pallas_call(expert_kernel, out_shape=(jax.ShapeDtypeStruct((rows, widt...]
where the time goes in v7:
time: 73.8 us; the launch traced here: 73.5 us
  blocking collectives  27.9 us (38%)
  Pallas kernels  27.4 us (37%)
  starting transfers between devices  12.8 us (17%)
  waiting for transfers between devices  4.32 us (6%)
  local copies, waits for them, and re-layouts  0.92 us (1%)
    all_to_all x1, blocking collectives, fast(): lax.all_to_all(outgoing, 'role', split_axis=0, concat_axis=0, tiled=True)  16.4 us
    ppermute x7, starting transfers between devices, fast(): messages[step] = lax.ppermute(messages[step], 'role', pairs)  12.5 us
    pallas_call x1, Pallas kernels, run_experts(): pl.pallas_call(expert_kernel, out_shape=(jax.ShapeDtypeStruct((rows, widt...  11.6 us
    all_to_all x1, blocking collectives, fast(): lax.all_to_all(summed.reshape(roles, CAP, width), 'role', split_axis=0, c...  11.4 us
    pallas_call x1, Pallas kernels, load(): pl.pallas_call(load_kernel, out_shape=VMEM((3, gate.shape[0], gate.shape[...  7.39 us
    pallas_call x1, Pallas kernels, attend(): pl.pallas_call(attend_kernel, out_shape=(VMEM(weight.shape, weight.dtype)...  5.3 us
  transfers between devices with their start and end apart: 10, of which 3 were waited for; matrix products, arithmetic and copies ran while one was open for 0% of the time, Pallas kernels for 10%

profile of v7, /device:TPU:0, one launch (start us, length us, event | category | flops | bytes accessed | tf_op | source)
XLA Modules:
  0.0 73.5 jit_solution(3663997627459939757)
XLA Ops:
  0.0 0.0 copy-start
  0.0 0.8 %copy-done = bf16[4,7168]{1,0:T(4,128)(2,1)S(1)} copy-done((bf16[4,7168]{1,0:T(4,128)(2,1)S(1)}, bf16[4,7168]{1,0:T(4,128)(2,1)}, u32[]{:S(2)}) %copy-start) | copy-done | bytes 57368
  0.8 5.3 %attend.1 = (bf16[4096,896]{1,0:T(8,128)(2,1)S(1)}, bf16[8,4608]{1,0:T(8,128)(2,1)S(1)}, bf16[8,4608]{1,0:T(8,128)(2,1)S(1)}, bf16[8,4608]{1,0:T(8,128)(2,1)S(1)...) custom-call(bf16[4,7168]{1,0:T(4,128)(2,1)S(1)} %copy-done, ...), custom_call_target="tpu_custom_call" | custom-call | tf_op jit(solution)/shard_map/attend/pallas_call | solution.py:128
  6.1 3.0 %collective-permute-start = (bf16[8,4608]{1,0:T(8,128)(2,1)S(1)}, bf16[8,4608]{1,0:T(8,128)(2,1)S(1)}, u32[]{:S(2)}, u32[]{:S(2)}) collective-permute-start(bf16[8,4608]{1,0:T(8,128)(2,1)S(1)} %get-tuple-element.27), channel_id=1, source_target_pairs={{0,2},{2,0},{4,6},{6,4},{8,10},{10,8},{12,14},{14,12},{1,3},{3,1},... | collective-permute-start | bytes 221192 | tf_op jit(solution)/shard_map/ppermute | solution.py:420
  9.2 1.6 %collective-permute-start.1 = (bf16[8,4608]{1,0:T(8,128)(2,1)S(1)}, bf16[8,4608]{1,0:T(8,128)(2,1)S(1)}, u32[]{:S(2)}, u32[]{:S(2)}) collective-permute-start(bf16[8,4608]{1,0:T(8,128)(2,1)S(1)} %get-tuple-element.28), channel_id=1, source_target_pairs={{0,4},{2,6},{4,0},{6,2},{8,12},{10,14},{12,8},{14,10},{1,5},{3,7},... | collective-permute-start | bytes 221192 | tf_op jit(solution)/shard_map/ppermute | solution.py:420
  10.7 0.0 collective-permute-start.2
  10.7 3.0 %collective-permute-start.3 = (bf16[8,4608]{1,0:T(8,128)(2,1)S(1)}, bf16[8,4608]{1,0:T(8,128)(2,1)S(1)}, u32[]{:S(2)}, u32[]{:S(2)}) collective-permute-start(bf16[8,4608]{1,0:T(8,128)(2,1)S(1)} %get-tuple-element.30), channel_id=1, source_target_pairs={{0,8},{2,10},{4,12},{6,14},{8,0},{10,2},{12,4},{14,6},{1,9},{3,11}... | collective-permute-start | bytes 221192 | tf_op jit(solution)/shard_map/ppermute | solution.py:420
  13.7 1.3 %collective-permute-start.4 = (bf16[8,4608]{1,0:T(8,128)(2,1)S(1)}, bf16[8,4608]{1,0:T(8,128)(2,1)S(1)}, u32[]{:S(2)}, u32[]{:S(2)}) collective-permute-start(bf16[8,4608]{1,0:T(8,128)(2,1)S(1)} %get-tuple-element.31), channel_id=1, source_target_pairs={{0,10},{2,8},{4,14},{6,12},{8,2},{10,0},{12,6},{14,4},{1,11},{3,9}... | collective-permute-start | bytes 221192 | tf_op jit(solution)/shard_map/ppermute | solution.py:420
  15.0 0.0 collective-permute-done.refs_1_
  15.0 3.6 %collective-permute-start.5 = (bf16[8,4608]{1,0:T(8,128)(2,1)S(1)}, bf16[8,4608]{1,0:T(8,128)(2,1)S(1)}, u32[]{:S(2)}, u32[]{:S(2)}) collective-permute-start(bf16[8,4608]{1,0:T(8,128)(2,1)S(1)} %get-tuple-element.32), channel_id=1, source_target_pairs={{0,12},{2,14},{4,8},{6,10},{8,4},{10,6},{12,0},{14,2},{1,13},{3,15... | collective-permute-start | bytes 221192 | tf_op jit(solution)/shard_map/ppermute | solution.py:420
  18.6 0.0 collective-permute-done.1.refs_2_
  18.6 0.0 collective-permute-start.6
  18.6 0.0 copy-start.1
  18.6 7.4 %load.1.both_ref = bf16[3,7168,512]{2,1,0:T(8,128)(2,1)S(1)} custom-call(bf16[7168,1024]{1,0:T(8,128)(2,1)} %gate_hbm.1, bf16[7168,1024]{1,0:T(8,128)(2,1)} %up_hbm.3, bf16[8,4608]{1,0:T(8,128)(2,1)S(1)} %get-tuple-element.34.after_ref.refs_0_), custom_call_target="tpu_custom_call" | custom-call | bytes 22020096 | tf_op jit(solution)/shard_map/load/pallas_call | solution.py:203
  26.0 0.0 collective-permute-done.2.refs_3_
  26.0 0.0 collective-permute-done.3.refs_4_
  26.1 0.0 collective-permute-done.4.refs_5_
  26.1 0.0 collective-permute-done.5.refs_6_
  26.1 0.0 collective-permute-done.6.refs_7_
  26.1 1.4 %project.1.mine_ref = f32[64,896]{1,0:T(8,128)S(1)} custom-call(bf16[4096,896]{1,0:T(8,128)(2,1)S(1)} %get-tuple-element.25.weight_ref, bf16[8,4608]{1,0:T(8,128)(2,1)S(1)} %get-tuple-element.34.after_ref.refs_0_, bf16[8,4608]{1,0:T(8,128)(2,1)S(1)} %collective-permute-done.refs_1_, bf16[8,4608]{1,0:T(8,128)(2,1)S(1)} %collective-permute-done.1.refs_2_, ...), custom_call_target="tpu_custom_call" | custom-call | tf_op jit(solution)/shard_map/project/pallas_call | solution.py:228
  27.4 0.1 collective-permute-start.7
  27.5 1.5 %collective-permute-done.7.other_ref = f32[64,896]{1,0:T(8,128)S(1)} collective-permute-done((f32[64,896]{1,0:T(8,128)S(1)}, f32[64,896]{1,0:T(8,128)S(1)}, u32[]{:S(2)}, u32[]{:S(2)}) %collective-permute-start.7) | collective-permute-done | bytes 229408 | tf_op jit(solution)/shard_map/ppermute | solution.py:423
  29.0 0.3 dispatch.1
  29.3 16.4 %all_to_all.10.received_ref = bf16[8,16,1152]{2,1,0:T(8,128)(2,1)S(1)} all-to-all(bf16[8,16,1152]{2,1,0:T(8,128)(2,1)S(1)} %dispatch.1), channel_id=1, replica_groups=mesh['groups'=2,'role'=8,'head'=2] {'role'}, dimensions={0} | all-to-all | bytes 589824 | tf_op jit(solution)/shard_map/all_to_all | solution.py:425
  45.8 0.0 copy-done.1
  45.8 0.2 normalise.1.mine_ref
  46.0 0.0 copy-start.2
  46.0 0.0 copy-start.3
  46.0 0.1 collective-permute-start.8
  46.1 1.5 %collective-permute-done.8.other_ref = bf16[16,7168]{1,0:T(8,128)(2,1)S(1)} collective-permute-done((bf16[16,7168]{1,0:T(8,128)(2,1)S(1)}, bf16[16,7168]{1,0:T(8,128)(2,1)S(1)}, u32[]{:S(2)}, u32[]{:S(2)}) %collective-permute-start.8) | collective-permute-done | bytes 229408 | tf_op jit(solution)/shard_map/ppermute | solution.py:427
  47.5 11.6 %experts.1 = (f32[16,7168]{1,0:T(8,128)S(1)}, bf16[16,7168]{1,0:T(8,128)(2,1)S(1)}) custom-call(bf16[16,7168]{1,0:T(8,128)(2,1)S(1)} %normalise.1.mine_ref, bf16[16,7168]{1,0:T(8,128)(2,1)S(1)} %collective-permute-done.8.other_ref, bf16[3,7168,512]{2,1,0:T(8,128)(2,1)S(1)} %load.1.both_ref, bf16[7168,1024]{1,0:T(8,128)(2,1)} %up_hbm.3, ...), custom_call_target="tpu_custom_call" | custom-call | flops 1409286144 | bytes 22020096 | tf_op jit(solution)/shard_map/experts/pallas_call | solution.py:344
  59.1 0.2 collective-permute-start.9
  59.3 1.4 %collective-permute-done.9 = bf16[16,7168]{1,0:T(8,128)(2,1)S(1)} collective-permute-done((bf16[16,7168]{1,0:T(8,128)(2,1)S(1)}, bf16[16,7168]{1,0:T(8,128)(2,1)S(1)}, u32[]{:S(2)}, u32[]{:S(2)}) %collective-permute-start.9) | collective-permute-done | bytes 229408 | tf_op jit(solution)/shard_map/ppermute | solution.py:429
  60.7 0.1 reshape.7
  60.8 11.4 %all_to_all.11.returned_ref = bf16[8,2,7168]{2,1,0:T(2,128)(2,1)S(1)} all-to-all(bf16[8,2,7168]{2,1,0:T(2,128)(2,1)S(1)} %reshape.7), channel_id=1, replica_groups=mesh['groups'=2,'role'=8,'head'=2] {'role'}, dimensions={0} | all-to-all | bytes 458752 | tf_op jit(solution)/shard_map/all_to_all | solution.py:431
  72.2 0.0 copy-done.2
  72.2 0.0 copy-done.3
  72.2 1.3 %combine.1 = bf16[4,7168]{1,0:T(4,128)(2,1)} custom-call(s32[2,4]{1,0:T(2,128)S(1)} %bitcast.6, f32[2,4]{1,0:T(2,128)S(1)} %bitcast.7, bf16[8,16,1152]{2,1,0:T(8,128)(2,1)S(1)} %all_to_all.10.received_ref, bf16[8,2,7168]{2,1,0:T(2,128)(2,1)S(1)} %all_to_all.11.returned_ref), custom_call_target="tpu_custom_call" | custom-call | tf_op jit(solution)/shard_map/combine/pallas_call | solution.py:177
  (1 shorter events, 0.0 us)
Async XLA Ops:
  0.0 0.8 %copy-start = (bf16[4,7168]{1,0:T(4,128)(2,1)S(1)}, bf16[4,7168]{1,0:T(4,128)(2,1)}, u32[]{:S(2)}) copy-start(bf16[4,7168]{1,0:T(4,128)(2,1)} %resid_ref.1) | copy-start | bytes 172036
  6.1 8.9 %collective-permute-start = (bf16[8,4608]{1,0:T(8,128)(2,1)S(1)}, bf16[8,4608]{1,0:T(8,128)(2,1)S(1)}, u32[]{:S(2)}, u32[]{:S(2)}) collective-permute-start(bf16[8,4608]{1,0:T(8,128)(2,1)S(1)} %get-tuple-element.27), channel_id=1, source_target_pairs={{0,2},{2,0},{4,6},{6,4},{8,10},{10,8},{12,14},{14,12},{1,3},{3,1},... | collective-permute-start | bytes 221192 | tf_op jit(solution)/shard_map/ppermute | solution.py:420
  9.2 9.5 %collective-permute-start.1 = (bf16[8,4608]{1,0:T(8,128)(2,1)S(1)}, bf16[8,4608]{1,0:T(8,128)(2,1)S(1)}, u32[]{:S(2)}, u32[]{:S(2)}) collective-permute-start(bf16[8,4608]{1,0:T(8,128)(2,1)S(1)} %get-tuple-element.28), channel_id=1, source_target_pairs={{0,4},{2,6},{4,0},{6,2},{8,12},{10,14},{12,8},{14,10},{1,5},{3,7},... | collective-permute-start | bytes 221192 | tf_op jit(solution)/shard_map/ppermute | solution.py:420
  10.7 15.3 %collective-permute-start.2 = (bf16[8,4608]{1,0:T(8,128)(2,1)S(1)}, bf16[8,4608]{1,0:T(8,128)(2,1)S(1)}, u32[]{:S(2)}, u32[]{:S(2)}) collective-permute-start(bf16[8,4608]{1,0:T(8,128)(2,1)S(1)} %get-tuple-element.29), channel_id=1, source_target_pairs={{0,6},{2,4},{4,2},{6,0},{8,14},{10,12},{12,10},{14,8},{1,7},{3,5},... | collective-permute-start | bytes 221192 | tf_op jit(solution)/shard_map/ppermute | solution.py:420
  10.7 15.3 %collective-permute-start.3 = (bf16[8,4608]{1,0:T(8,128)(2,1)S(1)}, bf16[8,4608]{1,0:T(8,128)(2,1)S(1)}, u32[]{:S(2)}, u32[]{:S(2)}) collective-permute-start(bf16[8,4608]{1,0:T(8,128)(2,1)S(1)} %get-tuple-element.30), channel_id=1, source_target_pairs={{0,8},{2,10},{4,12},{6,14},{8,0},{10,2},{12,4},{14,6},{1,9},{3,11}... | collective-permute-start | bytes 221192 | tf_op jit(solution)/shard_map/ppermute | solution.py:420
  13.7 12.3 %collective-permute-start.4 = (bf16[8,4608]{1,0:T(8,128)(2,1)S(1)}, bf16[8,4608]{1,0:T(8,128)(2,1)S(1)}, u32[]{:S(2)}, u32[]{:S(2)}) collective-permute-start(bf16[8,4608]{1,0:T(8,128)(2,1)S(1)} %get-tuple-element.31), channel_id=1, source_target_pairs={{0,10},{2,8},{4,14},{6,12},{8,2},{10,0},{12,6},{14,4},{1,11},{3,9}... | collective-permute-start | bytes 221192 | tf_op jit(solution)/shard_map/ppermute | solution.py:420
  15.0 11.1 %collective-permute-start.5 = (bf16[8,4608]{1,0:T(8,128)(2,1)S(1)}, bf16[8,4608]{1,0:T(8,128)(2,1)S(1)}, u32[]{:S(2)}, u32[]{:S(2)}) collective-permute-start(bf16[8,4608]{1,0:T(8,128)(2,1)S(1)} %get-tuple-element.32), channel_id=1, source_target_pairs={{0,12},{2,14},{4,8},{6,10},{8,4},{10,6},{12,0},{14,2},{1,13},{3,15... | collective-permute-start | bytes 221192 | tf_op jit(solution)/shard_map/ppermute | solution.py:420
  18.6 7.5 %collective-permute-start.6 = (bf16[8,4608]{1,0:T(8,128)(2,1)S(1)}, bf16[8,4608]{1,0:T(8,128)(2,1)S(1)}, u32[]{:S(2)}, u32[]{:S(2)}) collective-permute-start(bf16[8,4608]{1,0:T(8,128)(2,1)S(1)} %get-tuple-element.33), channel_id=1, source_target_pairs={{0,14},{2,12},{4,10},{6,8},{8,6},{10,4},{12,2},{14,0},{1,15},{3,13... | collective-permute-start | bytes 221192 | tf_op jit(solution)/shard_map/ppermute | solution.py:420
  18.6 27.1 %copy-start.1 = (f32[7168]{0:T(1024)S(1)}, f32[7168]{0:T(1024)}, u32[]{:S(2)}) copy-start(f32[7168]{0:T(1024)} %param.18) | copy-start | bytes 86020
  27.4 1.6 %collective-permute-start.7 = (f32[64,896]{1,0:T(8,128)S(1)}, f32[64,896]{1,0:T(8,128)S(1)}, u32[]{:S(2)}, u32[]{:S(2)}) collective-permute-start(f32[64,896]{1,0:T(8,128)S(1)} %project.1.mine_ref), channel_id=1, source_target_pairs={{0,1},{1,0},{2,3},{3,2},{4,5},{5,4},{6,7},{7,6},{8,9},{9,8},{10,11... | collective-permute-start | bytes 688136 | tf_op jit(solution)/shard_map/ppermute | solution.py:423
  46.0 26.3 %copy-start.2 = (s32[4,2]{0,1:T(2,128)S(1)}, s32[4,2]{0,1:T(2,128)}, u32[]{:S(2)}) copy-start(s32[4,2]{0,1:T(2,128)} %param.19) | copy-start | bytes 100
  46.0 26.3 %copy-start.3 = (f32[4,2]{0,1:T(2,128)S(1)}, f32[4,2]{0,1:T(2,128)}, u32[]{:S(2)}) copy-start(f32[4,2]{0,1:T(2,128)} %param.20) | copy-start | bytes 100
  46.0 1.6 %collective-permute-start.8 = (bf16[16,7168]{1,0:T(8,128)(2,1)S(1)}, bf16[16,7168]{1,0:T(8,128)(2,1)S(1)}, u32[]{:S(2)}, u32[]{:S(2)}) collective-permute-start(bf16[16,7168]{1,0:T(8,128)(2,1)S(1)} %normalise.1.mine_ref), channel_id=1, source_target_pairs={{0,1},{1,0},{2,3},{3,2},{4,5},{5,4},{6,7},{7,6},{8,9},{9,8},{10,11... | collective-permute-start | bytes 688136 | tf_op jit(solution)/shard_map/ppermute | solution.py:427
  59.1 1.6 %collective-permute-start.9 = (bf16[16,7168]{1,0:T(8,128)(2,1)S(1)}, bf16[16,7168]{1,0:T(8,128)(2,1)S(1)}, u32[]{:S(2)}, u32[]{:S(2)}) collective-permute-start(bf16[16,7168]{1,0:T(8,128)(2,1)S(1)} %get-tuple-element.44), channel_id=1, source_target_pairs={{0,1},{1,0},{2,3},{3,2},{4,5},{5,4},{6,7},{7,6},{8,9},{9,8},{10,11... | collective-permute-start | bytes 688136 | tf_op jit(solution)/shard_map/ppermute | solution.py:429
